TPU v7x, 256 devices: a whole 4x4x8 slice. The times are simulated.
256 devices in a mesh: dp: 8 (over y, x_hi), seq: 32 (over z, x_lo, core).
Axes of the slice: x: 4 (x_hi: 2, x_lo: 2; x = x_hi * 2 + x_lo), y: 4, z: 8, core: 2. Of those that a mesh axis runs over, the one named last changes fastest.
Arguments:
- inputs_x: bfloat16 [8, 4096, 3072], P('dp', 'seq'), may hold values from -0.046875 to 0.046875
- queries: bfloat16 [8, 4096, 4096], P('dp', 'seq'), may hold values from -6 to 6
- keys: bfloat16 [8, 4096, 4096], P('dp', 'seq'), may hold values from -1.25 to 1.25
- values: bfloat16 [8, 4096, 4096], P('dp', 'seq'), may hold values from -1.25 to 1.25
- grad_out: bfloat16 [8, 4096, 4096], P('dp', 'seq'), may hold values from -0.0625 to 0.0625
- decay_exp: int32 [32], P('seq'), may hold values from 0 to 7
- state_in: float32 [8, 32, 128, 128], P('dp', 'seq'), may hold values from -12 to 12
Outputs:
- grad_queries: bfloat16 [8, 4096, 4096], P('dp', 'seq')
- grad_keys: bfloat16 [8, 4096, 4096], P('dp', 'seq')
- grad_values: bfloat16 [8, 4096, 4096], P('dp', 'seq')
- weight_grads: float32 [2, 32, 768, 512], P(None, 'seq', 'dp')
- state_grad: float32 [8, 32, 128, 128], P('dp', 'seq')
All inputs are finite; a program needn't handle non-finite values.
Results may differ from a plain program's by a relative error of at most 0.0029.
Values may be sent and summed in bfloat16 or wider, within the bound.
No kernel may reach another device: no remote copies, remote signals or barrier semaphores. Data moves between devices by JAX's collectives and lax.ppermute only.
A program may use at most 128 MiB of HBM per device.

v0:
```python
import jax
import jax.numpy as jnp
from jax import lax
from jax.sharding import PartitionSpec as P

BLOCK = 256
ROW_GROUPS = 4


exact_mode = lax.Precision.HIGHEST


def rates(decay_exp, length):
    return -jnp.power(2.0, decay_exp.astype(jnp.float32)) / length


def split_blocks(tensor, head_count):
    length = tensor.shape[1]
    head_width = tensor.shape[2] // head_count
    blocked = tensor[0].reshape(length // BLOCK, BLOCK, head_count, head_width)
    return blocked.transpose(2, 0, 1, 3)


def join_blocks(tensor):
    head_count, block_count, block_len, head_width = tensor.shape
    joined = tensor.transpose(1, 2, 0, 3).reshape(
        1, block_count * block_len, head_count * head_width
    )
    return joined.astype(jnp.bfloat16)


def forward_states(key_blocks, value_blocks, log_rate, state_first):
    offsets = jnp.arange(BLOCK, dtype=jnp.float32)
    weighted = key_blocks.astype(jnp.float32) * jnp.exp(log_rate * (BLOCK - 1.0 - offsets))[:, None]
    updates = jnp.einsum(
        "bia,bic->bac", weighted, value_blocks.astype(jnp.float32), precision=exact_mode
    )
    whole_decay = jnp.exp(log_rate * BLOCK)

    def advance(state, update):
        return (whole_decay * state + update, state)

    unused, states = lax.scan(advance, state_first, updates)
    return states


def reverse_states(query_blocks, grad_blocks, log_rate):
    offsets = jnp.arange(BLOCK, dtype=jnp.float32)
    weighted = query_blocks.astype(jnp.float32) * jnp.exp(log_rate * offsets)[:, None]
    updates = jnp.einsum(
        "bja,bjc->bac", weighted, grad_blocks.astype(jnp.float32), precision=exact_mode
    )
    whole_decay = jnp.exp(log_rate * BLOCK)

    def retreat(state, update):
        return (whole_decay * state + update, state)

    first_state, later = lax.scan(retreat, jnp.zeros_like(updates[0]), updates, reverse=True)
    return (later, first_state)


def block_grads(query_blocks, key_blocks, value_blocks, grad_blocks, forward, later, log_rate):
    offsets = jnp.arange(BLOCK, dtype=jnp.float32)
    spread = offsets[:, None] - offsets[None, :]
    lower = jnp.where(spread >= 0.0, jnp.exp(log_rate * jnp.maximum(spread, 0.0)), 0.0)
    head_scale = jnp.exp(log_rate * (offsets + 1.0))[:, None]
    tail_scale = jnp.exp(log_rate * (BLOCK - offsets))[:, None]
    grad_scores = (
        jnp.einsum("bja,bia->bji", grad_blocks, value_blocks, preferred_element_type=jnp.float32)
        * lower
    )
    key_scores = (
        jnp.einsum("bja,bia->bji", query_blocks, key_blocks, preferred_element_type=jnp.float32)
        * lower
    )
    query_wide = query_blocks.astype(jnp.float32)
    key_wide = key_blocks.astype(jnp.float32)
    value_wide = value_blocks.astype(jnp.float32)
    grad_wide = grad_blocks.astype(jnp.float32)
    grad_query = head_scale * jnp.einsum("bja,bca->bjc", grad_wide, forward, precision=exact_mode)
    grad_query = grad_query + jnp.einsum(
        "bji,bic->bjc", grad_scores, key_wide, precision=exact_mode
    )
    grad_key = tail_scale * jnp.einsum("bia,bca->bic", value_wide, later, precision=exact_mode)
    grad_key = grad_key + jnp.einsum("bji,bjc->bic", grad_scores, query_wide, precision=exact_mode)
    grad_value = tail_scale * jnp.einsum("bia,bac->bic", key_wide, later, precision=exact_mode)
    grad_value = grad_value + jnp.einsum(
        "bji,bjc->bic", key_scores, grad_wide, precision=exact_mode
    )
    return (grad_query, grad_key, grad_value)


def weight_blocks(inputs_x, token_keys, token_values, seq_count):
    row_groups = ROW_GROUPS
    col_groups = seq_count // row_groups
    tok_count = inputs_x.shape[1]
    row_count = inputs_x.shape[2] // row_groups
    col_count = token_keys.shape[2] // col_groups
    row_pieces = inputs_x[0].reshape(tok_count, row_groups, row_count).transpose(1, 0, 2)
    row_send = jnp.repeat(row_pieces, col_groups, axis=0)
    col_pieces = jnp.stack(
        (
            token_keys[0].reshape(tok_count, col_groups, col_count),
            token_values[0].reshape(tok_count, col_groups, col_count),
        ),
        axis=2,
    )
    col_pieces = col_pieces.transpose(1, 0, 2, 3).reshape(col_groups, tok_count, 2 * col_count)
    col_send = jnp.tile(col_pieces, (row_groups, 1, 1))
    row_block = lax.all_to_all(row_send, "seq", split_axis=0, concat_axis=1, tiled=True)[0]
    col_block = lax.all_to_all(col_send, "seq", split_axis=0, concat_axis=1, tiled=True)[0]
    summed = lax.psum_scatter(
        jnp.dot(row_block.T, col_block, preferred_element_type=jnp.float32),
        "dp",
        scatter_dimension=0,
        tiled=True,
    )
    share = summed.shape[0]
    return summed.reshape(share, 2, col_count).transpose(1, 0, 2)[:, None]


def per_device(inputs_x, queries, keys, values, grad_out, decay_exp, state_in):
    seq_count = lax.axis_size("seq")
    head_count = decay_exp.shape[0]
    query_heads, key_heads, value_heads, grad_heads = (
        lax.all_to_all(queries, "seq", split_axis=2, concat_axis=1, tiled=True),
        lax.all_to_all(keys, "seq", split_axis=2, concat_axis=1, tiled=True),
        lax.all_to_all(values, "seq", split_axis=2, concat_axis=1, tiled=True),
        lax.all_to_all(grad_out, "seq", split_axis=2, concat_axis=1, tiled=True),
    )
    log_rate = rates(decay_exp, key_heads.shape[1])
    key_blocks = split_blocks(key_heads, head_count)
    value_blocks = split_blocks(value_heads, head_count)
    forward = jax.vmap(forward_states)(key_blocks, value_blocks, log_rate, state_in[0])
    query_blocks = split_blocks(query_heads, head_count)
    grad_blocks = split_blocks(grad_heads, head_count)
    later, first_state = jax.vmap(reverse_states)(query_blocks, grad_blocks, log_rate)
    grad_query, grad_key, grad_value = jax.vmap(block_grads)(
        query_blocks, key_blocks, value_blocks, grad_blocks, forward, later, log_rate
    )
    state_grad = (jnp.exp(log_rate)[:, None, None] * first_state)[None]
    token_queries, token_keys, token_values = (
        lax.all_to_all(join_blocks(grad_query), "seq", split_axis=1, concat_axis=2, tiled=True),
        lax.all_to_all(join_blocks(grad_key), "seq", split_axis=1, concat_axis=2, tiled=True),
        lax.all_to_all(join_blocks(grad_value), "seq", split_axis=1, concat_axis=2, tiled=True),
    )
    weight_grads = weight_blocks(inputs_x, token_keys, token_values, seq_count)
    return (token_queries, token_keys, token_values, weight_grads, state_grad)


def solution(mesh):
    in_specs = (
        P("dp", "seq", None),
        P("dp", "seq", None),
        P("dp", "seq", None),
        P("dp", "seq", None),
        P("dp", "seq", None),
        P("seq"),
        P("dp", "seq", None, None),
    )
    out_specs = (
        P("dp", "seq", None),
        P("dp", "seq", None),
        P("dp", "seq", None),
        P(None, "seq", "dp", None),
        P("dp", "seq", None, None),
    )
    return jax.shard_map(
        per_device, mesh=mesh, in_specs=in_specs, out_specs=out_specs, check_vma=False
    )
```

profile of v0, /device:TPU:32, one launch (start us, length us, event | category | flops | bytes accessed | tf_op | source)
XLA Modules:
  0.0 841.4 jit_solution(13212903610690916706)
XLA Ops:
  7.2 5.0 copy.144
  12.7 22.4 %reduce.1 = bf16[4096,128]{1,0:T(8,128)(2,1)S(1)} reduce(bf16[4096,1,128]{2,1,0:T(2,128)(2,1)S(1)} %bitcast.165, bf16[]{:T(256)} %broadcast.111), dimensions={1}, to_apply=%bitcast.93.reduce_sub_computation | reduce | bytes 2097154
  36.2 9.7 %all-to-all-start.2 = ((bf16[32,2,8192]{2,1,0:T(2,128)(2,1)}), bf16[32,2,8192]{2,1,0:T(2,128)(2,1)S(1)}, u32[]{:S(2)}, u32[]{:S(2)}) async-start(bf16[32,2,8192]{2,1,0:T(2,128)(2,1)} %reshape.255), calls=%async_computation.2 | async-start | bytes 2097152 | tf_op jit(solution)/shard_map/all_to_all | solution.py:129
  45.9 5.0 copy.150
  50.9 23.4 %reduce.4 = bf16[4096,128]{1,0:T(8,128)(2,1)} reduce(bf16[4096,1,128]{2,1,0:T(2,128)(2,1)S(1)} %bitcast.169, bf16[]{:T(256)} %broadcast.111), dimensions={1}, to_apply=%bitcast.99.reduce_sub_computation | reduce | bytes 2097154
  76.5 8.8 %all-to-all-start.4 = ((bf16[32,2,8192]{2,1,0:T(2,128)(2,1)}), bf16[32,2,8192]{2,1,0:T(2,128)(2,1)}, u32[]{:S(2)}, u32[]{:S(2)}) async-start(bf16[32,2,8192]{2,1,0:T(2,128)(2,1)} %reshape.261), calls=%async_computation.4 | async-start | bytes 2097152 | tf_op jit(solution)/shard_map/all_to_all | solution.py:126
  85.3 5.0 copy.140
  90.3 23.4 %reduce.2 = bf16[4096,128]{1,0:T(8,128)(2,1)} reduce(bf16[4096,1,128]{2,1,0:T(2,128)(2,1)S(1)} %bitcast.170, bf16[]{:T(256)} %broadcast.111), dimensions={1}, to_apply=%bitcast.95.reduce_sub_computation | reduce | bytes 2097154
  115.8 8.3 all-to-all-start.1
  124.1 5.0 copy.138
  129.2 23.4 %reduce = bf16[4096,128]{1,0:T(8,128)(2,1)} reduce(bf16[4096,1,128]{2,1,0:T(2,128)(2,1)S(1)} %bitcast.171, bf16[]{:T(256)} %broadcast.111), dimensions={1}, to_apply=%bitcast.91.reduce_sub_computation | reduce | bytes 2097154
  159.3 4.3 reshape.262
  166.4 2.9 fusion.21
  169.3 18.6 %all-to-all-start = ((bf16[32,2,8192]{2,1,0:T(2,128)(2,1)}), bf16[32,2,8192]{2,1,0:T(2,128)(2,1)}, u32[]{:S(2)}, u32[]{:S(2)}) async-start(bf16[32,2,8192]{2,1,0:T(2,128)(2,1)} %reshape.253), calls=%async_computation | async-start | bytes 2097152 | tf_op jit(solution)/shard_map/all_to_all | solution.py:127
  187.9 14.4 %while.30 = (s32[]{:T(128)}, f32[1,128,128]{2,1,0:T(8,128)S(1)}, f32[16,1,128,128]{3,2,1,0:T(8,128)S(1)}, f32[1]{0:T(128)}, f32[16,1,128,128]{3,2,1,0:T(8,128)}, /*index=5*/s32[]{:T(128)}, s32[]{:T(128)}, s32[]{:T(128)}) while((s32[]{:T(128)}, f32[1,128,128]{2,1,0:T(8,128)S(1)}, f32[16,1,128,128]{3,2,1,0:T(8,128)S(1)}, ...), condition=%wide.region_3.4_spmd.clone, body=%wide.region_2.3_spmd.clone.sunk | while | flops 65540 | bytes 327808 | solution.py:58
  202.4 5.9 reshape.258
  208.3 2.7 copy.184
  219.1 17.0 %copy.194 = bf16[1,4096,128]{2,0,1:T(2,128)(2,1)} copy(bf16[1,4096,128]{2,1,0:T(8,128)(2,1)S(1)} %bitcast.176) | data formatting | bytes 2097152 | tf_op jit(solution)/shard_map/convert_element_type | solution.py:29
  236.1 23.4 %reduce.5 = bf16[4096,128]{1,0:T(8,128)(2,1)S(1)} reduce(bf16[4096,1,128]{2,1,0:T(2,128)(2,1)} %bitcast.167, bf16[]{:T(256)} %broadcast.111), dimensions={1}, to_apply=%bitcast.123.reduce_sub_computation | reduce | bytes 2097154
  260.7 8.7 %all-to-all-start.5 = ((bf16[32,2,8192]{2,1,0:T(2,128)(2,1)}), bf16[32,2,8192]{2,1,0:T(2,128)(2,1)}, u32[]{:S(2)}, u32[]{:S(2)}) async-start(bf16[32,2,8192]{2,1,0:T(2,128)(2,1)} %reshape.263), calls=%async_computation.5 | async-start | bytes 2097152 | tf_op jit(solution)/shard_map/all_to_all | solution.py:144
  269.4 5.8 reshape.254
  275.2 2.7 copy.183
  287.9 4.3 copy.193
  292.2 24.4 %reduce.6 = bf16[4096,128]{1,0:T(8,128)(2,1)} reduce(bf16[4096,1,128]{2,1,0:T(2,128)(2,1)} %bitcast.168, bf16[]{:T(256)} %broadcast.111), dimensions={1}, to_apply=%bitcast.122.reduce_sub_computation | reduce | bytes 2097154
  318.7 8.3 all-to-all-start.6
  327.1 2.7 reshape_squeeze.3
  331.8 23.3 %all-to-all-done.6 = bf16[32,2,8192]{2,1,0:T(2,128)(2,1)} async-done(((bf16[32,2,8192]{2,1,0:T(2,128)(2,1)}), bf16[32,2,8192]{2,1,0:T(2,128)(2,1)}, u32[]{:S(2)}, u32[]{:S(2)}) %all-to-all-start.6) | async-done | bytes 1048608 | tf_op jit(solution)/shard_map/all_to_all | solution.py:145
  355.2 4.5 broadcast_in_dim.28
  359.7 6.2 all-to-all-start.8
  365.9 5.8 reshape.264
  371.7 2.7 copy.188
  374.4 2.3 copy.158
  376.7 5.8 reshape.266
  382.5 2.7 copy.189
  390.7 115.8 %all-to-all-done.8 = bf16[32,128,768]{2,1,0:T(8,128)(2,1)} async-done(((bf16[32,128,768]{2,1,0:T(8,128)(2,1)}), bf16[32,128,768]{2,1,0:T(8,128)(2,1)}, u32[]{:S(2)}, u32[]{:S(2)}) %all-to-all-start.8) | async-done | bytes 6291488 | tf_op jit(solution)/shard_map/all_to_all | solution.py:110
  506.4 6.7 tile.11
  513.2 6.2 all-to-all-start.7
  519.4 2.9 fusion.18
  522.3 6.2 fusion.4
  528.5 176.3 %all-to-all-done.7 = bf16[32,128,1024]{1,2,0:T(8,128)(2,1)} async-done(((bf16[32,128,1024]{1,2,0:T(8,128)(2,1)}), bf16[32,128,1024]{1,2,0:T(8,128)(2,1)}, u32[]{:S(2)}, u32[]{:S(2)}) %all-to-all-start.7) | async-done | bytes 8388640 | tf_op jit(solution)/shard_map/all_to_all | solution.py:111
  704.9 12.2 %convolution_bitcast_fusion = f32[768,1024]{0,1:T(8,128)} fusion(bf16[32,128,1024]{1,2,0:T(8,128)(2,1)} %all-to-all-done.7, bf16[32,128,768]{2,1,0:T(8,128)(2,1)} %all-to-all-done.8), kind=kOutput, calls=%fused_computation.26 | convolution fusion | flops 6442450944 | bytes 17825792 | tf_op jit(solution)/shard_map/dot_general | solution.py:113
  717.1 3.5 copy.181
  721.7 24.2 %while.29 = (s32[]{:T(128)}, f32[1,128,128]{2,1,0:T(8,128)S(1)}, f32[16,1,128,128]{3,2,1,0:T(8,128)}, f32[1]{0:T(128)}, f32[16,1,128,128]{3,2,1,0:T(8,128)}, /*index=5*/s32[]{:T(128)}) while((s32[]{:T(128)}, f32[1,128,128]{2,1,0:T(8,128)S(1)}, f32[16,1,128,128]{3,2,1,0:T(8,128)}, f32[1]{0:T(128)}, f32[16,1,128,128]{3,2,1,0:T(8,128)}, ...), condition=%wide.region_1.2_spmd, body=%wide.region_0.1_spmd.sunk | while | flops 32770 | bytes 327769 | solution.py:43
  745.9 3.3 fusion.8
  750.8 16.7 %copy.195 = bf16[1,4096,128]{2,0,1:T(2,128)(2,1)S(1)} copy(bf16[1,4096,128]{2,1,0:T(8,128)(2,1)S(1)} %bitcast.181) | data formatting | bytes 2097152 | tf_op jit(solution)/shard_map/convert_element_type | solution.py:29
  767.6 22.4 %reduce.3 = bf16[4096,128]{1,0:T(8,128)(2,1)S(1)} reduce(bf16[4096,1,128]{2,1,0:T(2,128)(2,1)S(1)} %bitcast.166, bf16[]{:T(256)} %broadcast.111), dimensions={1}, to_apply=%bitcast.124.reduce_sub_computation | reduce | bytes 2097154
  791.1 5.2 all-to-all-start.3
  797.0 27.5 %all-to-all-done.3 = bf16[32,2,8192]{2,1,0:T(2,128)(2,1)S(1)} async-done(((bf16[32,2,8192]{2,1,0:T(2,128)(2,1)}), bf16[32,2,8192]{2,1,0:T(2,128)(2,1)S(1)}, u32[]{:S(2)}, u32[]{:S(2)}) %all-to-all-start.3) | async-done | bytes 1048608 | tf_op jit(solution)/shard_map/all_to_all | solution.py:143
  (133 shorter events, 95.8 us)
Async XLA Ops:
  36.2 40.3 %all-to-all-start.2 = ((bf16[32,2,8192]{2,1,0:T(2,128)(2,1)}), bf16[32,2,8192]{2,1,0:T(2,128)(2,1)S(1)}, u32[]{:S(2)}, u32[]{:S(2)}) async-start(bf16[32,2,8192]{2,1,0:T(2,128)(2,1)} %reshape.255), calls=%async_computation.2 | async-start | bytes 2097152 | tf_op jit(solution)/shard_map/all_to_all | solution.py:129
  76.5 39.3 %all-to-all-start.4 = ((bf16[32,2,8192]{2,1,0:T(2,128)(2,1)}), bf16[32,2,8192]{2,1,0:T(2,128)(2,1)}, u32[]{:S(2)}, u32[]{:S(2)}) async-start(bf16[32,2,8192]{2,1,0:T(2,128)(2,1)} %reshape.261), calls=%async_computation.4 | async-start | bytes 2097152 | tf_op jit(solution)/shard_map/all_to_all | solution.py:126
  115.8 53.5 %all-to-all-start.1 = ((bf16[32,2,8192]{2,1,0:T(2,128)(2,1)}), bf16[32,2,8192]{2,1,0:T(2,128)(2,1)}, u32[]{:S(2)}, u32[]{:S(2)}) async-start(bf16[32,2,8192]{2,1,0:T(2,128)(2,1)} %reshape.257), calls=%async_computation.1 | async-start | bytes 2097152 | tf_op jit(solution)/shard_map/all_to_all | solution.py:128
  166.4 47.0 %copy-start.1 = (bf16[1,32,128,128]{3,2,1,0:T(8,128)(2,1)}, bf16[1,32,128,128]{3,2,1,0:T(8,128)(2,1)S(1)}, u32[]{:S(2)}) copy-start(bf16[1,32,128,128]{3,2,1,0:T(8,128)(2,1)S(1)} %copy.151) | copy-start | bytes 3145732
  169.3 91.4 %all-to-all-start = ((bf16[32,2,8192]{2,1,0:T(2,128)(2,1)}), bf16[32,2,8192]{2,1,0:T(2,128)(2,1)}, u32[]{:S(2)}, u32[]{:S(2)}) async-start(bf16[32,2,8192]{2,1,0:T(2,128)(2,1)} %reshape.253), calls=%async_computation | async-start | bytes 2097152 | tf_op jit(solution)/shard_map/all_to_all | solution.py:127
  202.3 8.7 %copy-start.4 = (f32[16,1,128,128]{3,2,1,0:T(8,128)}, f32[16,1,128,128]{3,2,1,0:T(8,128)S(1)}, u32[]{:S(2)}) copy-start(f32[16,1,128,128]{3,2,1,0:T(8,128)S(1)} %get-tuple-element.137) | copy-start | bytes 3145732
  213.3 2.1 copy-start
  213.4 2.1 copy-start.5
  260.7 58.0 %all-to-all-start.5 = ((bf16[32,2,8192]{2,1,0:T(2,128)(2,1)}), bf16[32,2,8192]{2,1,0:T(2,128)(2,1)}, u32[]{:S(2)}, u32[]{:S(2)}) async-start(bf16[32,2,8192]{2,1,0:T(2,128)(2,1)} %reshape.263), calls=%async_computation.5 | async-start | bytes 2097152 | tf_op jit(solution)/shard_map/all_to_all | solution.py:144
  281.4 2.1 copy-start.6
  318.7 36.4 %all-to-all-start.6 = ((bf16[32,2,8192]{2,1,0:T(2,128)(2,1)}), bf16[32,2,8192]{2,1,0:T(2,128)(2,1)}, u32[]{:S(2)}, u32[]{:S(2)}) async-start(bf16[32,2,8192]{2,1,0:T(2,128)(2,1)} %reshape.265), calls=%async_computation.6 | async-start | bytes 2097152 | tf_op jit(solution)/shard_map/all_to_all | solution.py:145
  359.7 146.8 %all-to-all-start.8 = ((bf16[32,128,768]{2,1,0:T(8,128)(2,1)}), bf16[32,128,768]{2,1,0:T(8,128)(2,1)}, u32[]{:S(2)}, u32[]{:S(2)}) async-start(bf16[32,128,768]{2,1,0:T(8,128)(2,1)} %bitcast.146), calls=%async_computation.8 | async-start | bytes 12582912 | tf_op jit(solution)/shard_map/all_to_all | solution.py:110
  513.2 191.7 %all-to-all-start.7 = ((bf16[32,128,1024]{1,2,0:T(8,128)(2,1)}), bf16[32,128,1024]{1,2,0:T(8,128)(2,1)}, u32[]{:S(2)}, u32[]{:S(2)}) async-start(bf16[32,128,1024]{1,2,0:T(8,128)(2,1)} %bitcast.137), calls=%async_computation.7 | async-start | bytes 16777216 | tf_op jit(solution)/shard_map/all_to_all | solution.py:111
  519.4 312.9 %reduce-scatter.4.cloned.1.call-start = ((), (), s32[]{:S(2)}) async-start(), calls=%async_computation.10 | async-start | bytes 3538944
  720.6 1.1 copy-start.8
  720.6 25.3 %copy-start.7 = (f32[16,256,128]{1,2,0:T(8,128)S(1)}, f32[16,256,128]{1,2,0:T(8,128)}, u32[]{:S(2)}) copy-start(f32[16,256,128]{1,2,0:T(8,128)} %fusion.4) | copy-start | bytes 6291460
  791.1 33.4 %all-to-all-start.3 = ((bf16[32,2,8192]{2,1,0:T(2,128)(2,1)}), bf16[32,2,8192]{2,1,0:T(2,128)(2,1)S(1)}, u32[]{:S(2)}, u32[]{:S(2)}) async-start(bf16[32,2,8192]{2,1,0:T(2,128)(2,1)} %reshape.259), calls=%async_computation.3 | async-start | bytes 2097152 | tf_op jit(solution)/shard_map/all_to_all | solution.py:143
  826.6 3.0 copy-start.2
  828.3 2.6 copy-start.3
Sparse Core Ops, SparseCore 0:
  720.7 81.7 reduce-scatter.3
where the time goes:
time: 856 us; the launch traced here: 841 us
  waiting for transfers between devices  343 us (40%)
  other arithmetic  193 us (23%)
  local copies, waits for them, and re-layouts  171 us (20%)
  starting transfers between devices  80 us (9%)
  matrix products  38.3 us (4%)
  between operations  15.4 us (2%)
    all_to_all x1, waiting for transfers between devices, weight_blocks(): lax.all_to_all(col_send, 'seq', split_axis=0, concat_axis=1, tiled=True)[0]  176 us
    unnamed x8, other arithmetic  163 us
    all_to_all x1, waiting for transfers between devices, weight_blocks(): lax.all_to_all(row_send, 'seq', split_axis=0, concat_axis=1, tiled=True)[0]  116 us
    unnamed x49, local copies, waits for them, and re-layouts  85 us
    convert_element_type x6, local copies, waits for them, and re-layouts, join_blocks(): return joined.astype(jnp.bfloat16)  43.6 us
    all_to_all x1, waiting for transfers between devices, per_device(): lax.all_to_all(join_blocks(grad_query), 'seq', split_axis=1, concat_axis=...  27.5 us
    all_to_all x1, waiting for transfers between devices, per_device(): lax.all_to_all(join_blocks(grad_value), 'seq', split_axis=1, concat_axis=...  23.3 us
    all_to_all x1, starting transfers between devices, per_device(): lax.all_to_all(keys, 'seq', split_axis=2, concat_axis=1, tiled=True)  18.6 us
  transfers between devices with their start and end apart: 10, of which 4 were waited for; matrix products, arithmetic and copies ran while one was open for 41% of the time, Pallas kernels for 0%

commit v1 on v0

v1 whole, which is shorter than its diff:
```python
import functools

import jax
import jax.numpy as jnp
from jax import lax
from jax.experimental import pallas as pl
from jax.experimental.pallas import tpu as pltpu
from jax.sharding import Mesh
from jax.sharding import PartitionSpec as P

WIDTH = 128
f32 = jnp.float32
bf16 = jnp.bfloat16
PLANE = ("y", "xh", "xl", "core")
QUAD = ("xl", "core")
CHAIN = ("z", "xl", "core")


def log_rate(exponent, length):
    return -(jnp.left_shift(1, exponent).astype(f32)) * (1.0 / length)


def power_of(rate, steps):
    return jnp.exp(jnp.full((1, WIDTH), rate * steps, f32))


def halves(wide):
    high = wide.astype(bf16)
    return high, (wide - high.astype(f32)).astype(bf16)


def dot(left, right, dims):
    return lax.dot_general(left, right, (dims, ((), ())), preferred_element_type=f32)


def update_kernel(exp_ref, left_ref, right_ref, out_ref, *, reverse, length):
    group = pl.program_id(0)
    span = left_ref.shape[0]
    rows = lax.broadcasted_iota(jnp.int32, (span, WIDTH), 0).astype(f32)
    steps = rows if reverse else (span - 1.0) - rows
    for slot in range(4):
        rate = log_rate(exp_ref[4 * group + slot], length)
        lanes = pl.ds(slot * WIDTH, WIDTH)
        high, low = halves(left_ref[:, lanes].astype(f32) * jnp.exp(rate * steps))
        right = right_ref[:, lanes]
        out_ref[slot, 0] = dot(
            jnp.concatenate((high, low), 0), jnp.concatenate((right, right), 0), ((0,), (0,))
        )


def join_kernel(exp_ref, slot_ref, parts_ref, out_ref, *, reverse, length, span):
    rate = log_rate(exp_ref[4 * pl.program_id(0) + slot_ref[0]], length)
    decay = power_of(rate, span)
    order = (3, 2, 1, 0) if reverse else (0, 1, 2, 3)
    total = parts_ref[order[0], 0]
    for item in order[1:]:
        total = decay * total + parts_ref[item, 0]
    out_ref[0] = total


def scan_forward_kernel(exp_ref, first_ref, parts_ref, out_ref, *, length, span):
    decay = power_of(log_rate(exp_ref[0], length), span)
    state = first_ref[...]
    for item in range(parts_ref.shape[0]):
        out_ref[item] = state
        state = decay * state + parts_ref[item]


def scan_reverse_kernel(exp_ref, parts_ref, out_ref, grad_ref, *, length, span):
    rate = log_rate(exp_ref[0], length)
    decay = power_of(rate, span)
    state = jnp.zeros(parts_ref.shape[1:], f32)
    for item in reversed(range(parts_ref.shape[0])):
        out_ref[item] = state
        state = decay * state + parts_ref[item]
    grad_ref[...] = power_of(rate, 1.0) * state


def spread_kernel(exp_ref, slot_ref, parts_ref, edge_ref, out_ref, *, reverse, length, span):
    rate = log_rate(exp_ref[4 * pl.program_id(0) + slot_ref[0]], length)
    decay = power_of(rate, span)
    state = edge_ref[0]
    for item in (3, 2, 1, 0) if reverse else (0, 1, 2, 3):
        out_ref[item, 0] = state
        state = decay * state + parts_ref[item, 0]


def key_value_kernel(
    exp_ref, query_ref, key_ref, value_ref, grad_ref, later_ref, gk_ref, gv_ref, send_ref, *, length
):
    group = pl.program_id(0)
    span = query_ref.shape[0]
    source = lax.broadcasted_iota(jnp.int32, (span, span), 0)
    target = lax.broadcasted_iota(jnp.int32, (span, span), 1)
    gap = (target - source).astype(f32)
    left = span - lax.broadcasted_iota(jnp.int32, (span, WIDTH), 0).astype(f32)
    for slot in range(4):
        rate = log_rate(exp_ref[4 * group + slot], length)
        lanes = pl.ds(slot * WIDTH, WIDTH)
        query, key = query_ref[:, lanes], key_ref[:, lanes]
        value, grad = value_ref[:, lanes], grad_ref[:, lanes]
        mask = jnp.where(gap >= 0.0, jnp.exp(rate * jnp.maximum(gap, 0.0)), 0.0)
        tail = jnp.exp(rate * left)
        grad_scores = jnp.concatenate(halves(dot(value, grad, ((1,), (1,))) * mask), 1)
        key_scores = jnp.concatenate(halves(dot(key, query, ((1,), (1,))) * mask), 1)
        high, low = halves(later_ref[slot, 0])
        gk = tail * dot(
            jnp.concatenate((value, value), 1), jnp.concatenate((high, low), 1), ((1,), (1,))
        )
        gk = gk + dot(grad_scores, jnp.concatenate((query, query), 0), ((1,), (0,)))
        gv = tail * dot(
            jnp.concatenate((key, key), 1), jnp.concatenate((high, low), 0), ((1,), (0,))
        )
        gv = gv + dot(key_scores, jnp.concatenate((grad, grad), 0), ((1,), (0,)))
        gk_ref[:, lanes] = gk.astype(bf16)
        gv_ref[:, lanes] = gv.astype(bf16)
        send_ref[slot, 0] = gk.astype(bf16)
        send_ref[4 + slot, 0] = gv.astype(bf16)


def query_kernel(exp_ref, key_ref, value_ref, grad_ref, state_ref, gq_ref, *, length):
    group = pl.program_id(0)
    span = key_ref.shape[0]
    target = lax.broadcasted_iota(jnp.int32, (span, span), 0)
    source = lax.broadcasted_iota(jnp.int32, (span, span), 1)
    gap = (target - source).astype(f32)
    done = 1.0 + lax.broadcasted_iota(jnp.int32, (span, WIDTH), 0).astype(f32)
    for slot in range(4):
        rate = log_rate(exp_ref[4 * group + slot], length)
        lanes = pl.ds(slot * WIDTH, WIDTH)
        key, value, grad = key_ref[:, lanes], value_ref[:, lanes], grad_ref[:, lanes]
        mask = jnp.where(gap >= 0.0, jnp.exp(rate * jnp.maximum(gap, 0.0)), 0.0)
        scores = jnp.concatenate(halves(dot(grad, value, ((1,), (1,))) * mask), 1)
        high, low = halves(state_ref[slot, 0])
        gq = jnp.exp(rate * done) * dot(
            jnp.concatenate((grad, grad), 1), jnp.concatenate((high, low), 1), ((1,), (1,))
        )
        gq = gq + dot(scores, jnp.concatenate((key, key), 0), ((1,), (0,)))
        gq_ref[:, lanes] = gq.astype(bf16)


def weight_kernel(cols_ref, rows_ref, out_ref, turned):
    @pl.when(pl.program_id(0) == 0)
    def _():
        turned[...] = cols_ref[...].T

    product = dot(turned[...], rows_ref[...], ((1,), (0,))).T
    out_ref[0] = product[:, :WIDTH]
    out_ref[1] = product[:, WIDTH:]


SMEM = pl.BlockSpec(memory_space=pltpu.SMEM)


def call(kernel, grid, in_specs, out_specs, out_shape, args, scratch=(), name=None):
    return pl.pallas_call(
        kernel,
        grid=grid,
        in_specs=in_specs,
        out_specs=out_specs,
        out_shape=out_shape,
        scratch_shapes=scratch,
        name=name,
        compiler_params=pltpu.CompilerParams(vmem_limit_bytes=48 * 1024 * 1024),
    )(*args)


def per_device(inputs_x, queries, keys, values, grad_out, decay_exp, state_in):
    span = queries.shape[1]
    features = queries.shape[2]
    groups = features // (4 * WIDTH)
    depth = lax.axis_size("z")
    length = span * lax.axis_size(CHAIN)
    tile = (WIDTH, WIDTH)
    query, key, value, grad = queries[0], keys[0], values[0], grad_out[0]
    exps = lax.all_gather(decay_exp, CHAIN, axis=0, tiled=True)
    slot = lax.axis_index(QUAD).astype(jnp.int32)[None]
    rows = lax.all_gather(inputs_x[0], PLANE, axis=0, tiled=True)

    head_cols = pl.BlockSpec((span, 4 * WIDTH), lambda i: (0, i))
    quad_tiles = pl.BlockSpec((4, 1) + tile, lambda i: (0, i, 0, 0))
    one_tile = pl.BlockSpec((1,) + tile, lambda i: (i, 0, 0))
    quad_shape = jax.ShapeDtypeStruct((4, groups) + tile, f32)
    line_shape = jax.ShapeDtypeStruct((groups,) + tile, f32)
    token_shape = jax.ShapeDtypeStruct((span, features), bf16)

    def exchange(array, axes):
        return lax.all_to_all(array, axes, split_axis=0, concat_axis=0, tiled=True)

    def updates(left, right, reverse):
        return call(
            functools.partial(update_kernel, reverse=reverse, length=length),
            (groups,), [SMEM, head_cols, head_cols], quad_tiles, quad_shape, (exps, left, right),
            name="updates",
        )

    def joined(parts, reverse):
        return call(
            functools.partial(join_kernel, reverse=reverse, length=length, span=span),
            (groups,), [SMEM, SMEM, quad_tiles], one_tile, line_shape, (exps, slot, parts),
            name="joined",
        )

    def spread(parts, edge, reverse):
        return call(
            functools.partial(spread_kernel, reverse=reverse, length=length, span=span),
            (groups,), [SMEM, SMEM, quad_tiles, one_tile], quad_tiles, quad_shape,
            (exps, slot, parts, edge), name="spread",
        )

    whole = pl.BlockSpec((depth,) + tile, lambda: (0, 0, 0))
    single = pl.BlockSpec(tile, lambda: (0, 0))

    reverse_parts = exchange(updates(query, grad, True), QUAD)
    reverse_groups = exchange(joined(reverse_parts, True), "z")
    reverse_edges, state_grad = call(
        functools.partial(scan_reverse_kernel, length=length, span=4.0 * span),
        (), [SMEM, whole], [whole, single],
        [line_shape, jax.ShapeDtypeStruct(tile, f32)], (decay_exp, reverse_groups), name="scan",
    )
    reverse_edges = exchange(reverse_edges, "z")
    later = exchange(spread(reverse_parts, reverse_edges, True), QUAD)
    grad_key, grad_value, send = call(
        functools.partial(key_value_kernel, length=length),
        (groups,), [SMEM] + 4 * [head_cols] + [quad_tiles],
        [head_cols, head_cols, pl.BlockSpec((8, 1, span, WIDTH), lambda i: (0, i % 4, 0, i // 4))],
        [token_shape, token_shape, jax.ShapeDtypeStruct((8, 4, span, 2 * WIDTH), bf16)],
        (exps, query, key, value, grad, later), name="key_value",
    )
    cols = exchange(send.reshape(32, span, 2 * WIDTH), PLANE).reshape(32 * span, 2 * WIDTH)

    forward_parts = exchange(updates(key, value, False), QUAD)
    forward_groups = exchange(joined(forward_parts, False), "z")
    forward_edges = call(
        functools.partial(scan_forward_kernel, length=length, span=4.0 * span),
        (), [SMEM, single, whole], whole, line_shape,
        (decay_exp, state_in[0, 0], forward_groups), name="scan",
    )
    forward_edges = exchange(forward_edges, "z")
    states = exchange(spread(forward_parts, forward_edges, False), QUAD)
    grad_query = call(
        functools.partial(query_kernel, length=length),
        (groups,), [SMEM] + 3 * [head_cols] + [quad_tiles], head_cols, token_shape,
        (exps, key, value, grad, states), name="query",
    )

    tokens, width = rows.shape
    block = width // 4
    partial = call(
        weight_kernel, (4,),
        [pl.BlockSpec((tokens, 2 * WIDTH), lambda i: (0, 0)), pl.BlockSpec((tokens, block), lambda i: (0, i))],
        pl.BlockSpec((2, block, WIDTH), lambda i: (i, 0, 0)),
        jax.ShapeDtypeStruct((8, block, WIDTH), f32),
        (cols, rows), scratch=[pltpu.VMEM((2 * WIDTH, tokens), bf16)], name="weight",
    )
    summed = lax.psum_scatter(partial, "z", scatter_dimension=0, tiled=True)
    pieces = exchange(summed.reshape(8, block // 8, WIDTH), ("y", "xh"))
    pieces = pieces.reshape(2, 4, block // 8, WIDTH).transpose(0, 2, 1, 3)
    weight_grads = pieces.reshape(2, 1, block // 8, 4 * WIDTH)
    return (
        grad_query[None], grad_key[None], grad_value[None], weight_grads, state_grad[None, None]
    )


def solution(mesh):
    fine = Mesh(mesh.devices.reshape(4, 2, 8, 2, 2), ("y", "xh", "z", "xl", "core"))
    dp, seq = ("y", "xh"), CHAIN
    tokens = P(dp, seq, None)
    in_specs = (tokens, tokens, tokens, tokens, tokens, P(seq), P(dp, seq, None, None))
    out_specs = (tokens, tokens, tokens, P(None, seq, dp, None), P(dp, seq, None, None))
    return jax.shard_map(
        per_device, mesh=fine, in_specs=in_specs, out_specs=out_specs, check_vma=False
    )
```

time: 856 us -> 332 us (0.39); the launches traced: 841 us -> 331 us
  waiting for transfers between devices: 343 us -> 36.5 us
  blocking collectives: 0 us -> 218 us
  other arithmetic: 193 us -> 0 us
  local copies, waits for them, and re-layouts: 171 us -> 10.2 us
  starting transfers between devices: 80 us -> 9.28 us
  Pallas kernels: 0 us -> 42.1 us
  matrix products: 38.3 us -> 0 us
    all_to_all x9 -> x2, waiting for transfers between devices: 343 us -> 35.8 us  [exchange(): return lax.all_to_all(array, axes, split_axis=0, concat_axis=0, tiled=True)]
    all_to_all x0 -> x8, blocking collectives: none -> 199 us  [exchange(): return lax.all_to_all(array, axes, split_axis=0, concat_axis=0, tiled=True)]
    unnamed x8 -> x0, other arithmetic: 163 us -> none
    unnamed x49 -> x23, local copies, waits for them, and re-layouts: 85 us -> 9.04 us
    all_to_all x9 -> x2, starting transfers between devices: 80 us -> 9.2 us  [exchange(): return lax.all_to_all(array, axes, split_axis=0, concat_axis=0, tiled=True)]
    convert_element_type x6 -> x0, local copies, waits for them, and re-layouts: 43.6 us -> none  [join_blocks(): return joined.astype(jnp.bfloat16)]
    pallas_call x0 -> x11, Pallas kernels: none -> 42.1 us  [call(): pl.pallas_call(kernel, grid=grid, in_specs=in_specs, out_specs=out_specs,...]
    dot_general x11 -> x0, matrix products: 38.3 us -> none  [the longest x1 12.2 us: weight_blocks(): jnp.dot(row_block.T, col_block, preferred_element_type=jnp.float32)]
  transfers between devices with their start and end apart: 10 -> 4, of which waited for: 4 -> 2; matrix products, arithmetic and copies ran while one was open for 41% -> 1% of each run, Pallas kernels for 0% -> 9%
where the time goes in v1:
time: 332 us; the launch traced here: 331 us
  blocking collectives  218 us (66%)
  Pallas kernels  42.1 us (13%)
  waiting for transfers between devices  36.5 us (11%)
  between operations  14.8 us (4%)
  local copies, waits for them, and re-layouts  10.2 us (3%)
  starting transfers between devices  9.28 us (3%)
    all_to_all x8, blocking collectives, exchange(): return lax.all_to_all(array, axes, split_axis=0, concat_axis=0, tiled=True)  199 us
    pallas_call x11, Pallas kernels, call(): pl.pallas_call(kernel, grid=grid, in_specs=in_specs, out_specs=out_specs,...  42.1 us
    all_to_all x2, waiting for transfers between devices, exchange(): return lax.all_to_all(array, axes, split_axis=0, concat_axis=0, tiled=True)  35.8 us
    unnamed x1, blocking collectives  18.5 us
    all_to_all x2, starting transfers between devices, exchange(): return lax.all_to_all(array, axes, split_axis=0, concat_axis=0, tiled=True)  9.2 us
    unnamed x23, local copies, waits for them, and re-layouts  9.04 us
  transfers between devices with their start and end apart: 4, of which 2 were waited for; matrix products, arithmetic and copies ran while one was open for 1% of the time, Pallas kernels for 9%

profile of v1, /device:TPU:32, one launch (start us, length us, event | category | flops | bytes accessed | tf_op | source)
XLA Modules:
  0.0 330.6 jit_solution(8600305266905585338)
XLA Ops:
  7.2 0.0 all-gather.3.cloned.1.call-start
  7.2 0.7 all-gather.3.cloned.1.call-update
  8.6 1.3 dynamic-slice
  9.8 0.8 dynamic-update-slice
  10.6 18.5 %all-reduce.exp_ref = s32[32]{0:T(128)S(1)} all-reduce(s32[32]{0:T(128)S(1)} %dynamic-update-slice), channel_id=1, replica_groups=mesh['y'=4,'xh'=2,'z'=8,'xl'=2,'core'=2] {'z','xl','core'}, use_global_device_ids=true, to_apply=%add | all-reduce | flops 32 | bytes 256
  29.0 0.0 copy-start.2
  29.0 1.2 copy-done.2
  30.3 0.0 copy-start.7
  30.3 1.2 copy-done.7
  31.5 3.4 %updates.3 = f32[4,8,128,128]{3,2,1,0:T(8,128)S(1)} custom-call(s32[32]{0:T(128)S(1)} %all-reduce.exp_ref, bf16[128,4096]{1,0:T(8,128)(2,1)S(1)} %bitcast.29, bf16[128,4096]{1,0:T(8,128)(2,1)S(1)} %bitcast.25), custom_call_target="tpu_custom_call" | custom-call | tf_op jit(solution)/shard_map/updates/pallas_call | solution.py:156
  34.9 0.0 copy-start.5
  34.9 1.4 copy-done.5
  36.2 3.6 %all-to-all-start.4 = ((f32[4,8,128,128]{3,2,1,0:T(8,128)}), f32[4,8,128,128]{3,2,1,0:T(8,128)S(1)}, u32[]{:S(2)}, u32[]{:S(2)}) async-start(f32[4,8,128,128]{3,2,1,0:T(8,128)} %copy-done.5), calls=%async_computation.4 | async-start | bytes 4194304 | tf_op jit(solution)/shard_map/all_to_all | solution.py:188
  39.8 0.0 reduce-scatter.2.cloned.1.call-start
  39.9 33.7 %all-to-all-done.4.parts_ref = f32[4,8,128,128]{3,2,1,0:T(8,128)S(1)} async-done(((f32[4,8,128,128]{3,2,1,0:T(8,128)}), f32[4,8,128,128]{3,2,1,0:T(8,128)S(1)}, u32[]{:S(2)}, u32[]{:S(2)}) %all-to-all-start.4) | async-done | bytes 2097184 | tf_op jit(solution)/shard_map/all_to_all | solution.py:188
  73.6 1.1 joined.3
  74.7 20.5 %all_to_all.50.parts_ref = f32[8,128,128]{2,1,0:T(8,128)S(1)} all-to-all(f32[8,128,128]{2,1,0:T(8,128)S(1)} %joined.3), channel_id=1, replica_groups=mesh['y'=4,'xh'=2,'z'=8,'xl'=2,'core'=2] {'z'}, dimensions={0} | all-to-all | bytes 1048576 | tf_op jit(solution)/shard_map/all_to_all | solution.py:188
  95.2 0.7 scan.3
  95.9 18.4 %all_to_all.51.edge_ref = f32[8,128,128]{2,1,0:T(8,128)S(1)} all-to-all(f32[8,128,128]{2,1,0:T(8,128)S(1)} %get-tuple-element.10), channel_id=1, replica_groups=mesh['y'=4,'xh'=2,'z'=8,'xl'=2,'core'=2] {'z'}, dimensions={0} | all-to-all | bytes 1048576 | tf_op jit(solution)/shard_map/all_to_all | solution.py:188
  114.3 1.3 spread.3
  115.6 0.0 copy-start
  115.6 0.0 copy-start.1
  115.6 0.0 copy-start.3
  115.7 0.0 copy-start.8
  115.7 29.2 %all_to_all.52.later_ref = f32[4,8,128,128]{3,2,1,0:T(8,128)} all-to-all(f32[4,8,128,128]{3,2,1,0:T(8,128)S(1)} %spread.3), channel_id=1, replica_groups=mesh['y'=4,'xh'=2,'z'=8,'xl'=2,'core'=2] {'xl','core'}, dimensions={0} | all-to-all | bytes 4194304 | tf_op jit(solution)/shard_map/all_to_all | solution.py:188
  144.9 0.0 copy-done
  144.9 0.0 copy-done.1
  144.9 0.0 copy-done.3
  144.9 0.0 copy-done.8
  144.9 10.0 %key_value.1 = (bf16[128,4096]{1,0:T(8,128)(2,1)}, bf16[128,4096]{1,0:T(8,128)(2,1)}, bf16[8,4,128,256]{3,2,1,0:T(8,128)(2,1)}) custom-call(s32[32]{0:T(128)S(1)} %all-reduce.exp_ref, bf16[128,4096]{1,0:T(8,128)(2,1)S(1)} %bitcast.30, bf16[128,4096]{1,0:T(8,128)(2,1)S(1)} %bitcast.19, bf16[128,4096]{1,0:T(8,128)(2,1)S(1)} %bitcast.22, ...), custom_call_target="tpu_custom_call" | custom-call | tf_op jit(solution)/shard_map/key_value/pallas_call | solution.py:156
  154.9 34.4 %all_to_all.53 = bf16[32,128,256]{2,1,0:T(8,128)(2,1)} all-to-all(bf16[32,128,256]{2,1,0:T(8,128)(2,1)} %bitcast.33), channel_id=1, replica_groups=mesh['y'=4,'xh'=2,'z'=8,'xl'=2,'core'=2] {'y','xh','xl','core'}, dimensions={0} | all-to-all | bytes 4194304 | tf_op jit(solution)/shard_map/all_to_all | solution.py:188
  189.3 1.6 copy-done.6
  190.9 13.7 %weight.1 = f32[8,768,128]{2,1,0:T(8,128)} custom-call(bf16[4096,256]{1,0:T(8,128)(2,1)S(1)} %bitcast.28, bf16[4096,3072]{1,0:T(8,128)(2,1)} %bitcast.32), custom_call_target="tpu_custom_call" | custom-call | tf_op jit(solution)/shard_map/weight/pallas_call | solution.py:156
  204.6 0.0 reduce-scatter.2.cloned.1.call-update
  204.7 3.4 %updates.2 = f32[4,8,128,128]{3,2,1,0:T(8,128)S(1)} custom-call(s32[32]{0:T(128)S(1)} %all-reduce.exp_ref, bf16[128,4096]{1,0:T(8,128)(2,1)S(1)} %bitcast.20, bf16[128,4096]{1,0:T(8,128)(2,1)S(1)} %bitcast.23), custom_call_target="tpu_custom_call" | custom-call | tf_op jit(solution)/shard_map/updates/pallas_call | solution.py:156
  208.0 28.2 %all_to_all.54.parts_ref = f32[4,8,128,128]{3,2,1,0:T(8,128)S(1)} all-to-all(f32[4,8,128,128]{3,2,1,0:T(8,128)S(1)} %updates.2), channel_id=1, replica_groups=mesh['y'=4,'xh'=2,'z'=8,'xl'=2,'core'=2] {'xl','core'}, dimensions={0} | all-to-all | bytes 4194304 | tf_op jit(solution)/shard_map/all_to_all | solution.py:188
  236.2 1.1 joined.2
  237.3 20.2 %all_to_all.55.parts_ref = f32[8,128,128]{2,1,0:T(8,128)S(1)} all-to-all(f32[8,128,128]{2,1,0:T(8,128)S(1)} %joined.2), channel_id=1, replica_groups=mesh['y'=4,'xh'=2,'z'=8,'xl'=2,'core'=2] {'z'}, dimensions={0} | all-to-all | bytes 1048576 | tf_op jit(solution)/shard_map/all_to_all | solution.py:188
  257.5 0.0 copy-done.9
  257.6 19.4 %all_to_all.56.edge_ref = f32[8,128,128]{2,1,0:T(8,128)S(1)} all-to-all(f32[8,128,128]{2,1,0:T(8,128)S(1)} %scan.2), channel_id=1, replica_groups=mesh['y'=4,'xh'=2,'z'=8,'xl'=2,'core'=2] {'z'}, dimensions={0} | all-to-all | bytes 1048576 | tf_op jit(solution)/shard_map/all_to_all | solution.py:188
  277.0 1.3 spread.2
  278.2 28.9 %all_to_all.57.state_ref = f32[4,8,128,128]{3,2,1,0:T(8,128)} all-to-all(f32[4,8,128,128]{3,2,1,0:T(8,128)S(1)} %spread.2), channel_id=1, replica_groups=mesh['y'=4,'xh'=2,'z'=8,'xl'=2,'core'=2] {'xl','core'}, dimensions={0} | all-to-all | bytes 4194304 | tf_op jit(solution)/shard_map/all_to_all | solution.py:188
  307.2 5.6 %all-to-all-start.9 = ((f32[8,96,128]{2,1,0:T(8,128)}), f32[8,96,128]{2,1,0:T(8,128)S(1)}, u32[]{:S(2)}, u32[]{:S(2)}) async-start(f32[8,96,128]{2,1,0:T(8,128)} %bitcast.37), calls=%async_computation.10 | async-start | bytes 786432 | tf_op jit(solution)/shard_map/all_to_all | solution.py:188
  312.8 1.6 copy-done.4
  314.3 6.2 %query.1 = bf16[128,4096]{1,0:T(8,128)(2,1)} custom-call(s32[32]{0:T(128)S(1)} %all-reduce.exp_ref, bf16[128,4096]{1,0:T(8,128)(2,1)S(1)} %bitcast.21, bf16[128,4096]{1,0:T(8,128)(2,1)S(1)} %bitcast.24, bf16[128,4096]{1,0:T(8,128)(2,1)S(1)} %bitcast.27, f32[4,8,128,128]{3,2,1,0:T(8,128)S(1)} %copy-done.4), custom_call_target="tpu_custom_call" | custom-call | tf_op jit(solution)/shard_map/query/pallas_call | solution.py:156
  320.5 2.0 all-to-all-done.9
  322.6 0.3 copy.14
  322.8 0.9 reshape.29
  (7 shorter events, 0.1 us)
Async XLA Ops:
  7.2 182.2 %all-gather.3.cloned.1.call-start = ((), (), s32[]{:S(2)}) async-start(), calls=%async_computation.12 | async-start | bytes 25952256 | tf_op jit(solution)/shard_map/all_gather | solution.py:178
  29.0 1.2 copy-start.2
  30.3 1.2 copy-start.7
  34.9 1.4 copy-start.5
  36.2 37.4 %all-to-all-start.4 = ((f32[4,8,128,128]{3,2,1,0:T(8,128)}), f32[4,8,128,128]{3,2,1,0:T(8,128)S(1)}, u32[]{:S(2)}, u32[]{:S(2)}) async-start(f32[4,8,128,128]{3,2,1,0:T(8,128)} %copy-done.5), calls=%async_computation.4 | async-start | bytes 4194304 | tf_op jit(solution)/shard_map/all_to_all | solution.py:188
  39.8 267.3 %reduce-scatter.2.cloned.1.call-start = ((), (), s32[]{:S(2)}) async-start(), calls=%async_computation.11 | async-start | bytes 3538944 | tf_op jit(solution)/shard_map/reduce_scatter | solution.py:256
  115.6 29.2 %copy-start = (bf16[1,128,4096]{2,1,0:T(8,128)(2,1)S(1)}, bf16[1,128,4096]{2,1,0:T(8,128)(2,1)}, u32[]{:S(2)}) copy-start(bf16[1,128,4096]{2,1,0:T(8,128)(2,1)} %param.9) | copy-start | bytes 3145732
  115.6 29.2 %copy-start.1 = (bf16[1,128,4096]{2,1,0:T(8,128)(2,1)S(1)}, bf16[1,128,4096]{2,1,0:T(8,128)(2,1)}, u32[]{:S(2)}) copy-start(bf16[1,128,4096]{2,1,0:T(8,128)(2,1)} %param.10) | copy-start | bytes 3145732
  115.6 29.2 %copy-start.3 = (bf16[1,128,4096]{2,1,0:T(8,128)(2,1)S(1)}, bf16[1,128,4096]{2,1,0:T(8,128)(2,1)}, u32[]{:S(2)}) copy-start(bf16[1,128,4096]{2,1,0:T(8,128)(2,1)} %param.11) | copy-start | bytes 3145732
  115.7 29.2 %copy-start.8 = (bf16[1,128,4096]{2,1,0:T(8,128)(2,1)S(1)}, bf16[1,128,4096]{2,1,0:T(8,128)(2,1)}, u32[]{:S(2)}) copy-start(bf16[1,128,4096]{2,1,0:T(8,128)(2,1)} %param.8) | copy-start | bytes 3145732
  189.3 1.6 copy-start.6
  236.2 21.3 %copy-start.9 = (f32[1,1,128,128]{3,2,1,0:T(8,128)S(1)}, f32[1,1,128,128]{3,2,1,0:T(8,128)}, u32[]{:S(2)}) copy-start(f32[1,1,128,128]{3,2,1,0:T(8,128)} %param.13) | copy-start | bytes 196612
  307.2 15.4 %all-to-all-start.9 = ((f32[8,96,128]{2,1,0:T(8,128)}), f32[8,96,128]{2,1,0:T(8,128)S(1)}, u32[]{:S(2)}, u32[]{:S(2)}) async-start(f32[8,96,128]{2,1,0:T(8,128)} %bitcast.37), calls=%async_computation.10 | async-start | bytes 786432 | tf_op jit(solution)/shard_map/all_to_all | solution.py:188
  312.8 1.6 copy-start.4
Sparse Core Ops, SparseCore 0:
  10.5 107.2 all-gather.2
  204.8 40.1 reduce-scatter.1

commit v2 on v1

v2 whole, which is shorter than its diff:
```python
import functools

import jax
import jax.numpy as jnp
from jax import lax
from jax.experimental import pallas as pl
from jax.experimental.pallas import tpu as pltpu
from jax.sharding import Mesh
from jax.sharding import PartitionSpec as P

WIDTH = 128
f32 = jnp.float32
bf16 = jnp.bfloat16
PLANE = ("y", "xh", "xl", "core")
QUAD = ("xl", "core")
CHAIN = ("z", "xl", "core")


def log_rate(exponent, length):
    return -(jnp.left_shift(1, exponent).astype(f32)) * (1.0 / length)


def power_of(rate, steps):
    return jnp.exp(jnp.full((1, WIDTH), rate * steps, f32))


def halves(wide):
    high = wide.astype(bf16)
    return high, (wide - high.astype(f32)).astype(bf16)


def dot(left, right, dims):
    return lax.dot_general(left, right, (dims, ((), ())), preferred_element_type=f32)


def update_kernel(here_ref, exp_ref, left_ref, right_ref, keep_ref, send_ref, *, reverse, length):
    group = pl.program_id(0)
    span = left_ref.shape[0]
    rows = lax.broadcasted_iota(jnp.int32, (span, WIDTH), 0).astype(f32)
    steps = rows if reverse else (span - 1.0) - rows
    for slot in range(4):
        rate = log_rate(exp_ref[4 * group + slot], length)
        lanes = pl.ds(slot * WIDTH, WIDTH)
        high, low = halves(left_ref[:, lanes].astype(f32) * jnp.exp(rate * steps))
        right = right_ref[:, lanes]
        update = dot(
            jnp.concatenate((high, low), 0), jnp.concatenate((right, right), 0), ((0,), (0,))
        )
        chip = jnp.bitwise_xor(here_ref[1], slot // 2)

        @pl.when(here_ref[2] == slot % 2)
        def _(update=update, chip=chip):
            keep_ref[0, chip] = update

        @pl.when(here_ref[2] != slot % 2)
        def _(update=update, chip=chip):
            send_ref[0, chip] = update


def weighed(mine, other, position, reverse, rate, span):
    position = position.astype(f32)
    later = position if reverse else 1.0 - position
    return power_of(rate, span * later) * mine + power_of(rate, span * (1.0 - later)) * other


def chip_kernel(
    here_ref, exp_ref, mine_ref, other_ref, after_ref, keep_ref, send_ref,
    *, reverse, length, span
):
    group = pl.program_id(0)
    for chip, out_ref in enumerate((keep_ref, send_ref)):
        head = 4 * group + 2 * jnp.bitwise_xor(here_ref[1], chip) + here_ref[2]
        rate = log_rate(exp_ref[head], length)
        out_ref[0] = weighed(
            mine_ref[0, chip], other_ref[0, chip], here_ref[2], reverse, rate, span
        )


def quad_kernel(here_ref, exp_ref, mine_ref, other_ref, out_ref, *, length, span):
    for group in range(out_ref.shape[0]):
        rate = log_rate(exp_ref[4 * group + 2 * here_ref[1] + here_ref[2]], length)
        out_ref[group] = weighed(
            mine_ref[group], other_ref[group], here_ref[1], True, rate, span
        )


def turn_kernel(
    here_ref, exp_ref, own_ref, parts_ref, mine_ref, other_ref, out_ref, grad_ref, *, length, span
):
    rate = log_rate(own_ref[0], length)
    decay = power_of(rate, 2.0 * span)
    state = jnp.zeros(grad_ref.shape, f32)
    for group in reversed(range(parts_ref.shape[0])):
        out_ref[group, 0] = state
        state = decay * state + parts_ref[group]
    grad_ref[...] = power_of(rate, 1.0) * state
    for group in range(parts_ref.shape[0]):
        rate = log_rate(exp_ref[4 * group + 2 * here_ref[1] + here_ref[2]], length)
        out_ref[group, 1] = weighed(
            mine_ref[group], other_ref[group], here_ref[1], False, rate, span
        )


def scan_kernel(own_ref, parts_ref, first_ref, after_ref, out_ref, *, length, span):
    decay = power_of(log_rate(own_ref[0], length), span)
    state = first_ref[...]
    for group in range(parts_ref.shape[0]):
        out_ref[group, 0] = state
        state = decay * state + parts_ref[group, 0]


def chip_state_kernel(
    here_ref, exp_ref, edge_ref, mine_ref, other_ref, keep_ref, send_ref, *, reverse, length, span
):
    behind = here_ref[1] == (0 if reverse else 1)
    for group in range(edge_ref.shape[0]):
        rate = log_rate(exp_ref[4 * group + 2 * here_ref[1] + here_ref[2]], length)
        edge = edge_ref[group, 0]
        past = power_of(rate, span) * edge
        keep_ref[group] = jnp.where(behind, past + other_ref[group], edge)
        send_ref[group] = jnp.where(behind, edge, past + mine_ref[group])


def core_state_kernel(
    here_ref, exp_ref, mine_edge_ref, other_edge_ref, mine_ref, other_ref, keep_ref, send_ref,
    *, reverse, length, span
):
    group = pl.program_id(0)
    behind = here_ref[2] == (0 if reverse else 1)
    for chip, edge_ref in enumerate((mine_edge_ref, other_edge_ref)):
        head = 4 * group + 2 * jnp.bitwise_xor(here_ref[1], chip) + here_ref[2]
        rate = log_rate(exp_ref[head], length)
        edge = edge_ref[0]
        past = power_of(rate, span) * edge
        keep_ref[0, chip] = jnp.where(behind, past + other_ref[0, chip], edge)
        send_ref[0, chip] = jnp.where(behind, edge, past + mine_ref[0, chip])


def picked(here_ref, mine_ref, other_ref, slot):
    chip = jnp.bitwise_xor(here_ref[1], slot // 2)
    return jnp.where(here_ref[2] == slot % 2, mine_ref[0, chip], other_ref[0, chip])


def key_value_kernel(
    here_ref, exp_ref, query_ref, key_ref, value_ref, grad_ref, mine_ref, other_ref,
    gk_ref, gv_ref, send_ref, *, length
):
    group = pl.program_id(0)
    span = query_ref.shape[0]
    source = lax.broadcasted_iota(jnp.int32, (span, span), 0)
    target = lax.broadcasted_iota(jnp.int32, (span, span), 1)
    gap = (target - source).astype(f32)
    left = span - lax.broadcasted_iota(jnp.int32, (span, WIDTH), 0).astype(f32)
    for slot in range(4):
        rate = log_rate(exp_ref[4 * group + slot], length)
        lanes = pl.ds(slot * WIDTH, WIDTH)
        query, key = query_ref[:, lanes], key_ref[:, lanes]
        value, grad = value_ref[:, lanes], grad_ref[:, lanes]
        mask = jnp.where(gap >= 0.0, jnp.exp(rate * jnp.maximum(gap, 0.0)), 0.0)
        tail = jnp.exp(rate * left)
        grad_scores = jnp.concatenate(halves(dot(value, grad, ((1,), (1,))) * mask), 1)
        key_scores = jnp.concatenate(halves(dot(key, query, ((1,), (1,))) * mask), 1)
        high, low = halves(picked(here_ref, mine_ref, other_ref, slot))
        gk = tail * dot(
            jnp.concatenate((value, value), 1), jnp.concatenate((high, low), 1), ((1,), (1,))
        )
        gk = gk + dot(grad_scores, jnp.concatenate((query, query), 0), ((1,), (0,)))
        gv = tail * dot(
            jnp.concatenate((key, key), 1), jnp.concatenate((high, low), 0), ((1,), (0,))
        )
        gv = gv + dot(key_scores, jnp.concatenate((grad, grad), 0), ((1,), (0,)))
        gk_ref[:, lanes] = gk.astype(bf16)
        gv_ref[:, lanes] = gv.astype(bf16)
        send_ref[slot, 0] = gk.astype(bf16)
        send_ref[4 + slot, 0] = gv.astype(bf16)


def query_kernel(
    here_ref, exp_ref, key_ref, value_ref, grad_ref, mine_ref, other_ref, gq_ref, *, length
):
    group = pl.program_id(0)
    span = key_ref.shape[0]
    target = lax.broadcasted_iota(jnp.int32, (span, span), 0)
    source = lax.broadcasted_iota(jnp.int32, (span, span), 1)
    gap = (target - source).astype(f32)
    done = 1.0 + lax.broadcasted_iota(jnp.int32, (span, WIDTH), 0).astype(f32)
    for slot in range(4):
        rate = log_rate(exp_ref[4 * group + slot], length)
        lanes = pl.ds(slot * WIDTH, WIDTH)
        key, value, grad = key_ref[:, lanes], value_ref[:, lanes], grad_ref[:, lanes]
        mask = jnp.where(gap >= 0.0, jnp.exp(rate * jnp.maximum(gap, 0.0)), 0.0)
        scores = jnp.concatenate(halves(dot(grad, value, ((1,), (1,))) * mask), 1)
        high, low = halves(picked(here_ref, mine_ref, other_ref, slot))
        gq = jnp.exp(rate * done) * dot(
            jnp.concatenate((grad, grad), 1), jnp.concatenate((high, low), 1), ((1,), (1,))
        )
        gq = gq + dot(scores, jnp.concatenate((key, key), 0), ((1,), (0,)))
        gq_ref[:, lanes] = gq.astype(bf16)


def weight_kernel(cols_ref, rows_ref, out_ref, turned):
    @pl.when(pl.program_id(0) == 0)
    def _():
        turned[...] = cols_ref[...].T

    product = dot(turned[...], rows_ref[...], ((1,), (0,))).T
    out_ref[0] = product[:, :WIDTH]
    out_ref[1] = product[:, WIDTH:]


SMEM = pl.BlockSpec(memory_space=pltpu.SMEM)
FREE = pl.BlockSpec(memory_space=pl.ANY)


def call(kernel, grid, in_specs, out_specs, out_shape, args, scratch=(), name=None):
    return pl.pallas_call(
        kernel,
        grid=grid,
        in_specs=in_specs,
        out_specs=out_specs,
        out_shape=out_shape,
        scratch_shapes=scratch,
        name=name,
        compiler_params=pltpu.CompilerParams(vmem_limit_bytes=48 * 1024 * 1024),
    )(*args)


def exchange(array, axes):
    return lax.all_to_all(array, axes, split_axis=0, concat_axis=0, tiled=True)


def per_device(inputs_x, queries, keys, values, grad_out, decay_exp, state_in):
    span = queries.shape[1]
    features = queries.shape[2]
    groups = features // (4 * WIDTH)
    length = span * lax.axis_size(CHAIN)
    tile = (WIDTH, WIDTH)
    query, key, value, grad = queries[0], keys[0], values[0], grad_out[0]
    exps = lax.all_gather(decay_exp, CHAIN, axis=0, tiled=True)
    here = jnp.stack([lax.axis_index(axis) for axis in CHAIN]).astype(jnp.int32)
    rows = lax.all_gather(inputs_x[0], PLANE, axis=0, tiled=True)

    head_cols = pl.BlockSpec((span, 4 * WIDTH), lambda i: (0, i))
    pair_tiles = pl.BlockSpec((1, 2) + tile, lambda i: (i, 0, 0, 0))
    line_tile = pl.BlockSpec((1,) + tile, lambda i: (i, 0, 0))
    line = pl.BlockSpec((groups,) + tile, lambda i: (0, 0, 0))
    single = pl.BlockSpec(tile, lambda i: (0, 0))
    pair_shape = jax.ShapeDtypeStruct((groups, 2) + tile, f32)
    line_shape = jax.ShapeDtypeStruct((groups,) + tile, f32)
    tile_shape = jax.ShapeDtypeStruct(tile, f32)
    token_shape = jax.ShapeDtypeStruct((span, features), bf16)

    def swap(array, axis):
        return lax.ppermute(array, axis, [(0, 1), (1, 0)])

    def run(body, grid, in_specs, out_specs, out_shape, args, after=None, scratch=(), name=None, **sizes):
        if after is not None:
            in_specs, args = in_specs + [FREE], args + (after,)
        return call(
            functools.partial(body, length=length, **sizes), grid, in_specs, out_specs, out_shape,
            args, scratch, name,
        )

    def updates(left, right, reverse):
        return run(
            update_kernel, (groups,), [SMEM, SMEM, head_cols, head_cols], [pair_tiles, pair_tiles],
            [pair_shape, pair_shape], (here, exps, left, right), reverse=reverse, name="updates",
        )

    def chip(mine, other, reverse, after):
        return run(
            chip_kernel, (groups,), [SMEM, SMEM, pair_tiles, pair_tiles], [line_tile, line_tile],
            [line_shape, line_shape], (here, exps, mine, other), after,
            reverse=reverse, span=float(span), name="chip",
        )

    def chip_state(edges, item, mine, other, reverse):
        spec = pl.BlockSpec((groups, 1) + tile, lambda i: (0, item, 0, 0))
        return run(
            chip_state_kernel, (1,), [SMEM, SMEM, spec, line, line], [line, line],
            [line_shape, line_shape], (here, exps, edges, mine, other),
            reverse=reverse, span=2.0 * span, name="chip_state",
        )

    def core_state(mine_edge, other_edge, mine, other, reverse):
        return run(
            core_state_kernel, (groups,),
            [SMEM, SMEM, line_tile, line_tile, pair_tiles, pair_tiles], [pair_tiles, pair_tiles],
            [pair_shape, pair_shape], (here, exps, mine_edge, other_edge, mine, other),
            reverse=reverse, span=float(span), name="core_state",
        )

    r_mine, sent = updates(query, grad, True)
    r_other = swap(sent, "core")
    f_mine, sent = updates(key, value, False)
    f_other = swap(sent, "core")
    r_chip, sent = chip(r_mine, r_other, True, f_mine)
    r_next = swap(sent, "xl")
    r_parts = exchange(run(
        quad_kernel, (1,), [SMEM, SMEM, line, line], line, line_shape,
        (here, exps, r_chip, r_next), span=2.0 * span, name="quad",
    ), "z")
    f_chip, sent = chip(f_mine, f_other, False, r_next)
    f_next = swap(sent, "xl")
    turned, state_grad = run(
        turn_kernel, (1,), [SMEM, SMEM, SMEM, line, line, line],
        [pl.BlockSpec((groups, 2) + tile, lambda i: (0, 0, 0, 0)), single],
        [pair_shape, tile_shape],
        (here, exps, decay_exp, r_parts, f_chip, f_next), span=2.0 * span, name="turn",
    )
    turned = exchange(turned, "z")
    r_edge, sent = chip_state(turned, 0, r_chip, r_next, True)
    r_far = swap(sent, "xl")
    mine, sent = core_state(r_edge, r_far, r_mine, r_other, True)
    other = swap(sent, "core")
    grad_key, grad_value, send = run(
        key_value_kernel, (groups,), [SMEM, SMEM] + 4 * [head_cols] + 2 * [pair_tiles],
        [head_cols, head_cols, pl.BlockSpec((8, 1, span, WIDTH), lambda i: (0, i % 4, 0, i // 4))],
        [token_shape, token_shape, jax.ShapeDtypeStruct((8, 4, span, 2 * WIDTH), bf16)],
        (here, exps, query, key, value, grad, mine, other), name="key_value",
    )
    cols = exchange(send.reshape(32, span, 2 * WIDTH), PLANE).reshape(32 * span, 2 * WIDTH)

    tokens, width = rows.shape
    block = width // 4
    partial = call(
        weight_kernel, (4,),
        [
            pl.BlockSpec((tokens, 2 * WIDTH), lambda i: (0, 0)),
            pl.BlockSpec((tokens, block), lambda i: (0, i)),
        ],
        pl.BlockSpec((2, block, WIDTH), lambda i: (i, 0, 0)),
        jax.ShapeDtypeStruct((8, block, WIDTH), f32),
        (cols, rows), scratch=[pltpu.VMEM((2 * WIDTH, tokens), bf16)], name="weight",
    )
    f_edges = exchange(run(
        scan_kernel, (1,),
        [SMEM, pl.BlockSpec((groups, 1) + tile, lambda i: (0, 1, 0, 0)), single, FREE],
        pl.BlockSpec((groups, 1) + tile, lambda i: (0, 0, 0, 0)),
        jax.ShapeDtypeStruct((groups, 1) + tile, f32),
        (decay_exp, turned, state_in[0, 0], partial), span=4.0 * span, name="scan",
    ), "z")
    f_edge, sent = chip_state(f_edges, 0, f_chip, f_next, False)
    f_far = swap(sent, "xl")
    mine, sent = core_state(f_edge, f_far, f_mine, f_other, False)
    other = swap(sent, "core")
    grad_query = run(
        query_kernel, (groups,), [SMEM, SMEM] + 3 * [head_cols] + 2 * [pair_tiles], head_cols,
        token_shape, (here, exps, key, value, grad, mine, other), name="query",
    )
    summed = lax.psum_scatter(partial, "z", scatter_dimension=0, tiled=True)
    pieces = exchange(summed.reshape(8, block // 8, WIDTH), ("y", "xh"))
    pieces = pieces.reshape(2, 4, block // 8, WIDTH).transpose(0, 2, 1, 3)
    weight_grads = pieces.reshape(2, 1, block // 8, 4 * WIDTH)
    return (
        grad_query[None], grad_key[None], grad_value[None], weight_grads, state_grad[None, None]
    )


def solution(mesh):
    fine = Mesh(mesh.devices.reshape(4, 2, 8, 2, 2), ("y", "xh", "z", "xl", "core"))
    dp, seq = ("y", "xh"), CHAIN
    tokens = P(dp, seq, None)
    in_specs = (tokens, tokens, tokens, tokens, tokens, P(seq), P(dp, seq, None, None))
    out_specs = (tokens, tokens, tokens, P(None, seq, dp, None), P(dp, seq, None, None))
    return jax.shard_map(
        per_device, mesh=fine, in_specs=in_specs, out_specs=out_specs, check_vma=False
    )
```

time: 332 us -> 297 us (0.89)
  blocking collectives: 218 us -> 112 us
  waiting for transfers between devices: 36.5 us -> 72 us
  Pallas kernels: 42.1 us -> 61.1 us
  local copies, waits for them, and re-layouts: 10.2 us -> 21.2 us
  starting transfers between devices: 9.28 us -> 13 us
    all_to_all x8 -> x3, blocking collectives: 199 us -> 93.3 us  [exchange(): return lax.all_to_all(array, axes, split_axis=0, concat_axis=0, tiled=True)]
    ppermute x0 -> x8, waiting for transfers between devices: none -> 67.1 us  [swap(): return lax.ppermute(array, axis, [(0, 1), (1, 0)])]
    all_to_all x2, waiting for transfers between devices: 35.8 us -> 0.01 us  [exchange(): return lax.all_to_all(array, axes, split_axis=0, concat_axis=0, tiled=True)]
    pallas_call x11 -> x14, Pallas kernels: 42.1 us -> 61.1 us  [call(): pl.pallas_call(kernel, grid=grid, in_specs=in_specs, out_specs=out_specs,...]
    unnamed x23 -> x65, local copies, waits for them, and re-layouts: 9.04 us -> 20 us
    ppermute x0 -> x8, starting transfers between devices: none -> 4.56 us  [swap(): return lax.ppermute(array, axis, [(0, 1), (1, 0)])]
    reduce_scatter x1, waiting for transfers between devices: 0.01 us -> 4.24 us  [per_device(): summed = lax.psum_scatter(partial, 'z', scatter_dimension=0, tiled=True)]
  transfers between devices with their start and end apart: 4 -> 12, of which waited for: 2 -> 6; matrix products, arithmetic and copies ran while one was open for 1% -> 1% of each run, Pallas kernels for 9% -> 16%
where the time goes in v2:
time: 297 us; the launch traced here: 294 us
  blocking collectives  112 us (38%)
  waiting for transfers between devices  72 us (24%)
  Pallas kernels  61.1 us (21%)
  local copies, waits for them, and re-layouts  21.2 us (7%)
  between operations  14.9 us (5%)
  starting transfers between devices  13 us (4%)
    all_to_all x3, blocking collectives, exchange(): return lax.all_to_all(array, axes, split_axis=0, concat_axis=0, tiled=True)  93.3 us
    ppermute x8, waiting for transfers between devices, swap(): return lax.ppermute(array, axis, [(0, 1), (1, 0)])  67.1 us
    pallas_call x14, Pallas kernels, call(): pl.pallas_call(kernel, grid=grid, in_specs=in_specs, out_specs=out_specs,...  61.1 us
    unnamed x65, local copies, waits for them, and re-layouts  20 us
    unnamed x1, blocking collectives  18.5 us
    all_to_all x2, starting transfers between devices, exchange(): return lax.all_to_all(array, axes, split_axis=0, concat_axis=0, tiled=True)  8.42 us
  transfers between devices with their start and end apart: 12, of which 6 were waited for; matrix products, arithmetic and copies ran while one was open for 1% of the time, Pallas kernels for 16%

profile of v2, /device:TPU:32, one launch (start us, length us, event | category | flops | bytes accessed | tf_op | source)
XLA Modules:
  0.0 294.0 jit_solution(7812128167790783582)
XLA Ops:
  7.2 0.7 all-gather.3.cloned.1.call-update
  8.6 1.3 dynamic-slice
  9.8 0.8 dynamic-update-slice
  10.6 18.5 %all-reduce.exp_ref = s32[32]{0:T(128)S(1)} all-reduce(s32[32]{0:T(128)S(1)} %dynamic-update-slice), channel_id=1, replica_groups=mesh['y'=4,'xh'=2,'z'=8,'xl'=2,'core'=2] {'z','xl','core'}, use_global_device_ids=true, to_apply=%add | all-reduce | flops 32 | bytes 256
  29.1 1.2 copy-done.4
  30.4 1.2 copy-done.14
  31.6 8.1 %updates.2 = (f32[8,2,128,128]{3,2,1,0:T(8,128)S(1)}, f32[8,2,128,128]{3,2,1,0:T(8,128)S(1)}) custom-call(s32[3]{0:T(128)S(1)} %pad_add_fusion.here_ref, s32[32]{0:T(128)S(1)} %all-reduce.exp_ref, bf16[128,4096]{1,0:T(8,128)(2,1)S(1)} %bitcast.31, bf16[128,4096]{1,0:T(8,128)(2,1)S(1)} %bitcast.27), custom_call_target="tpu_custom_call" | custom-call | tf_op jit(solution)/shard_map/updates/pallas_call | solution.py:216
  39.8 8.8 %updates.3 = (f32[8,2,128,128]{3,2,1,0:T(8,128)S(1)}, f32[8,2,128,128]{3,2,1,0:T(8,128)}) custom-call(s32[3]{0:T(128)S(1)} %pad_add_fusion.here_ref, s32[32]{0:T(128)S(1)} %all-reduce.exp_ref, bf16[128,4096]{1,0:T(8,128)(2,1)S(1)} %bitcast.21, bf16[128,4096]{1,0:T(8,128)(2,1)S(1)} %bitcast.24), custom_call_target="tpu_custom_call" | custom-call | tf_op jit(solution)/shard_map/updates/pallas_call | solution.py:216
  49.1 1.0 chip.2
  50.0 0.9 collective-permute-start.1
  51.0 21.7 %collective-permute-done.1.other_ref.after_ref = f32[8,128,128]{2,1,0:T(8,128)S(1)} collective-permute-done((f32[8,128,128]{2,1,0:T(8,128)S(1)}, f32[8,128,128]{2,1,0:T(8,128)S(1)}, u32[]{:S(2)}, u32[]{:S(2)}) %collective-permute-start.1) | collective-permute-done | bytes 524320 | tf_op jit(solution)/shard_map/ppermute | solution.py:254
  73.3 0.8 copy-done.22
  74.1 0.8 copy-done.23
  74.9 5.0 %all-to-all-start = ((f32[8,128,128]{2,1,0:T(8,128)}), f32[8,128,128]{2,1,0:T(8,128)S(1)}, u32[]{:S(2)}, u32[]{:S(2)}) async-start(f32[8,128,128]{2,1,0:T(8,128)} %copy-done.22), calls=%async_computation | async-start | bytes 1048576 | tf_op jit(solution)/shard_map/all_to_all | solution.py:229
  79.9 4.0 %chip.3 = (f32[8,128,128]{2,1,0:T(8,128)S(1)}, f32[8,128,128]{2,1,0:T(8,128)S(1)}) custom-call(s32[3]{0:T(128)S(1)} %pad_add_fusion.here_ref, s32[32]{0:T(128)S(1)} %all-reduce.exp_ref, f32[8,2,128,128]{3,2,1,0:T(8,128)S(1)} %get-tuple-element.28.after_ref.mine_ref, f32[8,2,128,128]{3,2,1,0:T(8,128)} %collective-permute-done.2.other_ref, ...), custom_call_target="tpu_custom_call" | custom-call | tf_op jit(solution)/shard_map/chip/pallas_call | solution.py:216
  83.9 0.8 copy-done.16
  84.7 1.4 collective-permute-start.3
  86.1 23.3 %collective-permute-done.3.other_ref = f32[8,128,128]{2,1,0:T(8,128)S(1)} collective-permute-done((f32[8,128,128]{2,1,0:T(8,128)S(1)}, f32[8,128,128]{2,1,0:T(8,128)S(1)}, u32[]{:S(2)}, u32[]{:S(2)}) %collective-permute-start.3) | collective-permute-done | bytes 524320 | tf_op jit(solution)/shard_map/ppermute | solution.py:254
  109.4 0.8 copy-done.19
  110.3 1.2 copy-done.17
  111.5 1.0 copy-done.20
  112.5 1.2 turn.1
  113.7 30.9 %all_to_all.25.edge_ref.parts_ref = f32[8,2,128,128]{3,2,1,0:T(8,128)S(1)} all-to-all(f32[8,2,128,128]{3,2,1,0:T(8,128)S(1)} %get-tuple-element.34), channel_id=1, replica_groups=mesh['y'=4,'xh'=2,'z'=8,'xl'=2,'core'=2] {'z'}, dimensions={0} | all-to-all | bytes 2097152 | tf_op jit(solution)/shard_map/all_to_all | solution.py:229
  144.7 1.0 copy-done.9
  145.7 0.7 chip_state.2
  146.4 1.3 collective-permute-start.4
  147.7 7.9 %collective-permute-done.4.other_edge_ref = f32[8,128,128]{2,1,0:T(8,128)S(1)} collective-permute-done((f32[8,128,128]{2,1,0:T(8,128)S(1)}, f32[8,128,128]{2,1,0:T(8,128)S(1)}, u32[]{:S(2)}, u32[]{:S(2)}) %collective-permute-start.4) | collective-permute-done | bytes 524320 | tf_op jit(solution)/shard_map/ppermute | solution.py:254
  155.7 1.0 core_state.2
  156.8 2.6 collective-permute-done.5.other_ref
  159.5 1.0 copy-done.30
  160.4 10.0 %key_value.1 = (bf16[128,4096]{1,0:T(8,128)(2,1)}, bf16[128,4096]{1,0:T(8,128)(2,1)}, bf16[8,4,128,256]{3,2,1,0:T(8,128)(2,1)}) custom-call(s32[3]{0:T(128)S(1)} %pad_add_fusion.here_ref, s32[32]{0:T(128)S(1)} %all-reduce.exp_ref, bf16[128,4096]{1,0:T(8,128)(2,1)S(1)} %bitcast.32, bf16[128,4096]{1,0:T(8,128)(2,1)S(1)} %bitcast.22, ...), custom_call_target="tpu_custom_call" | custom-call | tf_op jit(solution)/shard_map/key_value/pallas_call | solution.py:216
  170.4 36.0 %all_to_all.26 = bf16[32,128,256]{2,1,0:T(8,128)(2,1)} all-to-all(bf16[32,128,256]{2,1,0:T(8,128)(2,1)} %bitcast.35), channel_id=1, replica_groups=mesh['y'=4,'xh'=2,'z'=8,'xl'=2,'core'=2] {'y','xh','xl','core'}, dimensions={0} | all-to-all | bytes 4194304 | tf_op jit(solution)/shard_map/all_to_all | solution.py:229
  206.5 1.6 copy-done.7
  208.0 13.6 %weight.1.after_ref = f32[8,768,128]{2,1,0:T(8,128)} custom-call(bf16[4096,256]{1,0:T(8,128)(2,1)S(1)} %bitcast.30, bf16[4096,3072]{1,0:T(8,128)(2,1)} %bitcast.34), custom_call_target="tpu_custom_call" | custom-call | tf_op jit(solution)/shard_map/weight/pallas_call | solution.py:216
  221.7 0.8 copy-done.29
  222.5 26.4 %all_to_all.27.edge_ref = f32[8,1,128,128]{3,2,1,0:T(8,128)S(1)} all-to-all(f32[8,1,128,128]{3,2,1,0:T(8,128)S(1)} %scan.1), channel_id=1, replica_groups=mesh['y'=4,'xh'=2,'z'=8,'xl'=2,'core'=2] {'z'}, dimensions={0} | all-to-all | bytes 1048576 | tf_op jit(solution)/shard_map/all_to_all | solution.py:229
  248.9 0.7 chip_state.3
  249.8 11.4 %collective-permute-done.6.other_edge_ref = f32[8,128,128]{2,1,0:T(8,128)S(1)} collective-permute-done((f32[8,128,128]{2,1,0:T(8,128)S(1)}, f32[8,128,128]{2,1,0:T(8,128)S(1)}, u32[]{:S(2)}, u32[]{:S(2)}) %collective-permute-start.6) | collective-permute-done | bytes 524320 | tf_op jit(solution)/shard_map/ppermute | solution.py:254
  261.2 5.3 %core_state.3 = (f32[8,2,128,128]{3,2,1,0:T(8,128)S(1)}, f32[8,2,128,128]{3,2,1,0:T(8,128)}) custom-call(s32[3]{0:T(128)S(1)} %pad_add_fusion.here_ref, s32[32]{0:T(128)S(1)} %all-reduce.exp_ref, f32[8,128,128]{2,1,0:T(8,128)S(1)} %get-tuple-element.40.mine_edge_ref, f32[8,128,128]{2,1,0:T(8,128)S(1)} %collective-permute-done.6.other_edge_ref, ...), custom_call_target="tpu_custom_call" | custom-call | tf_op jit(solution)/shard_map/core_state/pallas_call | solution.py:216
  266.6 1.0 copy-done.25
  267.6 4.2 %reduce-scatter.2.cloned.1.call-done = f32[1,768,128]{2,1,0:T(8,128)} async-done(((f32[8,768,128]{2,1,0:T(8,128)}), f32[1,768,128]{2,1,0:T(8,128)}) %reduce-scatter.2.cloned.1.call-update) | async-done | bytes 393232 | tf_op jit(solution)/shard_map/reduce_scatter | solution.py:351
  271.8 3.5 %all-to-all-start.4 = ((f32[8,96,128]{2,1,0:T(8,128)}), f32[8,96,128]{2,1,0:T(8,128)S(1)}, u32[]{:S(2)}, u32[]{:S(2)}) async-start(f32[8,96,128]{2,1,0:T(8,128)} %bitcast.39), calls=%async_computation.5 | async-start | bytes 786432 | tf_op jit(solution)/shard_map/all_to_all | solution.py:229
  275.3 1.0 copy-done.27
  276.2 1.2 copy-done.6
  277.5 1.2 copy-done.26
  278.7 1.2 copy-done.28
  279.9 6.1 %query.1 = bf16[128,4096]{1,0:T(8,128)(2,1)} custom-call(s32[3]{0:T(128)S(1)} %pad_add_fusion.here_ref, s32[32]{0:T(128)S(1)} %all-reduce.exp_ref, bf16[128,4096]{1,0:T(8,128)(2,1)S(1)} %bitcast.23, bf16[128,4096]{1,0:T(8,128)(2,1)S(1)} %bitcast.26, bf16[128,4096]{1,0:T(8,128)(2,1)S(1)} %bitcast.29, f32[8,2,128,128]{3,2,1,0:T(8,128)S(1)} %copy-done.26, ...), custom_call_target="tpu_custom_call" | custom-call | tf_op jit(solution)/shard_map/query/pallas_call | solution.py:216
  286.3 0.9 reshape.29
  (64 shorter events, 2.1 us)
Async XLA Ops:
  7.2 32.6 %copy-start.1 = (bf16[1,128,4096]{2,1,0:T(8,128)(2,1)S(1)}, bf16[1,128,4096]{2,1,0:T(8,128)(2,1)}, u32[]{:S(2)}) copy-start(bf16[1,128,4096]{2,1,0:T(8,128)(2,1)} %param.10) | copy-start | bytes 3145732
  7.2 32.6 %copy-start = (bf16[1,128,4096]{2,1,0:T(8,128)(2,1)S(1)}, bf16[1,128,4096]{2,1,0:T(8,128)(2,1)}, u32[]{:S(2)}) copy-start(bf16[1,128,4096]{2,1,0:T(8,128)(2,1)} %param.9) | copy-start | bytes 3145732
  7.2 199.3 %all-gather.3.cloned.1.call-start = ((), (), s32[]{:S(2)}) async-start(), calls=%async_computation.7 | async-start | bytes 25952256 | tf_op jit(solution)/shard_map/all_gather | solution.py:241
  29.1 1.2 copy-start.4
  30.4 1.2 copy-start.14
  39.7 33.0 %copy-start.10 = (f32[8,2,128,128]{3,2,1,0:T(8,128)}, f32[8,2,128,128]{3,2,1,0:T(8,128)S(1)}, u32[]{:S(2)}) copy-start(f32[8,2,128,128]{3,2,1,0:T(8,128)S(1)} %get-tuple-element.26.mine_ref) | copy-start | bytes 3145732
  39.7 9.4 %collective-permute-start = (f32[8,2,128,128]{3,2,1,0:T(8,128)S(1)}, f32[8,2,128,128]{3,2,1,0:T(8,128)S(1)}, u32[]{:S(2)}, u32[]{:S(2)}) collective-permute-start(f32[8,2,128,128]{3,2,1,0:T(8,128)S(1)} %get-tuple-element.27), channel_id=1, source_target_pairs={{0,1},{1,0},{2,3},{3,2},{4,5},{5,4},{6,7},{7,6},{8,9},{9,8},{10,11... | collective-permute-start | bytes 3145736 | tf_op jit(solution)/shard_map/ppermute | solution.py:254
  48.6 31.3 %collective-permute-start.2 = (f32[8,2,128,128]{3,2,1,0:T(8,128)}, f32[8,2,128,128]{3,2,1,0:T(8,128)}, u32[]{:S(2)}, u32[]{:S(2)}) collective-permute-start(f32[8,2,128,128]{3,2,1,0:T(8,128)} %get-tuple-element.31), channel_id=1, source_target_pairs={{0,1},{1,0},{2,3},{3,2},{4,5},{5,4},{6,7},{7,6},{8,9},{9,8},{10,11... | collective-permute-start | bytes 3145736 | tf_op jit(solution)/shard_map/ppermute | solution.py:254
  49.1 23.6 %copy-start.12 = (f32[8,2,128,128]{3,2,1,0:T(8,128)}, f32[8,2,128,128]{3,2,1,0:T(8,128)S(1)}, u32[]{:S(2)}) copy-start(f32[8,2,128,128]{3,2,1,0:T(8,128)S(1)} %collective-permute-done.other_ref) | copy-start | bytes 3145732
  50.0 22.6 %collective-permute-start.1 = (f32[8,128,128]{2,1,0:T(8,128)S(1)}, f32[8,128,128]{2,1,0:T(8,128)S(1)}, u32[]{:S(2)}, u32[]{:S(2)}) collective-permute-start(f32[8,128,128]{2,1,0:T(8,128)S(1)} %get-tuple-element.30), channel_id=1, source_target_pairs={{0,2},{2,0},{1,3},{3,1},{4,6},{6,4},{5,7},{7,5},{8,10},{10,8},{9,1... | collective-permute-start | bytes 1572872 | tf_op jit(solution)/shard_map/ppermute | solution.py:254
  72.7 41.1 %copy-start.8 = (f32[8,128,128]{2,1,0:T(8,128)}, f32[8,128,128]{2,1,0:T(8,128)S(1)}, u32[]{:S(2)}) copy-start(f32[8,128,128]{2,1,0:T(8,128)S(1)} %collective-permute-done.1.other_ref.after_ref) | copy-start | bytes 1572868
  73.3 0.8 copy-start.22
  74.1 0.8 copy-start.23
  74.9 35.3 %all-to-all-start = ((f32[8,128,128]{2,1,0:T(8,128)}), f32[8,128,128]{2,1,0:T(8,128)S(1)}, u32[]{:S(2)}, u32[]{:S(2)}) async-start(f32[8,128,128]{2,1,0:T(8,128)} %copy-done.22), calls=%async_computation | async-start | bytes 1048576 | tf_op jit(solution)/shard_map/all_to_all | solution.py:229
  79.9 191.9 %reduce-scatter.2.cloned.1.call-start = ((), (), s32[]{:S(2)}) async-start(), calls=%async_computation.6 | async-start | bytes 3538944 | tf_op jit(solution)/shard_map/reduce_scatter | solution.py:351
  83.9 0.8 copy-start.16
  84.7 24.7 %collective-permute-start.3 = (f32[8,128,128]{2,1,0:T(8,128)S(1)}, f32[8,128,128]{2,1,0:T(8,128)S(1)}, u32[]{:S(2)}, u32[]{:S(2)}) collective-permute-start(f32[8,128,128]{2,1,0:T(8,128)S(1)} %get-tuple-element.33), channel_id=1, source_target_pairs={{0,2},{2,0},{1,3},{3,1},{4,6},{6,4},{5,7},{7,5},{8,10},{10,8},{9,1... | collective-permute-start | bytes 1572872 | tf_op jit(solution)/shard_map/ppermute | solution.py:254
  109.4 0.8 copy-start.19
  110.2 45.4 %copy-start.11 = (f32[8,2,128,128]{3,2,1,0:T(8,128)S(1)}, f32[8,2,128,128]{3,2,1,0:T(8,128)}, u32[]{:S(2)}) copy-start(f32[8,2,128,128]{3,2,1,0:T(8,128)} %copy-done.10) | copy-start | bytes 3145732
  110.3 45.4 %copy-start.13 = (f32[8,2,128,128]{3,2,1,0:T(8,128)S(1)}, f32[8,2,128,128]{3,2,1,0:T(8,128)}, u32[]{:S(2)}) copy-start(f32[8,2,128,128]{3,2,1,0:T(8,128)} %copy-done.12) | copy-start | bytes 3145732
  110.3 1.2 copy-start.17
  111.5 1.0 copy-start.20
  112.5 32.2 %copy-start.24 = (f32[8,128,128]{2,1,0:T(8,128)S(1)}, f32[8,128,128]{2,1,0:T(8,128)}, u32[]{:S(2)}) copy-start(f32[8,128,128]{2,1,0:T(8,128)} %copy-done.23) | copy-start | bytes 1572868
  144.7 1.0 copy-start.9
  145.7 14.7 %copy-start.2 = (bf16[1,128,4096]{2,1,0:T(8,128)(2,1)S(1)}, bf16[1,128,4096]{2,1,0:T(8,128)(2,1)}, u32[]{:S(2)}) copy-start(bf16[1,128,4096]{2,1,0:T(8,128)(2,1)} %param.10) | copy-start | bytes 3145732
  145.7 14.7 %copy-start.5 = (bf16[1,128,4096]{2,1,0:T(8,128)(2,1)S(1)}, bf16[1,128,4096]{2,1,0:T(8,128)(2,1)}, u32[]{:S(2)}) copy-start(bf16[1,128,4096]{2,1,0:T(8,128)(2,1)} %param.11) | copy-start | bytes 3145732
  145.7 14.7 %copy-start.15 = (bf16[1,128,4096]{2,1,0:T(8,128)(2,1)S(1)}, bf16[1,128,4096]{2,1,0:T(8,128)(2,1)}, u32[]{:S(2)}) copy-start(bf16[1,128,4096]{2,1,0:T(8,128)(2,1)} %param.8) | copy-start | bytes 3145732
  146.4 9.3 %collective-permute-start.4 = (f32[8,128,128]{2,1,0:T(8,128)S(1)}, f32[8,128,128]{2,1,0:T(8,128)S(1)}, u32[]{:S(2)}, u32[]{:S(2)}) collective-permute-start(f32[8,128,128]{2,1,0:T(8,128)S(1)} %get-tuple-element.36), channel_id=1, source_target_pairs={{0,2},{2,0},{1,3},{3,1},{4,6},{6,4},{5,7},{7,5},{8,10},{10,8},{9,1... | collective-permute-start | bytes 1572872 | tf_op jit(solution)/shard_map/ppermute | solution.py:254
  156.7 2.7 collective-permute-start.5
  159.5 1.0 copy-start.30
  206.5 1.6 copy-start.7
  221.6 0.8 copy-start.29
  221.6 27.3 %copy-start.18 = (f32[8,128,128]{2,1,0:T(8,128)S(1)}, f32[8,128,128]{2,1,0:T(8,128)}, u32[]{:S(2)}) copy-start(f32[8,128,128]{2,1,0:T(8,128)} %copy-done.16) | copy-start | bytes 1572868
  221.7 27.2 %copy-start.21 = (f32[8,128,128]{2,1,0:T(8,128)S(1)}, f32[8,128,128]{2,1,0:T(8,128)}, u32[]{:S(2)}) copy-start(f32[8,128,128]{2,1,0:T(8,128)} %copy-done.19) | copy-start | bytes 1572868
  222.5 53.7 %copy-start.3 = (bf16[1,128,4096]{2,1,0:T(8,128)(2,1)S(1)}, bf16[1,128,4096]{2,1,0:T(8,128)(2,1)}, u32[]{:S(2)}) copy-start(bf16[1,128,4096]{2,1,0:T(8,128)(2,1)} %param.10) | copy-start | bytes 3145732
  249.6 11.7 %collective-permute-start.6 = (f32[8,128,128]{2,1,0:T(8,128)S(1)}, f32[8,128,128]{2,1,0:T(8,128)S(1)}, u32[]{:S(2)}, u32[]{:S(2)}) collective-permute-start(f32[8,128,128]{2,1,0:T(8,128)S(1)} %get-tuple-element.41), channel_id=1, source_target_pairs={{0,2},{2,0},{1,3},{3,1},{4,6},{6,4},{5,7},{7,5},{8,10},{10,8},{9,1... | collective-permute-start | bytes 1572872 | tf_op jit(solution)/shard_map/ppermute | solution.py:254
  266.6 1.0 copy-start.25
  267.6 7.7 %collective-permute-start.7 = (f32[8,2,128,128]{3,2,1,0:T(8,128)}, f32[8,2,128,128]{3,2,1,0:T(8,128)S(1)}, u32[]{:S(2)}, u32[]{:S(2)}) collective-permute-start(f32[8,2,128,128]{3,2,1,0:T(8,128)} %get-tuple-element.43), channel_id=1, source_target_pairs={{0,1},{1,0},{2,3},{3,2},{4,5},{5,4},{6,7},{7,6},{8,9},{9,8},{10,11... | collective-permute-start | bytes 3145736 | tf_op jit(solution)/shard_map/ppermute | solution.py:254
  271.8 14.2 %all-to-all-start.4 = ((f32[8,96,128]{2,1,0:T(8,128)}), f32[8,96,128]{2,1,0:T(8,128)S(1)}, u32[]{:S(2)}, u32[]{:S(2)}) async-start(f32[8,96,128]{2,1,0:T(8,128)} %bitcast.39), calls=%async_computation.5 | async-start | bytes 786432 | tf_op jit(solution)/shard_map/all_to_all | solution.py:229
  275.3 1.0 copy-start.27
  276.2 1.2 copy-start.6
  277.5 1.2 copy-start.26
  278.7 1.2 copy-start.28
Sparse Core Ops, SparseCore 0:
  10.6 116.9 all-gather.2
  221.8 49.9 reduce-scatter.1

commit v3 on v2

--- a/solution.py
+++ b/solution.py
@@ -33,28 +33,21 @@
     return lax.dot_general(left, right, (dims, ((), ())), preferred_element_type=f32)
 
 
-def update_kernel(here_ref, exp_ref, left_ref, right_ref, keep_ref, send_ref, *, reverse, length):
+def update_kernel(here_ref, exp_ref, left_ref, right_ref, *refs, reverse, length):
     group = pl.program_id(0)
     span = left_ref.shape[0]
     rows = lax.broadcasted_iota(jnp.int32, (span, WIDTH), 0).astype(f32)
     steps = rows if reverse else (span - 1.0) - rows
-    for slot in range(4):
-        rate = log_rate(exp_ref[4 * group + slot], length)
-        lanes = pl.ds(slot * WIDTH, WIDTH)
-        high, low = halves(left_ref[:, lanes].astype(f32) * jnp.exp(rate * steps))
-        right = right_ref[:, lanes]
-        update = dot(
-            jnp.concatenate((high, low), 0), jnp.concatenate((right, right), 0), ((0,), (0,))
-        )
-        chip = jnp.bitwise_xor(here_ref[1], slot // 2)
-
-        @pl.when(here_ref[2] == slot % 2)
-        def _(update=update, chip=chip):
-            keep_ref[0, chip] = update
-
-        @pl.when(here_ref[2] != slot % 2)
-        def _(update=update, chip=chip):
-            send_ref[0, chip] = update
+    for core, out_ref in enumerate(refs[-2:]):
+        for chip in range(2):
+            slot = 2 * jnp.bitwise_xor(here_ref[1], chip) + jnp.bitwise_xor(here_ref[2], core)
+            rate = log_rate(exp_ref[4 * group + slot], length)
+            lanes = pl.ds(pl.multiple_of(slot * WIDTH, WIDTH), WIDTH)
+            high, low = halves(left_ref[:, lanes].astype(f32) * jnp.exp(rate * steps))
+            right = right_ref[:, lanes]
+            out_ref[0, chip] = dot(
+                jnp.concatenate((high, low), 0), jnp.concatenate((right, right), 0), ((0,), (0,))
+            )
 
 
 def weighed(mine, other, position, reverse, rate, span):
@@ -64,9 +57,9 @@
 
 
 def chip_kernel(
-    here_ref, exp_ref, mine_ref, other_ref, after_ref, keep_ref, send_ref,
-    *, reverse, length, span
-):
+    here_ref, exp_ref, mine_ref, other_ref, *refs, reverse, length, span
+):
+    keep_ref, send_ref = refs[-2:]
     group = pl.program_id(0)
     for chip, out_ref in enumerate((keep_ref, send_ref)):
         head = 4 * group + 2 * jnp.bitwise_xor(here_ref[1], chip) + here_ref[2]
@@ -84,29 +77,35 @@
         )
 
 
-def turn_kernel(
-    here_ref, exp_ref, own_ref, parts_ref, mine_ref, other_ref, out_ref, grad_ref, *, length, span
-):
+def scan_kernel(own_ref, parts_ref, out_ref, grad_ref, *, length, span):
     rate = log_rate(own_ref[0], length)
-    decay = power_of(rate, 2.0 * span)
+    decay = power_of(rate, span)
     state = jnp.zeros(grad_ref.shape, f32)
     for group in reversed(range(parts_ref.shape[0])):
-        out_ref[group, 0] = state
+        out_ref[group] = state
         state = decay * state + parts_ref[group]
     grad_ref[...] = power_of(rate, 1.0) * state
-    for group in range(parts_ref.shape[0]):
+
+
+def line_kernel(
+    here_ref, exp_ref, mine_ref, other_ref, first_ref, after_ref, out_ref, *, length, span
+):
+    count = mine_ref.shape[0]
+    for group in range(count):
         rate = log_rate(exp_ref[4 * group + 2 * here_ref[1] + here_ref[2]], length)
-        out_ref[group, 1] = weighed(
+        out_ref[group] = weighed(
             mine_ref[group], other_ref[group], here_ref[1], False, rate, span
         )
-
-
-def scan_kernel(own_ref, parts_ref, first_ref, after_ref, out_ref, *, length, span):
-    decay = power_of(log_rate(own_ref[0], length), span)
-    state = first_ref[...]
-    for group in range(parts_ref.shape[0]):
-        out_ref[group, 0] = state
-        state = decay * state + parts_ref[group, 0]
+    out_ref[count] = first_ref[...]
+
+
+def edge_kernel(here_ref, exp_ref, parts_ref, first_ref, after_ref, out_ref, *, length, span):
+    rate = log_rate(exp_ref[4 * pl.program_id(0) + 2 * here_ref[1] + here_ref[2]], length)
+    decay = power_of(rate, span)
+    state = first_ref[0, 0]
+    for group in range(parts_ref.shape[0] - 1):
+        state = jnp.where(here_ref[0] > group, decay * state + parts_ref[group, 0], state)
+    out_ref[0] = state
 
 
 def chip_state_kernel(
@@ -115,7 +114,7 @@
     behind = here_ref[1] == (0 if reverse else 1)
     for group in range(edge_ref.shape[0]):
         rate = log_rate(exp_ref[4 * group + 2 * here_ref[1] + here_ref[2]], length)
-        edge = edge_ref[group, 0]
+        edge = edge_ref[group]
         past = power_of(rate, span) * edge
         keep_ref[group] = jnp.where(behind, past + other_ref[group], edge)
         send_ref[group] = jnp.where(behind, edge, past + mine_ref[group])
@@ -261,23 +260,23 @@
             args, scratch, name,
         )
 
-    def updates(left, right, reverse):
+    def updates(left, right, reverse, after=None):
         return run(
             update_kernel, (groups,), [SMEM, SMEM, head_cols, head_cols], [pair_tiles, pair_tiles],
-            [pair_shape, pair_shape], (here, exps, left, right), reverse=reverse, name="updates",
-        )
-
-    def chip(mine, other, reverse, after):
+            [pair_shape, pair_shape], (here, exps, left, right), after,
+            reverse=reverse, name="updates",
+        )
+
+    def chip(mine, other, reverse, after=None):
         return run(
             chip_kernel, (groups,), [SMEM, SMEM, pair_tiles, pair_tiles], [line_tile, line_tile],
             [line_shape, line_shape], (here, exps, mine, other), after,
             reverse=reverse, span=float(span), name="chip",
         )
 
-    def chip_state(edges, item, mine, other, reverse):
-        spec = pl.BlockSpec((groups, 1) + tile, lambda i: (0, item, 0, 0))
+    def chip_state(edges, mine, other, reverse):
         return run(
-            chip_state_kernel, (1,), [SMEM, SMEM, spec, line, line], [line, line],
+            chip_state_kernel, (1,), [SMEM, SMEM, line, line, line], [line, line],
             [line_shape, line_shape], (here, exps, edges, mine, other),
             reverse=reverse, span=2.0 * span, name="chip_state",
         )
@@ -292,25 +291,29 @@
 
     r_mine, sent = updates(query, grad, True)
     r_other = swap(sent, "core")
-    f_mine, sent = updates(key, value, False)
+    r_chip, sent = chip(r_mine, r_other, True)
+    r_next = swap(sent, "xl")
+    f_mine, sent = updates(key, value, False, r_chip)
     f_other = swap(sent, "core")
-    r_chip, sent = chip(r_mine, r_other, True, f_mine)
-    r_next = swap(sent, "xl")
     r_parts = exchange(run(
         quad_kernel, (1,), [SMEM, SMEM, line, line], line, line_shape,
         (here, exps, r_chip, r_next), span=2.0 * span, name="quad",
     ), "z")
     f_chip, sent = chip(f_mine, f_other, False, r_next)
     f_next = swap(sent, "xl")
-    turned, state_grad = run(
-        turn_kernel, (1,), [SMEM, SMEM, SMEM, line, line, line],
-        [pl.BlockSpec((groups, 2) + tile, lambda i: (0, 0, 0, 0)), single],
-        [pair_shape, tile_shape],
-        (here, exps, decay_exp, r_parts, f_chip, f_next), span=2.0 * span, name="turn",
-    )
-    turned = exchange(turned, "z")
-    r_edge, sent = chip_state(turned, 0, r_chip, r_next, True)
+    r_edges, state_grad = run(
+        scan_kernel, (1,), [SMEM, line], [line, single], [line_shape, tile_shape],
+        (decay_exp, r_parts), span=4.0 * span, name="scan",
+    )
+    r_edges = exchange(r_edges, "z")
+    r_edge, sent = chip_state(r_edges, r_chip, r_next, True)
     r_far = swap(sent, "xl")
+    f_parts = lax.all_gather(run(
+        line_kernel, (1,), [SMEM, SMEM, line, line, single],
+        pl.BlockSpec((groups + 1,) + tile, lambda i: (0, 0, 0)),
+        jax.ShapeDtypeStruct((groups + 1,) + tile, f32),
+        (here, exps, f_chip, f_next, state_in[0, 0]), r_edge, span=2.0 * span, name="line",
+    ), "z")
     mine, sent = core_state(r_edge, r_far, r_mine, r_other, True)
     other = swap(sent, "core")
     grad_key, grad_value, send = run(
@@ -333,14 +336,16 @@
         jax.ShapeDtypeStruct((8, block, WIDTH), f32),
         (cols, rows), scratch=[pltpu.VMEM((2 * WIDTH, tokens), bf16)], name="weight",
     )
-    f_edges = exchange(run(
-        scan_kernel, (1,),
-        [SMEM, pl.BlockSpec((groups, 1) + tile, lambda i: (0, 1, 0, 0)), single, FREE],
-        pl.BlockSpec((groups, 1) + tile, lambda i: (0, 0, 0, 0)),
-        jax.ShapeDtypeStruct((groups, 1) + tile, f32),
-        (decay_exp, turned, state_in[0, 0], partial), span=4.0 * span, name="scan",
-    ), "z")
-    f_edge, sent = chip_state(f_edges, 0, f_chip, f_next, False)
+    f_edges = run(
+        edge_kernel, (groups,),
+        [
+            SMEM, SMEM, pl.BlockSpec((groups, 1) + tile, lambda i: (0, i, 0, 0)),
+            pl.BlockSpec((1, 1) + tile, lambda i: (i, groups, 0, 0)),
+        ],
+        line_tile, line_shape, (here, exps, f_parts, f_parts), partial,
+        span=4.0 * span, name="edge",
+    )
+    f_edge, sent = chip_state(f_edges, f_chip, f_next, False)
     f_far = swap(sent, "xl")
     mine, sent = core_state(f_edge, f_far, f_mine, f_other, False)
     other = swap(sent, "core")

time: 297 us -> 275 us (0.926)
  blocking collectives: 112 us -> 53.4 us
  waiting for transfers between devices: 72 us -> 96.2 us
  starting transfers between devices: 13 us -> 23.5 us
    all_to_all x3 -> x1, blocking collectives: 93.3 us -> 34.9 us  [exchange(): return lax.all_to_all(array, axes, split_axis=0, concat_axis=0, tiled=True)]
    all_to_all x2 -> x3, waiting for transfers between devices: 0.01 us -> 19.4 us  [exchange(): return lax.all_to_all(array, axes, split_axis=0, concat_axis=0, tiled=True)]
    reduce_scatter x1, waiting for transfers between devices: 4.24 us -> 17.3 us  [per_device(): summed = lax.psum_scatter(partial, 'z', scatter_dimension=0, tiled=True)]
    all_to_all x2 -> x3, starting transfers between devices: 8.42 us -> 19.5 us  [exchange(): return lax.all_to_all(array, axes, split_axis=0, concat_axis=0, tiled=True)]
    ppermute x8, waiting for transfers between devices: 67.1 us -> 58.8 us  [swap(): return lax.ppermute(array, axis, [(0, 1), (1, 0)])]
    pallas_call x14 -> x15, Pallas kernels: 61.1 us -> 62.8 us  [call(): pl.pallas_call(kernel, grid=grid, in_specs=in_specs, out_specs=out_specs,...]
    unnamed x65 -> x57, local copies, waits for them, and re-layouts: 20 us -> 21 us
  transfers between devices with their start and end apart: 12 -> 14, of which waited for: 6 -> 10; matrix products, arithmetic and copies ran while one was open for 1% -> 1% of each run, Pallas kernels for 16% -> 23%
where the time goes in v3:
time: 275 us; the launch traced here: 273 us
  waiting for transfers between devices  96.2 us (35%)
  Pallas kernels  62.8 us (23%)
  blocking collectives  53.4 us (19%)
  starting transfers between devices  23.5 us (9%)
  local copies, waits for them, and re-layouts  22.1 us (8%)
  between operations  14.6 us (5%)
    pallas_call x15, Pallas kernels, call(): pl.pallas_call(kernel, grid=grid, in_specs=in_specs, out_specs=out_specs,...  62.8 us
    ppermute x8, waiting for transfers between devices, swap(): return lax.ppermute(array, axis, [(0, 1), (1, 0)])  58.8 us
    all_to_all x1, blocking collectives, exchange(): return lax.all_to_all(array, axes, split_axis=0, concat_axis=0, tiled=True)  34.9 us
    unnamed x57, local copies, waits for them, and re-layouts  21 us
    all_to_all x3, starting transfers between devices, exchange(): return lax.all_to_all(array, axes, split_axis=0, concat_axis=0, tiled=True)  19.5 us
    all_to_all x3, waiting for transfers between devices, exchange(): return lax.all_to_all(array, axes, split_axis=0, concat_axis=0, tiled=True)  19.4 us
    unnamed x1, blocking collectives  18.5 us
    reduce_scatter x1, waiting for transfers between devices, per_device(): summed = lax.psum_scatter(partial, 'z', scatter_dimension=0, tiled=True)  17.3 us
  transfers between devices with their start and end apart: 14, of which 10 were waited for; matrix products, arithmetic and copies ran while one was open for 1% of the time, Pallas kernels for 23%

profile of v3, /device:TPU:32, one launch (start us, length us, event | category | flops | bytes accessed | tf_op | source)
XLA Modules:
  0.0 272.6 jit_solution(15396491659277643289)
XLA Ops:
  8.6 1.3 dynamic-slice
  10.6 18.5 %all-reduce.exp_ref = s32[32]{0:T(128)S(1)} all-reduce(s32[32]{0:T(128)S(1)} %dynamic-update-slice), channel_id=1, replica_groups=mesh['y'=4,'xh'=2,'z'=8,'xl'=2,'core'=2] {'z','xl','core'}, use_global_device_ids=true, to_apply=%add | all-reduce | flops 32 | bytes 256
  29.1 1.2 copy-done.2
  30.4 1.2 copy-done.12
  31.6 3.3 %updates.2 = (f32[8,2,128,128]{3,2,1,0:T(8,128)S(1)}, f32[8,2,128,128]{3,2,1,0:T(8,128)S(1)}) custom-call(s32[3]{0:T(128)S(1)} %pad_add_fusion.here_ref, s32[32]{0:T(128)S(1)} %all-reduce.exp_ref, bf16[128,4096]{1,0:T(8,128)(2,1)S(1)} %bitcast.32, bf16[128,4096]{1,0:T(8,128)(2,1)S(1)} %bitcast.28), custom_call_target="tpu_custom_call" | custom-call | tf_op jit(solution)/shard_map/updates/pallas_call | solution.py:215
  35.0 2.6 collective-permute-done.other_ref
  37.7 1.0 chip.2
  38.7 0.9 collective-permute-start.2
  39.6 13.6 %collective-permute-done.2.refs_0_.other_ref = f32[8,128,128]{2,1,0:T(8,128)S(1)} collective-permute-done((f32[8,128,128]{2,1,0:T(8,128)S(1)}, f32[8,128,128]{2,1,0:T(8,128)S(1)}, u32[]{:S(2)}, u32[]{:S(2)}) %collective-permute-start.2) | collective-permute-done | bytes 524320 | tf_op jit(solution)/shard_map/ppermute | solution.py:253
  54.6 7.3 %all-to-all-start = ((f32[8,128,128]{2,1,0:T(8,128)}), f32[8,128,128]{2,1,0:T(8,128)}, u32[]{:S(2)}, u32[]{:S(2)}) async-start(f32[8,128,128]{2,1,0:T(8,128)} %copy-done.15), calls=%async_computation | async-start | bytes 1048576 | tf_op jit(solution)/shard_map/all_to_all | solution.py:228
  61.9 4.9 %updates.3 = (f32[8,2,128,128]{3,2,1,0:T(8,128)S(1)}, f32[8,2,128,128]{3,2,1,0:T(8,128)}) custom-call(s32[3]{0:T(128)S(1)} %pad_add_fusion.here_ref, s32[32]{0:T(128)S(1)} %all-reduce.exp_ref, bf16[128,4096]{1,0:T(8,128)(2,1)S(1)} %bitcast.22, bf16[128,4096]{1,0:T(8,128)(2,1)S(1)} %bitcast.25, f32[8,128,128]{2,1,0:T(8,128)S(1)} %get-tuple-element.28.refs_0_.mine_ref), custom_call_target="tpu_custom_call" | custom-call | tf_op jit(solution)/shard_map/updates/pallas_call | solution.py:215
  66.8 1.0 copy-done.5
  67.8 10.2 %all-to-all-done.parts_ref = f32[8,128,128]{2,1,0:T(8,128)} async-done(((f32[8,128,128]{2,1,0:T(8,128)}), f32[8,128,128]{2,1,0:T(8,128)}, u32[]{:S(2)}, u32[]{:S(2)}) %all-to-all-start) | async-done | bytes 524320 | tf_op jit(solution)/shard_map/all_to_all | solution.py:228
  78.0 1.9 scan.1
  80.7 5.4 %all-to-all-start.1 = ((f32[8,128,128]{2,1,0:T(8,128)}), f32[8,128,128]{2,1,0:T(8,128)}, u32[]{:S(2)}, u32[]{:S(2)}) async-start(f32[8,128,128]{2,1,0:T(8,128)} %copy-done.23), calls=%async_computation.1 | async-start | bytes 1048576 | tf_op jit(solution)/shard_map/all_to_all | solution.py:228
  86.1 1.2 copy-done.6
  87.3 5.2 %chip.3 = (f32[8,128,128]{2,1,0:T(8,128)S(1)}, f32[8,128,128]{2,1,0:T(8,128)}) custom-call(s32[3]{0:T(128)S(1)} %pad_add_fusion.here_ref, s32[32]{0:T(128)S(1)} %all-reduce.exp_ref, f32[8,2,128,128]{3,2,1,0:T(8,128)S(1)} %copy-done.6, f32[8,2,128,128]{3,2,1,0:T(8,128)} %collective-permute-done.1.other_ref, ...), custom_call_target="tpu_custom_call" | custom-call | tf_op jit(solution)/shard_map/chip/pallas_call | solution.py:215
  92.5 0.8 copy-done.16
  93.3 1.0 collective-permute-start.3
  94.4 8.3 %all-to-all-done.1.edge_ref = f32[8,128,128]{2,1,0:T(8,128)} async-done(((f32[8,128,128]{2,1,0:T(8,128)}), f32[8,128,128]{2,1,0:T(8,128)}, u32[]{:S(2)}, u32[]{:S(2)}) %all-to-all-start.1) | async-done | bytes 524320 | tf_op jit(solution)/shard_map/all_to_all | solution.py:228
  102.7 1.2 chip_state.2
  104.7 14.6 %collective-permute-done.3.other_ref = f32[8,128,128]{2,1,0:T(8,128)} collective-permute-done((f32[8,128,128]{2,1,0:T(8,128)}, f32[8,128,128]{2,1,0:T(8,128)}, u32[]{:S(2)}, u32[]{:S(2)}) %collective-permute-start.3) | collective-permute-done | bytes 524320 | tf_op jit(solution)/shard_map/ppermute | solution.py:253
  119.3 1.0 copy-done.17
  120.3 1.1 line.1
  121.5 0.8 copy-done.14
  123.2 1.1 collective-permute-start.4
  124.3 12.0 %collective-permute-done.4.other_edge_ref = f32[8,128,128]{2,1,0:T(8,128)S(1)} collective-permute-done((f32[8,128,128]{2,1,0:T(8,128)}, f32[8,128,128]{2,1,0:T(8,128)S(1)}, u32[]{:S(2)}, u32[]{:S(2)}) %collective-permute-start.4) | collective-permute-done | bytes 524320 | tf_op jit(solution)/shard_map/ppermute | solution.py:253
  136.3 1.3 copy-done.9
  137.6 1.2 copy-done.11
  138.8 1.0 copy-done.20
  139.9 1.0 core_state.2
  141.0 2.6 collective-permute-done.5.other_ref
  143.7 1.0 copy-done.26
  144.7 10.0 %key_value.1 = (bf16[128,4096]{1,0:T(8,128)(2,1)}, bf16[128,4096]{1,0:T(8,128)(2,1)}, bf16[8,4,128,256]{3,2,1,0:T(8,128)(2,1)}) custom-call(s32[3]{0:T(128)S(1)} %pad_add_fusion.here_ref, s32[32]{0:T(128)S(1)} %all-reduce.exp_ref, bf16[128,4096]{1,0:T(8,128)(2,1)S(1)} %bitcast.33, bf16[128,4096]{1,0:T(8,128)(2,1)S(1)} %bitcast.23, ...), custom_call_target="tpu_custom_call" | custom-call | tf_op jit(solution)/shard_map/key_value/pallas_call | solution.py:215
  154.6 34.9 %all_to_all.20 = bf16[32,128,256]{2,1,0:T(8,128)(2,1)} all-to-all(bf16[32,128,256]{2,1,0:T(8,128)(2,1)} %bitcast.38), channel_id=1, replica_groups=mesh['y'=4,'xh'=2,'z'=8,'xl'=2,'core'=2] {'y','xh','xl','core'}, dimensions={0} | all-to-all | bytes 4194304 | tf_op jit(solution)/shard_map/all_to_all | solution.py:228
  189.5 1.6 copy-done.4
  191.1 13.6 %weight.1.after_ref = f32[8,768,128]{2,1,0:T(8,128)} custom-call(bf16[4096,256]{1,0:T(8,128)(2,1)S(1)} %bitcast.31, bf16[4096,3072]{1,0:T(8,128)(2,1)} %bitcast.35), custom_call_target="tpu_custom_call" | custom-call | tf_op jit(solution)/shard_map/weight/pallas_call | solution.py:215
  204.8 5.0 %edge.1.edge_ref = f32[8,128,128]{2,1,0:T(8,128)S(1)} custom-call(s32[3]{0:T(128)S(1)} %pad_add_fusion.here_ref, s32[32]{0:T(128)S(1)} %all-reduce.exp_ref, f32[8,9,128,128]{3,2,1,0:T(8,128)} %bitcast.36, f32[8,9,128,128]{3,2,1,0:T(8,128)} %bitcast.37, f32[8,768,128]{2,1,0:T(8,128)} %weight.1.after_ref), custom_call_target="tpu_custom_call" | custom-call | tf_op jit(solution)/shard_map/edge/pallas_call | solution.py:215
  209.8 1.2 chip_state.3
  211.7 13.4 %collective-permute-done.6.other_edge_ref = f32[8,128,128]{2,1,0:T(8,128)S(1)} collective-permute-done((f32[8,128,128]{2,1,0:T(8,128)S(1)}, f32[8,128,128]{2,1,0:T(8,128)S(1)}, u32[]{:S(2)}, u32[]{:S(2)}) %collective-permute-start.6) | collective-permute-done | bytes 524320 | tf_op jit(solution)/shard_map/ppermute | solution.py:253
  225.0 5.3 %core_state.3 = (f32[8,2,128,128]{3,2,1,0:T(8,128)S(1)}, f32[8,2,128,128]{3,2,1,0:T(8,128)}) custom-call(s32[3]{0:T(128)S(1)} %pad_add_fusion.here_ref, s32[32]{0:T(128)S(1)} %all-reduce.exp_ref, f32[8,128,128]{2,1,0:T(8,128)S(1)} %get-tuple-element.40.mine_edge_ref, f32[8,128,128]{2,1,0:T(8,128)S(1)} %collective-permute-done.6.other_edge_ref, ...), custom_call_target="tpu_custom_call" | custom-call | tf_op jit(solution)/shard_map/core_state/pallas_call | solution.py:215
  230.4 1.0 copy-done.21
  231.4 17.3 %reduce-scatter.2.cloned.1.call-done = f32[1,768,128]{2,1,0:T(8,128)} async-done(((f32[8,768,128]{2,1,0:T(8,128)}), f32[1,768,128]{2,1,0:T(8,128)}) %reduce-scatter.2.cloned.1.call-update) | async-done | bytes 393232 | tf_op jit(solution)/shard_map/reduce_scatter | solution.py:356
  248.6 6.8 %all-to-all-start.3 = ((f32[8,96,128]{2,1,0:T(8,128)}), f32[8,96,128]{2,1,0:T(8,128)S(1)}, u32[]{:S(2)}, u32[]{:S(2)}) async-start(f32[8,96,128]{2,1,0:T(8,128)} %bitcast.42), calls=%async_computation.4 | async-start | bytes 786432 | tf_op jit(solution)/shard_map/all_to_all | solution.py:228
  255.4 1.2 copy-done.22
  256.7 7.4 %query.1 = bf16[128,4096]{1,0:T(8,128)(2,1)} custom-call(s32[3]{0:T(128)S(1)} %pad_add_fusion.here_ref, s32[32]{0:T(128)S(1)} %all-reduce.exp_ref, bf16[128,4096]{1,0:T(8,128)(2,1)S(1)} %bitcast.24, bf16[128,4096]{1,0:T(8,128)(2,1)S(1)} %bitcast.27, bf16[128,4096]{1,0:T(8,128)(2,1)S(1)} %bitcast.30, f32[8,2,128,128]{3,2,1,0:T(8,128)S(1)} %copy-done.22, ...), custom_call_target="tpu_custom_call" | custom-call | tf_op jit(solution)/shard_map/query/pallas_call | solution.py:215
  264.1 0.9 all-to-all-done.3
  265.2 0.9 reshape.29
  (60 shorter events, 6.6 us)
Async XLA Ops:
  7.2 182.4 %all-gather.7.cloned.1.call-start = ((), (), s32[]{:S(2)}) async-start(), calls=%async_computation.7 | async-start | bytes 25952256 | tf_op jit(solution)/shard_map/all_gather | solution.py:240
  29.1 1.2 copy-start.2
  30.3 1.2 copy-start.12
  31.6 30.3 %copy-start = (bf16[1,128,4096]{2,1,0:T(8,128)(2,1)S(1)}, bf16[1,128,4096]{2,1,0:T(8,128)(2,1)}, u32[]{:S(2)}) copy-start(bf16[1,128,4096]{2,1,0:T(8,128)(2,1)} %param.9) | copy-start | bytes 3145732
  31.6 30.3 %copy-start.1 = (bf16[1,128,4096]{2,1,0:T(8,128)(2,1)S(1)}, bf16[1,128,4096]{2,1,0:T(8,128)(2,1)}, u32[]{:S(2)}) copy-start(bf16[1,128,4096]{2,1,0:T(8,128)(2,1)} %param.10) | copy-start | bytes 3145732
  34.9 18.2 %copy-start.8 = (f32[8,2,128,128]{3,2,1,0:T(8,128)}, f32[8,2,128,128]{3,2,1,0:T(8,128)S(1)}, u32[]{:S(2)}) copy-start(f32[8,2,128,128]{3,2,1,0:T(8,128)S(1)} %get-tuple-element.26.mine_ref) | copy-start | bytes 3145732
  34.9 2.7 %collective-permute-start = (f32[8,2,128,128]{3,2,1,0:T(8,128)S(1)}, f32[8,2,128,128]{3,2,1,0:T(8,128)S(1)}, u32[]{:S(2)}, u32[]{:S(2)}) collective-permute-start(f32[8,2,128,128]{3,2,1,0:T(8,128)S(1)} %get-tuple-element.27), channel_id=1, source_target_pairs={{0,1},{1,0},{2,3},{3,2},{4,5},{5,4},{6,7},{7,6},{8,9},{9,8},{10,11... | collective-permute-start | bytes 3145736 | tf_op jit(solution)/shard_map/ppermute | solution.py:253
  37.7 15.5 %copy-start.10 = (f32[8,2,128,128]{3,2,1,0:T(8,128)}, f32[8,2,128,128]{3,2,1,0:T(8,128)S(1)}, u32[]{:S(2)}) copy-start(f32[8,2,128,128]{3,2,1,0:T(8,128)S(1)} %collective-permute-done.other_ref) | copy-start | bytes 3145732
  38.7 14.5 %collective-permute-start.2 = (f32[8,128,128]{2,1,0:T(8,128)S(1)}, f32[8,128,128]{2,1,0:T(8,128)S(1)}, u32[]{:S(2)}, u32[]{:S(2)}) collective-permute-start(f32[8,128,128]{2,1,0:T(8,128)S(1)} %get-tuple-element.31), channel_id=1, source_target_pairs={{0,2},{2,0},{1,3},{3,1},{4,6},{6,4},{5,7},{7,5},{8,10},{10,8},{9,1... | collective-permute-start | bytes 1572872 | tf_op jit(solution)/shard_map/ppermute | solution.py:253
  53.8 0.8 copy-start.15
  54.6 23.4 %all-to-all-start = ((f32[8,128,128]{2,1,0:T(8,128)}), f32[8,128,128]{2,1,0:T(8,128)}, u32[]{:S(2)}, u32[]{:S(2)}) async-start(f32[8,128,128]{2,1,0:T(8,128)} %copy-done.15), calls=%async_computation | async-start | bytes 1048576 | tf_op jit(solution)/shard_map/all_to_all | solution.py:228
  66.8 1.0 copy-start.5
  67.8 51.5 %copy-start.24 = (f32[1,1,128,128]{3,2,1,0:T(8,128)S(1)}, f32[1,1,128,128]{3,2,1,0:T(8,128)}, u32[]{:S(2)}) copy-start(f32[1,1,128,128]{3,2,1,0:T(8,128)} %param.13) | copy-start | bytes 196612
  67.8 18.3 %collective-permute-start.1 = (f32[8,2,128,128]{3,2,1,0:T(8,128)}, f32[8,2,128,128]{3,2,1,0:T(8,128)}, u32[]{:S(2)}, u32[]{:S(2)}) collective-permute-start(f32[8,2,128,128]{3,2,1,0:T(8,128)} %get-tuple-element.30), channel_id=1, source_target_pairs={{0,1},{1,0},{2,3},{3,2},{4,5},{5,4},{6,7},{7,6},{8,9},{9,8},{10,11... | collective-permute-start | bytes 3145736 | tf_op jit(solution)/shard_map/ppermute | solution.py:253
  79.9 0.8 copy-start.23
  80.7 22.0 %all-to-all-start.1 = ((f32[8,128,128]{2,1,0:T(8,128)}), f32[8,128,128]{2,1,0:T(8,128)}, u32[]{:S(2)}, u32[]{:S(2)}) async-start(f32[8,128,128]{2,1,0:T(8,128)} %copy-done.23), calls=%async_computation.1 | async-start | bytes 1048576 | tf_op jit(solution)/shard_map/all_to_all | solution.py:228
  86.1 118.7 %all-gather.5.cloned.1.call-start = ((), (), s32[]{:S(2)}) async-start(), calls=%async_computation.6 | async-start | bytes 5308416 | tf_op jit(solution)/shard_map/all_gather | solution.py:311
  86.1 1.2 copy-start.6
  92.5 0.8 copy-start.16
  93.3 25.9 %collective-permute-start.3 = (f32[8,128,128]{2,1,0:T(8,128)}, f32[8,128,128]{2,1,0:T(8,128)}, u32[]{:S(2)}, u32[]{:S(2)}) collective-permute-start(f32[8,128,128]{2,1,0:T(8,128)} %get-tuple-element.33), channel_id=1, source_target_pairs={{0,2},{2,0},{1,3},{3,1},{4,6},{6,4},{5,7},{7,5},{8,10},{10,8},{9,1... | collective-permute-start | bytes 1572872 | tf_op jit(solution)/shard_map/ppermute | solution.py:253
  103.9 0.8 copy-start.25
  104.7 40.0 %copy-start.3 = (bf16[1,128,4096]{2,1,0:T(8,128)(2,1)S(1)}, bf16[1,128,4096]{2,1,0:T(8,128)(2,1)}, u32[]{:S(2)}) copy-start(bf16[1,128,4096]{2,1,0:T(8,128)(2,1)} %param.11) | copy-start | bytes 3145732
  119.3 1.0 copy-start.17
  121.4 0.9 copy-start.14
  122.3 0.8 copy-start.19
  123.1 125.5 %reduce-scatter.2.cloned.1.call-start = ((), (), s32[]{:S(2)}) async-start(), calls=%async_computation.5 | async-start | bytes 3538944 | tf_op jit(solution)/shard_map/reduce_scatter | solution.py:356
  123.2 13.1 %collective-permute-start.4 = (f32[8,128,128]{2,1,0:T(8,128)}, f32[8,128,128]{2,1,0:T(8,128)S(1)}, u32[]{:S(2)}, u32[]{:S(2)}) collective-permute-start(f32[8,128,128]{2,1,0:T(8,128)} %copy-done.25), channel_id=1, source_target_pairs={{0,2},{2,0},{1,3},{3,1},{4,6},{6,4},{5,7},{7,5},{8,10},{10,8},{9,1... | collective-permute-start | bytes 1572872 | tf_op jit(solution)/shard_map/ppermute | solution.py:253
  136.3 1.3 copy-start.9
  137.6 1.2 copy-start.11
  138.8 1.0 copy-start.20
  139.9 4.8 %copy-start.13 = (bf16[1,128,4096]{2,1,0:T(8,128)(2,1)S(1)}, bf16[1,128,4096]{2,1,0:T(8,128)(2,1)}, u32[]{:S(2)}) copy-start(bf16[1,128,4096]{2,1,0:T(8,128)(2,1)} %param.8) | copy-start | bytes 3145732
  140.9 2.7 %collective-permute-start.5 = (f32[8,2,128,128]{3,2,1,0:T(8,128)S(1)}, f32[8,2,128,128]{3,2,1,0:T(8,128)S(1)}, u32[]{:S(2)}, u32[]{:S(2)}) collective-permute-start(f32[8,2,128,128]{3,2,1,0:T(8,128)S(1)} %get-tuple-element.38), channel_id=1, source_target_pairs={{0,1},{1,0},{2,3},{3,2},{4,5},{5,4},{6,7},{7,6},{8,9},{9,8},{10,11... | collective-permute-start | bytes 3145736 | tf_op jit(solution)/shard_map/ppermute | solution.py:253
  143.7 1.0 copy-start.26
  189.5 1.6 copy-start.4
  204.8 5.0 %copy-start.18 = (f32[8,128,128]{2,1,0:T(8,128)S(1)}, f32[8,128,128]{2,1,0:T(8,128)}, u32[]{:S(2)}) copy-start(f32[8,128,128]{2,1,0:T(8,128)} %copy-done.16) | copy-start | bytes 1572868
  204.8 20.2 %copy-start.7 = (f32[8,2,128,128]{3,2,1,0:T(8,128)S(1)}, f32[8,2,128,128]{3,2,1,0:T(8,128)}, u32[]{:S(2)}) copy-start(f32[8,2,128,128]{3,2,1,0:T(8,128)} %copy-done.5) | copy-start | bytes 3145732
  211.0 14.0 %collective-permute-start.6 = (f32[8,128,128]{2,1,0:T(8,128)S(1)}, f32[8,128,128]{2,1,0:T(8,128)S(1)}, u32[]{:S(2)}, u32[]{:S(2)}) collective-permute-start(f32[8,128,128]{2,1,0:T(8,128)S(1)} %get-tuple-element.41), channel_id=1, source_target_pairs={{0,2},{2,0},{1,3},{3,1},{4,6},{6,4},{5,7},{7,5},{8,10},{10,8},{9,1... | collective-permute-start | bytes 1572872 | tf_op jit(solution)/shard_map/ppermute | solution.py:253
  230.4 1.0 copy-start.21
  231.4 24.1 %collective-permute-start.7 = (f32[8,2,128,128]{3,2,1,0:T(8,128)}, f32[8,2,128,128]{3,2,1,0:T(8,128)}, u32[]{:S(2)}, u32[]{:S(2)}) collective-permute-start(f32[8,2,128,128]{3,2,1,0:T(8,128)} %get-tuple-element.43), channel_id=1, source_target_pairs={{0,1},{1,0},{2,3},{3,2},{4,5},{5,4},{6,7},{7,6},{8,9},{9,8},{10,11... | collective-permute-start | bytes 3145736 | tf_op jit(solution)/shard_map/ppermute | solution.py:253
  248.6 16.3 %all-to-all-start.3 = ((f32[8,96,128]{2,1,0:T(8,128)}), f32[8,96,128]{2,1,0:T(8,128)S(1)}, u32[]{:S(2)}, u32[]{:S(2)}) async-start(f32[8,96,128]{2,1,0:T(8,128)} %bitcast.42), calls=%async_computation.4 | async-start | bytes 786432 | tf_op jit(solution)/shard_map/all_to_all | solution.py:228
  255.4 1.2 copy-start.22
Sparse Core Ops, SparseCore 0:
  10.5 112.1 all-gather.6
  124.5 58.9 all-gather.4
  204.9 43.6 reduce-scatter.1

commit v4 on v3

--- a/solution.py
+++ b/solution.py
@@ -13,7 +13,9 @@
 bf16 = jnp.bfloat16
 PLANE = ("y", "xh", "xl", "core")
 QUAD = ("xl", "core")
-CHAIN = ("z", "xl", "core")
+LINE = ("zh", "zl")
+CHAIN = ("zh", "zl", "xl", "core")
+FINAL = ("y", "xh", "zl")
 
 
 def log_rate(exponent, length):
@@ -69,7 +71,7 @@
         )
 
 
-def quad_kernel(here_ref, exp_ref, mine_ref, other_ref, out_ref, *, length, span):
+def quad_kernel(here_ref, exp_ref, mine_ref, other_ref, after_ref, out_ref, *, length, span):
     for group in range(out_ref.shape[0]):
         rate = log_rate(exp_ref[4 * group + 2 * here_ref[1] + here_ref[2]], length)
         out_ref[group] = weighed(
@@ -77,7 +79,7 @@
         )
 
 
-def scan_kernel(own_ref, parts_ref, out_ref, grad_ref, *, length, span):
+def scan_kernel(own_ref, parts_ref, after_ref, out_ref, grad_ref, *, length, span):
     rate = log_rate(own_ref[0], length)
     decay = power_of(rate, span)
     state = jnp.zeros(grad_ref.shape, f32)
@@ -109,8 +111,9 @@
 
 
 def chip_state_kernel(
-    here_ref, exp_ref, edge_ref, mine_ref, other_ref, keep_ref, send_ref, *, reverse, length, span
-):
+    here_ref, exp_ref, edge_ref, mine_ref, other_ref, *refs, reverse, length, span
+):
+    keep_ref, send_ref = refs[-2:]
     behind = here_ref[1] == (0 if reverse else 1)
     for group in range(edge_ref.shape[0]):
         rate = log_rate(exp_ref[4 * group + 2 * here_ref[1] + here_ref[2]], length)
@@ -121,9 +124,10 @@
 
 
 def core_state_kernel(
-    here_ref, exp_ref, mine_edge_ref, other_edge_ref, mine_ref, other_ref, keep_ref, send_ref,
-    *, reverse, length, span
-):
+    here_ref, exp_ref, mine_edge_ref, other_edge_ref, mine_ref, other_ref, *refs,
+    reverse, length, span
+):
+    keep_ref, send_ref = refs[-2:]
     group = pl.program_id(0)
     behind = here_ref[2] == (0 if reverse else 1)
     for chip, edge_ref in enumerate((mine_edge_ref, other_edge_ref)):
@@ -141,10 +145,11 @@
 
 
 def key_value_kernel(
-    here_ref, exp_ref, query_ref, key_ref, value_ref, grad_ref, mine_ref, other_ref,
-    gk_ref, gv_ref, send_ref, *, length
-):
-    group = pl.program_id(0)
+    here_ref, exp_ref, query_ref, key_ref, value_ref, grad_ref, mine_ref, other_ref, *refs,
+    length, first
+):
+    gk_ref, gv_ref, send_ref = refs[-3:]
+    group = first + pl.program_id(0)
     span = query_ref.shape[0]
     source = lax.broadcasted_iota(jnp.int32, (span, span), 0)
     target = lax.broadcasted_iota(jnp.int32, (span, span), 1)
@@ -197,14 +202,19 @@
         gq_ref[:, lanes] = gq.astype(bf16)
 
 
-def weight_kernel(cols_ref, rows_ref, out_ref, turned):
+def weight_kernel(cols_ref, rows_ref, *refs):
+    out_ref, turned = refs[-2:]
+
     @pl.when(pl.program_id(0) == 0)
     def _():
         turned[...] = cols_ref[...].T
 
     product = dot(turned[...], rows_ref[...], ((1,), (0,))).T
-    out_ref[0] = product[:, :WIDTH]
-    out_ref[1] = product[:, WIDTH:]
+    count = product.shape[0] // 16
+    for item in range(16):
+        out_ref[item % 2, pl.ds(item // 2 * count, count)] = product[
+            item * count : (item + 1) * count
+        ]
 
 
 SMEM = pl.BlockSpec(memory_space=pltpu.SMEM)
@@ -236,7 +246,7 @@
     tile = (WIDTH, WIDTH)
     query, key, value, grad = queries[0], keys[0], values[0], grad_out[0]
     exps = lax.all_gather(decay_exp, CHAIN, axis=0, tiled=True)
-    here = jnp.stack([lax.axis_index(axis) for axis in CHAIN]).astype(jnp.int32)
+    here = jnp.stack([lax.axis_index(axis) for axis in (LINE, "xl", "core")]).astype(jnp.int32)
     rows = lax.all_gather(inputs_x[0], PLANE, axis=0, tiled=True)
 
     head_cols = pl.BlockSpec((span, 4 * WIDTH), lambda i: (0, i))
@@ -274,18 +284,18 @@
             reverse=reverse, span=float(span), name="chip",
         )
 
-    def chip_state(edges, mine, other, reverse):
+    def chip_state(edges, mine, other, reverse, after=None):
         return run(
             chip_state_kernel, (1,), [SMEM, SMEM, line, line, line], [line, line],
-            [line_shape, line_shape], (here, exps, edges, mine, other),
+            [line_shape, line_shape], (here, exps, edges, mine, other), after,
             reverse=reverse, span=2.0 * span, name="chip_state",
         )
 
-    def core_state(mine_edge, other_edge, mine, other, reverse):
+    def core_state(mine_edge, other_edge, mine, other, reverse, after=None):
         return run(
             core_state_kernel, (groups,),
             [SMEM, SMEM, line_tile, line_tile, pair_tiles, pair_tiles], [pair_tiles, pair_tiles],
-            [pair_shape, pair_shape], (here, exps, mine_edge, other_edge, mine, other),
+            [pair_shape, pair_shape], (here, exps, mine_edge, other_edge, mine, other), after,
             reverse=reverse, span=float(span), name="core_state",
         )
 
@@ -297,45 +307,67 @@
     f_other = swap(sent, "core")
     r_parts = exchange(run(
         quad_kernel, (1,), [SMEM, SMEM, line, line], line, line_shape,
-        (here, exps, r_chip, r_next), span=2.0 * span, name="quad",
-    ), "z")
+        (here, exps, r_chip, r_next), f_mine, span=2.0 * span, name="quad",
+    ), LINE)
     f_chip, sent = chip(f_mine, f_other, False, r_next)
     f_next = swap(sent, "xl")
     r_edges, state_grad = run(
         scan_kernel, (1,), [SMEM, line], [line, single], [line_shape, tile_shape],
-        (decay_exp, r_parts), span=4.0 * span, name="scan",
+        (decay_exp, r_parts), f_chip, span=4.0 * span, name="scan",
     )
-    r_edges = exchange(r_edges, "z")
-    r_edge, sent = chip_state(r_edges, r_chip, r_next, True)
+    r_edges = exchange(r_edges, LINE)
+    r_edge, sent = chip_state(r_edges, r_chip, r_next, True, f_next)
     r_far = swap(sent, "xl")
     f_parts = lax.all_gather(run(
         line_kernel, (1,), [SMEM, SMEM, line, line, single],
         pl.BlockSpec((groups + 1,) + tile, lambda i: (0, 0, 0)),
         jax.ShapeDtypeStruct((groups + 1,) + tile, f32),
-        (here, exps, f_chip, f_next, state_in[0, 0]), r_edge, span=2.0 * span, name="line",
-    ), "z")
+        (here, exps, f_chip, f_next, state_in[0, 0]), r_far, span=2.0 * span, name="line",
+    ), LINE)
     mine, sent = core_state(r_edge, r_far, r_mine, r_other, True)
     other = swap(sent, "core")
-    grad_key, grad_value, send = run(
-        key_value_kernel, (groups,), [SMEM, SMEM] + 4 * [head_cols] + 2 * [pair_tiles],
-        [head_cols, head_cols, pl.BlockSpec((8, 1, span, WIDTH), lambda i: (0, i % 4, 0, i // 4))],
-        [token_shape, token_shape, jax.ShapeDtypeStruct((8, 4, span, 2 * WIDTH), bf16)],
-        (here, exps, query, key, value, grad, mine, other), name="key_value",
-    )
-    cols = exchange(send.reshape(32, span, 2 * WIDTH), PLANE).reshape(32 * span, 2 * WIDTH)
+    rest = here, exps, query, key, value, grad, mine, other
+    grads, halves_cols = (), []
+    for first in (0, groups // 2):
+        columns = pl.BlockSpec((span, 4 * WIDTH), lambda i, first=first: (0, first + i))
+        tiles = pl.BlockSpec((1, 2) + tile, lambda i, first=first: (first + i, 0, 0, 0))
+        *grads, send = pl.pallas_call(
+            functools.partial(key_value_kernel, length=length, first=first),
+            grid=(groups // 2,),
+            in_specs=[SMEM, SMEM] + 4 * [columns] + 2 * [tiles] + len(grads) * [FREE],
+            out_specs=[columns, columns, pl.BlockSpec((8, 1, span, WIDTH), lambda i: (0, i, 0, 0))],
+            out_shape=[
+                token_shape, token_shape, jax.ShapeDtypeStruct((8, 4, span, WIDTH), bf16)
+            ],
+            input_output_aliases={8 + item: item for item in range(len(grads))},
+            name="key_value",
+            compiler_params=pltpu.CompilerParams(vmem_limit_bytes=48 * 1024 * 1024),
+        )(*rest, *grads)
+        if halves_cols:
+            send, halves_cols[0] = lax.optimization_barrier((send, halves_cols[0]))
+        halves_cols.append(
+            exchange(send.reshape(32, span, WIDTH), PLANE).reshape(32 * span, WIDTH)
+        )
+    grad_key, grad_value = grads
 
     tokens, width = rows.shape
     block = width // 4
-    partial = call(
-        weight_kernel, (4,),
-        [
-            pl.BlockSpec((tokens, 2 * WIDTH), lambda i: (0, 0)),
-            pl.BlockSpec((tokens, block), lambda i: (0, i)),
-        ],
-        pl.BlockSpec((2, block, WIDTH), lambda i: (i, 0, 0)),
-        jax.ShapeDtypeStruct((8, block, WIDTH), f32),
-        (cols, rows), scratch=[pltpu.VMEM((2 * WIDTH, tokens), bf16)], name="weight",
-    )
+    def product(cols, after=()):
+        return call(
+            weight_kernel, (4,),
+            [
+                pl.BlockSpec((tokens, WIDTH), lambda i: (0, 0)),
+                pl.BlockSpec((tokens, block), lambda i: (0, i)),
+            ] + len(after) * [FREE],
+            pl.BlockSpec((2, block // 2, WIDTH), lambda i: (i, 0, 0)),
+            jax.ShapeDtypeStruct((8, block // 2, WIDTH), f32),
+            (cols, rows, *after), scratch=[pltpu.VMEM((WIDTH, tokens), bf16)], name="weight",
+        )
+
+    def scattered(partial):
+        return lax.psum_scatter(partial, LINE, scatter_dimension=0, tiled=True)
+
+    partial = product(halves_cols[0])
     f_edges = run(
         edge_kernel, (groups,),
         [
@@ -346,15 +378,17 @@
         span=4.0 * span, name="edge",
     )
     f_edge, sent = chip_state(f_edges, f_chip, f_next, False)
+    summed = [scattered(partial), scattered(product(halves_cols[1], (partial, f_edge)))]
     f_far = swap(sent, "xl")
-    mine, sent = core_state(f_edge, f_far, f_mine, f_other, False)
+    mine, sent = core_state(f_edge, f_far, f_mine, f_other, False, summed[0])
     other = swap(sent, "core")
     grad_query = run(
         query_kernel, (groups,), [SMEM, SMEM] + 3 * [head_cols] + 2 * [pair_tiles], head_cols,
         token_shape, (here, exps, key, value, grad, mine, other), name="query",
     )
-    summed = lax.psum_scatter(partial, "z", scatter_dimension=0, tiled=True)
-    pieces = exchange(summed.reshape(8, block // 8, WIDTH), ("y", "xh"))
+    summed[1], grad_query = lax.optimization_barrier((summed[1], grad_query))
+    pieces = jnp.concatenate([part.reshape(8, 1, block // 16, WIDTH) for part in summed], 1)
+    pieces = exchange(pieces.reshape(16, block // 16, WIDTH), FINAL)
     pieces = pieces.reshape(2, 4, block // 8, WIDTH).transpose(0, 2, 1, 3)
     weight_grads = pieces.reshape(2, 1, block // 8, 4 * WIDTH)
     return (
@@ -363,7 +397,7 @@
 
 
 def solution(mesh):
-    fine = Mesh(mesh.devices.reshape(4, 2, 8, 2, 2), ("y", "xh", "z", "xl", "core"))
+    fine = Mesh(mesh.devices.reshape(4, 2, 4, 2, 2, 2), ("y", "xh", "zh", "zl", "xl", "core"))
     dp, seq = ("y", "xh"), CHAIN
     tokens = P(dp, seq, None)
     in_specs = (tokens, tokens, tokens, tokens, tokens, P(seq), P(dp, seq, None, None))

time: 275 us -> 307 us (1.12)
  waiting for transfers between devices: 96.2 us -> 118 us
  blocking collectives: 53.4 us -> 35.1 us
  local copies, waits for them, and re-layouts: 22.1 us -> 39.8 us
  Pallas kernels: 62.8 us -> 67.9 us
  starting transfers between devices: 23.5 us -> 28.3 us
    all_to_all x1, blocking collectives: 34.9 us -> 16.7 us  [exchange(): return lax.all_to_all(array, axes, split_axis=0, concat_axis=0, tiled=True)]
    unnamed x57 -> x99, local copies, waits for them, and re-layouts: 21 us -> 38.6 us
    pallas_call x0 -> x2, Pallas kernels: none -> 11.5 us  [per_device(): pl.pallas_call(functools.partial(key_value_kernel, length=length, first=f...]
    all_to_all x3 -> x4, waiting for transfers between devices: 19.4 us -> 28.5 us  [exchange(): return lax.all_to_all(array, axes, split_axis=0, concat_axis=0, tiled=True)]
    ppermute x8, waiting for transfers between devices: 58.8 us -> 66.6 us  [swap(): return lax.ppermute(array, axis, [(0, 1), (1, 0)])]
    pallas_call x15, Pallas kernels: 62.8 us -> 56.3 us  [call(): pl.pallas_call(kernel, grid=grid, in_specs=in_specs, out_specs=out_specs,...]
    reduce_scatter x1 -> x2, waiting for transfers between devices: 17.3 us -> 22.1 us  [scattered(): return lax.psum_scatter(partial, LINE, scatter_dimension=0, tiled=True)]
    all_to_all x3 -> x4, starting transfers between devices: 19.5 us -> 24.2 us  [exchange(): return lax.all_to_all(array, axes, split_axis=0, concat_axis=0, tiled=True)]
  transfers between devices with their start and end apart: 14 -> 16, of which waited for: 10 -> 12; matrix products, arithmetic and copies ran while one was open for 1% -> 1% of each run, Pallas kernels for 23% -> 22%
where the time goes in v4:
time: 307 us; the launch traced here: 305 us
  waiting for transfers between devices  118 us (38%)
  Pallas kernels  67.9 us (22%)
  local copies, waits for them, and re-layouts  39.8 us (13%)
  blocking collectives  35.1 us (11%)
  starting transfers between devices  28.3 us (9%)
  between operations  14.7 us (5%)
    ppermute x8, waiting for transfers between devices, swap(): return lax.ppermute(array, axis, [(0, 1), (1, 0)])  66.6 us
    pallas_call x15, Pallas kernels, call(): pl.pallas_call(kernel, grid=grid, in_specs=in_specs, out_specs=out_specs,...  56.3 us
    unnamed x99, local copies, waits for them, and re-layouts  38.6 us
    all_to_all x4, waiting for transfers between devices, exchange(): return lax.all_to_all(array, axes, split_axis=0, concat_axis=0, tiled=True)  28.5 us
    all_to_all x4, starting transfers between devices, exchange(): return lax.all_to_all(array, axes, split_axis=0, concat_axis=0, tiled=True)  24.2 us
    reduce_scatter x2, waiting for transfers between devices, scattered(): return lax.psum_scatter(partial, LINE, scatter_dimension=0, tiled=True)  22.1 us
    unnamed x1, blocking collectives  18.5 us
    all_to_all x1, blocking collectives, exchange(): return lax.all_to_all(array, axes, split_axis=0, concat_axis=0, tiled=True)  16.7 us
  transfers between devices with their start and end apart: 16, of which 12 were waited for; matrix products, arithmetic and copies ran while one was open for 1% of the time, Pallas kernels for 22%

profile of v4, /device:TPU:32, one launch (start us, length us, event | category | flops | bytes accessed | tf_op | source)
XLA Modules:
  0.0 305.1 jit_solution(9102120718013572259)
XLA Ops:
  8.6 1.3 dynamic-slice
  10.6 18.5 %all-reduce.exp_ref = s32[32]{0:T(128)S(1)} all-reduce(s32[32]{0:T(128)S(1)} %dynamic-update-slice), channel_id=1, replica_groups=mesh['y'=4,'xh'=2,'zh'=4,'zl'=2,'xl'=2,'core'=2] {'zh','zl','xl','core'}, use_global_device_ids=true, to_apply=%add | all-reduce | flops 32 | bytes 256
  29.1 1.2 copy-done.2
  30.4 1.2 copy-done.6
  31.6 3.3 %updates.2 = (f32[8,2,128,128]{3,2,1,0:T(8,128)S(1)}, f32[8,2,128,128]{3,2,1,0:T(8,128)S(1)}) custom-call(s32[3]{0:T(128)S(1)} %pad_add_fusion.here_ref, s32[32]{0:T(128)S(1)} %all-reduce.exp_ref, bf16[128,4096]{1,0:T(8,128)(2,1)S(1)} %bitcast.42, bf16[128,4096]{1,0:T(8,128)(2,1)S(1)} %bitcast.38), custom_call_target="tpu_custom_call" | custom-call | tf_op jit(solution)/shard_map/updates/pallas_call | solution.py:225
  35.1 2.6 collective-permute-done.other_ref
  39.6 4.9 %updates.3 = (f32[8,2,128,128]{3,2,1,0:T(8,128)S(1)}, f32[8,2,128,128]{3,2,1,0:T(8,128)}) custom-call(s32[3]{0:T(128)S(1)} %pad_add_fusion.here_ref, s32[32]{0:T(128)S(1)} %all-reduce.exp_ref, bf16[128,4096]{1,0:T(8,128)(2,1)S(1)} %bitcast.30, bf16[128,4096]{1,0:T(8,128)(2,1)S(1)} %bitcast.34, f32[8,128,128]{2,1,0:T(8,128)S(1)} %get-tuple-element.35.refs_0_.mine_ref), custom_call_target="tpu_custom_call" | custom-call | tf_op jit(solution)/shard_map/updates/pallas_call | solution.py:225
  44.5 8.7 %collective-permute-done.1.other_ref.refs_0_ = f32[8,128,128]{2,1,0:T(8,128)S(1)} collective-permute-done((f32[8,128,128]{2,1,0:T(8,128)S(1)}, f32[8,128,128]{2,1,0:T(8,128)S(1)}, u32[]{:S(2)}, u32[]{:S(2)}) %collective-permute-start.1) | collective-permute-done | bytes 524320 | tf_op jit(solution)/shard_map/ppermute | solution.py:263
  55.4 7.3 %all-to-all-start = ((f32[8,128,128]{2,1,0:T(8,128)}), f32[8,128,128]{2,1,0:T(8,128)}, u32[]{:S(2)}, u32[]{:S(2)}) async-start(f32[8,128,128]{2,1,0:T(8,128)} %copy-done.32), calls=%async_computation | async-start | bytes 1048576 | tf_op jit(solution)/shard_map/all_to_all | solution.py:238
  63.8 4.0 %chip.3 = (f32[8,128,128]{2,1,0:T(8,128)S(1)}, f32[8,128,128]{2,1,0:T(8,128)S(1)}) custom-call(s32[3]{0:T(128)S(1)} %pad_add_fusion.here_ref, s32[32]{0:T(128)S(1)} %all-reduce.exp_ref, f32[8,2,128,128]{3,2,1,0:T(8,128)S(1)} %get-tuple-element.37.after_ref.mine_ref, f32[8,2,128,128]{3,2,1,0:T(8,128)} %collective-permute-done.2.other_ref, ...), custom_call_target="tpu_custom_call" | custom-call | tf_op jit(solution)/shard_map/chip/pallas_call | solution.py:225
  69.4 9.5 %all-to-all-done.parts_ref = f32[8,128,128]{2,1,0:T(8,128)} async-done(((f32[8,128,128]{2,1,0:T(8,128)}), f32[8,128,128]{2,1,0:T(8,128)}, u32[]{:S(2)}, u32[]{:S(2)}) %all-to-all-start) | async-done | bytes 524320 | tf_op jit(solution)/shard_map/all_to_all | solution.py:238
  78.8 1.1 copy-done.16
  79.9 1.7 scan.1
  82.4 5.6 %all-to-all-start.1 = ((f32[8,128,128]{2,1,0:T(8,128)}), f32[8,128,128]{2,1,0:T(8,128)}, u32[]{:S(2)}, u32[]{:S(2)}) async-start(f32[8,128,128]{2,1,0:T(8,128)} %copy-done.39), calls=%async_computation.1 | async-start | bytes 1048576 | tf_op jit(solution)/shard_map/all_to_all | solution.py:238
  88.0 1.1 collective-permute-start.3
  89.1 24.7 %collective-permute-done.3.refs_0_.other_ref = f32[8,128,128]{2,1,0:T(8,128)S(1)} collective-permute-done((f32[8,128,128]{2,1,0:T(8,128)}, f32[8,128,128]{2,1,0:T(8,128)S(1)}, u32[]{:S(2)}, u32[]{:S(2)}) %collective-permute-start.3) | collective-permute-done | bytes 524320 | tf_op jit(solution)/shard_map/ppermute | solution.py:263
  114.6 1.0 copy-done.11
  115.6 1.0 copy-done.14
  116.7 1.0 copy-done.20
  117.7 1.2 chip_state.2
  119.7 1.1 collective-permute-start.4
  120.8 11.7 %collective-permute-done.4.other_edge_ref.after_ref = f32[8,128,128]{2,1,0:T(8,128)S(1)} collective-permute-done((f32[8,128,128]{2,1,0:T(8,128)S(1)}, f32[8,128,128]{2,1,0:T(8,128)S(1)}, u32[]{:S(2)}, u32[]{:S(2)}) %collective-permute-start.4) | collective-permute-done | bytes 524320 | tf_op jit(solution)/shard_map/ppermute | solution.py:263
  132.5 1.0 copy-done.17
  136.9 1.2 copy-done.25
  138.1 1.2 copy-done.27
  140.4 1.0 copy-done.41
  141.4 1.0 core_state.2
  143.4 2.7 collective-permute-done.5.other_ref
  147.1 1.2 copy-done.7
  148.3 5.8 %key_value.2 = (bf16[128,4096]{1,0:T(8,128)(2,1)}, bf16[128,4096]{1,0:T(8,128)(2,1)}, bf16[8,4,128,128]{3,2,1,0:T(8,128)(2,1)S(1)}) custom-call(s32[3]{0:T(128)S(1)} %pad_add_fusion.here_ref, s32[32]{0:T(128)S(1)} %all-reduce.exp_ref, bf16[128,4096]{1,0:T(8,128)(2,1)S(1)} %bitcast.43, bf16[128,4096]{1,0:T(8,128)(2,1)S(1)} %bitcast.31, ...), custom_call_target="tpu_custom_call" | custom-call | tf_op jit(solution)/shard_map/key_value/pallas_call | solution.py:334
  155.0 6.7 %all-to-all-start.2 = ((bf16[32,128,128]{2,1,0:T(8,128)(2,1)}), bf16[32,128,128]{2,1,0:T(8,128)(2,1)}, u32[]{:S(2)}, u32[]{:S(2)}) async-start(bf16[32,128,128]{2,1,0:T(8,128)(2,1)} %bitcast.46), calls=%async_computation.2 | async-start | bytes 2097152 | tf_op jit(solution)/shard_map/all_to_all | solution.py:238
  161.8 1.2 copy-done.8
  163.0 5.8 %key_value.3 = (bf16[128,4096]{1,0:T(8,128)(2,1)}, bf16[128,4096]{1,0:T(8,128)(2,1)}, bf16[8,4,128,128]{3,2,1,0:T(8,128)(2,1)S(1)}) custom-call(s32[3]{0:T(128)S(1)} %pad_add_fusion.here_ref, s32[32]{0:T(128)S(1)} %all-reduce.exp_ref, bf16[128,4096]{1,0:T(8,128)(2,1)S(1)} %bitcast.44, ...), custom_call_target="tpu_custom_call", output_to_operand_aliasing={{0}: (8, {}), {1}: (9, {})} | custom-call | tf_op jit(solution)/shard_map/key_value/pallas_call | solution.py:334
  169.7 9.3 %all-to-all-done.2 = bf16[32,128,128]{2,1,0:T(8,128)(2,1)} async-done(((bf16[32,128,128]{2,1,0:T(8,128)(2,1)}), bf16[32,128,128]{2,1,0:T(8,128)(2,1)}, u32[]{:S(2)}, u32[]{:S(2)}) %all-to-all-start.2) | async-done | bytes 1048608 | tf_op jit(solution)/shard_map/all_to_all | solution.py:238
  179.0 11.6 %weight.2.after_ref.refs_0_ = f32[8,384,128]{2,1,0:T(8,128)} custom-call(bf16[4096,128]{1,0:T(8,128)(2,1)} %bitcast.9.cols_ref, bf16[4096,3072]{1,0:T(8,128)(2,1)} %bitcast.49), custom_call_target="tpu_custom_call" | custom-call | tf_op jit(solution)/shard_map/weight/pallas_call | solution.py:225
  190.7 4.7 %all-to-all-start.3 = ((bf16[32,128,128]{2,1,0:T(8,128)(2,1)}), bf16[32,128,128]{2,1,0:T(8,128)(2,1)}, u32[]{:S(2)}, u32[]{:S(2)}) async-start(bf16[32,128,128]{2,1,0:T(8,128)(2,1)} %bitcast.45), calls=%async_computation.3 | async-start | bytes 2097152 | tf_op jit(solution)/shard_map/all_to_all | solution.py:238
  195.7 4.9 %edge.1.edge_ref = f32[8,128,128]{2,1,0:T(8,128)S(1)} custom-call(s32[3]{0:T(128)S(1)} %pad_add_fusion.here_ref, s32[32]{0:T(128)S(1)} %all-reduce.exp_ref, f32[8,9,128,128]{3,2,1,0:T(8,128)} %bitcast.51, f32[8,9,128,128]{3,2,1,0:T(8,128)} %bitcast.52, f32[8,384,128]{2,1,0:T(8,128)} %weight.2.after_ref.refs_0_), custom_call_target="tpu_custom_call" | custom-call | tf_op jit(solution)/shard_map/edge/pallas_call | solution.py:225
  203.0 9.7 %all-to-all-done.3 = bf16[32,128,128]{2,1,0:T(8,128)(2,1)} async-done(((bf16[32,128,128]{2,1,0:T(8,128)(2,1)}), bf16[32,128,128]{2,1,0:T(8,128)(2,1)}, u32[]{:S(2)}, u32[]{:S(2)}) %all-to-all-start.3) | async-done | bytes 1048608 | tf_op jit(solution)/shard_map/all_to_all | solution.py:238
  212.7 1.0 copy-done.30
  213.7 10.5 %weight.3 = f32[8,384,128]{2,1,0:T(8,128)S(1)} custom-call(bf16[4096,128]{1,0:T(8,128)(2,1)} %bitcast.11.cols_ref, bf16[4096,3072]{1,0:T(8,128)(2,1)} %bitcast.50, f32[8,384,128]{2,1,0:T(8,128)} %weight.2.after_ref.refs_0_, f32[8,128,128]{2,1,0:T(8,128)S(1)} %copy-done.30), custom_call_target="tpu_custom_call" | custom-call | tf_op jit(solution)/shard_map/weight/pallas_call | solution.py:225
  224.3 1.1 copy-done.9
  226.2 13.6 %collective-permute-done.6.other_edge_ref = f32[8,128,128]{2,1,0:T(8,128)S(1)} collective-permute-done((f32[8,128,128]{2,1,0:T(8,128)}, f32[8,128,128]{2,1,0:T(8,128)S(1)}, u32[]{:S(2)}, u32[]{:S(2)}) %collective-permute-start.6) | collective-permute-done | bytes 524320 | tf_op jit(solution)/shard_map/ppermute | solution.py:263
  240.5 1.2 copy-done.5
  244.8 4.0 %core_state.3 = (f32[8,2,128,128]{3,2,1,0:T(8,128)S(1)}, f32[8,2,128,128]{3,2,1,0:T(8,128)S(1)}) custom-call(s32[3]{0:T(128)S(1)} %pad_add_fusion.here_ref, s32[32]{0:T(128)S(1)} %all-reduce.exp_ref, f32[8,128,128]{2,1,0:T(8,128)S(1)} %copy-done.31, f32[8,128,128]{2,1,0:T(8,128)S(1)} %copy-done.43, f32[8,2,128,128]{3,2,1,0:T(8,128)S(1)} %copy-done.5, ...), custom_call_target="tpu_custom_call" | custom-call | tf_op jit(solution)/shard_map/core_state/pallas_call | solution.py:225
  248.9 2.6 collective-permute-done.7.other_ref
  251.6 6.1 %query.1 = bf16[128,4096]{1,0:T(8,128)(2,1)} custom-call(s32[3]{0:T(128)S(1)} %pad_add_fusion.here_ref, s32[32]{0:T(128)S(1)} %all-reduce.exp_ref, bf16[128,4096]{1,0:T(8,128)(2,1)S(1)} %bitcast.33, bf16[128,4096]{1,0:T(8,128)(2,1)S(1)} %bitcast.37, bf16[128,4096]{1,0:T(8,128)(2,1)S(1)} %bitcast.41, f32[8,2,128,128]{3,2,1,0:T(8,128)S(1)} %get-tuple-element.54.mine_ref, ...), custom_call_target="tpu_custom_call" | custom-call | tf_op jit(solution)/shard_map/query/pallas_call | solution.py:225
  257.7 22.1 %reduce-scatter.3.cloned.1.call-done = f32[1,384,128]{2,1,0:T(8,128)} async-done(((f32[8,384,128]{2,1,0:T(8,128)}), f32[1,384,128]{2,1,0:T(8,128)}) %reduce-scatter.3.cloned.1.call-update) | async-done | bytes 196624 | tf_op jit(solution)/shard_map/reduce_scatter | solution.py:368
  280.8 16.7 %all_to_all.25 = f32[16,48,128]{2,1,0:T(8,128)S(1)} all-to-all(f32[16,48,128]{2,1,0:T(8,128)S(1)} %bitcast.53), channel_id=1, replica_groups=mesh['y'=4,'xh'=2,'zh'=4,'zl'=2,'xl'=2,'core'=2] {'y','xh','zl'}, dimensions={0} | all-to-all | bytes 786432 | tf_op jit(solution)/shard_map/all_to_all | solution.py:238
  (110 shorter events, 28.4 us)
Async XLA Ops:
  7.2 32.5 %copy-start = (bf16[1,128,4096]{2,1,0:T(8,128)(2,1)S(1)}, bf16[1,128,4096]{2,1,0:T(8,128)(2,1)}, u32[]{:S(2)}) copy-start(bf16[1,128,4096]{2,1,0:T(8,128)(2,1)} %param.9) | copy-start | bytes 3145732
  7.2 32.5 %copy-start.1 = (bf16[1,128,4096]{2,1,0:T(8,128)(2,1)S(1)}, bf16[1,128,4096]{2,1,0:T(8,128)(2,1)}, u32[]{:S(2)}) copy-start(bf16[1,128,4096]{2,1,0:T(8,128)(2,1)} %param.10) | copy-start | bytes 3145732
  7.2 171.8 %all-gather.5.cloned.1.call-start = ((), (), s32[]{:S(2)}) async-start(), calls=%async_computation.9 | async-start | bytes 25952256 | tf_op jit(solution)/shard_map/all_gather | solution.py:250
  29.1 1.2 copy-start.2
  30.4 1.2 copy-start.6
  34.9 4.7 %copy-start.24 = (f32[8,2,128,128]{3,2,1,0:T(8,128)}, f32[8,2,128,128]{3,2,1,0:T(8,128)S(1)}, u32[]{:S(2)}) copy-start(f32[8,2,128,128]{3,2,1,0:T(8,128)S(1)} %get-tuple-element.33.mine_ref) | copy-start | bytes 3145732
  35.0 2.7 collective-permute-start
  37.7 15.5 %copy-start.26 = (f32[8,2,128,128]{3,2,1,0:T(8,128)}, f32[8,2,128,128]{3,2,1,0:T(8,128)S(1)}, u32[]{:S(2)}) copy-start(f32[8,2,128,128]{3,2,1,0:T(8,128)S(1)} %collective-permute-done.other_ref) | copy-start | bytes 3145732
  38.7 14.5 %copy-start.10 = (f32[8,128,128]{2,1,0:T(8,128)}, f32[8,128,128]{2,1,0:T(8,128)S(1)}, u32[]{:S(2)}) copy-start(f32[8,128,128]{2,1,0:T(8,128)S(1)} %get-tuple-element.35.refs_0_.mine_ref) | copy-start | bytes 1572868
  38.7 14.5 %collective-permute-start.1 = (f32[8,128,128]{2,1,0:T(8,128)S(1)}, f32[8,128,128]{2,1,0:T(8,128)S(1)}, u32[]{:S(2)}, u32[]{:S(2)}) collective-permute-start(f32[8,128,128]{2,1,0:T(8,128)S(1)} %get-tuple-element.36), channel_id=1, source_target_pairs={{0,2},{2,0},{1,3},{3,1},{4,6},{6,4},{5,7},{7,5},{8,10},{10,8},{9,1... | collective-permute-start | bytes 1572872 | tf_op jit(solution)/shard_map/ppermute | solution.py:263
  44.5 34.3 %copy-start.4 = (f32[8,2,128,128]{3,2,1,0:T(8,128)}, f32[8,2,128,128]{3,2,1,0:T(8,128)S(1)}, u32[]{:S(2)}) copy-start(f32[8,2,128,128]{3,2,1,0:T(8,128)S(1)} %get-tuple-element.37.after_ref.mine_ref) | copy-start | bytes 3145732
  44.5 18.2 %collective-permute-start.2 = (f32[8,2,128,128]{3,2,1,0:T(8,128)}, f32[8,2,128,128]{3,2,1,0:T(8,128)}, u32[]{:S(2)}, u32[]{:S(2)}) collective-permute-start(f32[8,2,128,128]{3,2,1,0:T(8,128)} %get-tuple-element.38), channel_id=1, source_target_pairs={{0,1},{1,0},{2,3},{3,2},{4,5},{5,4},{6,7},{7,6},{8,9},{9,8},{10,11... | collective-permute-start | bytes 3145736 | tf_op jit(solution)/shard_map/ppermute | solution.py:263
  53.2 79.3 %copy-start.44 = (f32[1,1,128,128]{3,2,1,0:T(8,128)S(1)}, f32[1,1,128,128]{3,2,1,0:T(8,128)}, u32[]{:S(2)}) copy-start(f32[1,1,128,128]{3,2,1,0:T(8,128)} %param.13) | copy-start | bytes 196612
  55.4 23.4 %all-to-all-start = ((f32[8,128,128]{2,1,0:T(8,128)}), f32[8,128,128]{2,1,0:T(8,128)}, u32[]{:S(2)}, u32[]{:S(2)}) async-start(f32[8,128,128]{2,1,0:T(8,128)} %copy-done.32), calls=%async_computation | async-start | bytes 1048576 | tf_op jit(solution)/shard_map/all_to_all | solution.py:238
  62.7 1.0 copy-start.13
  78.8 1.1 copy-start.16
  82.4 64.6 %copy-start.3 = (bf16[1,128,4096]{2,1,0:T(8,128)(2,1)S(1)}, bf16[1,128,4096]{2,1,0:T(8,128)(2,1)}, u32[]{:S(2)}) copy-start(bf16[1,128,4096]{2,1,0:T(8,128)(2,1)} %param.11) | copy-start | bytes 3145732
  82.4 32.2 %all-to-all-start.1 = ((f32[8,128,128]{2,1,0:T(8,128)}), f32[8,128,128]{2,1,0:T(8,128)}, u32[]{:S(2)}, u32[]{:S(2)}) async-start(f32[8,128,128]{2,1,0:T(8,128)} %copy-done.39), calls=%async_computation.1 | async-start | bytes 1048576 | tf_op jit(solution)/shard_map/all_to_all | solution.py:238
  88.0 107.7 %all-gather.7.cloned.1.call-start = ((), (), s32[]{:S(2)}) async-start(), calls=%async_computation.10 | async-start | bytes 5308416 | tf_op jit(solution)/shard_map/all_gather | solution.py:321
  88.0 25.8 %collective-permute-start.3 = (f32[8,128,128]{2,1,0:T(8,128)}, f32[8,128,128]{2,1,0:T(8,128)S(1)}, u32[]{:S(2)}, u32[]{:S(2)}) collective-permute-start(f32[8,128,128]{2,1,0:T(8,128)} %copy-done.46), channel_id=1, source_target_pairs={{0,2},{2,0},{1,3},{3,1},{4,6},{6,4},{5,7},{7,5},{8,10},{10,8},{9,1... | collective-permute-start | bytes 1572872 | tf_op jit(solution)/shard_map/ppermute | solution.py:263
  114.6 1.0 copy-start.11
  115.6 1.0 copy-start.14
  116.7 1.0 copy-start.20
  119.7 12.8 %collective-permute-start.4 = (f32[8,128,128]{2,1,0:T(8,128)S(1)}, f32[8,128,128]{2,1,0:T(8,128)S(1)}, u32[]{:S(2)}, u32[]{:S(2)}) collective-permute-start(f32[8,128,128]{2,1,0:T(8,128)S(1)} %get-tuple-element.43), channel_id=1, source_target_pairs={{0,2},{2,0},{1,3},{3,1},{4,6},{6,4},{5,7},{7,5},{8,10},{10,8},{9,1... | collective-permute-start | bytes 1572872 | tf_op jit(solution)/shard_map/ppermute | solution.py:263
  132.5 1.0 copy-start.17
  133.6 1.0 copy-start.21
  136.9 1.2 copy-start.25
  138.1 1.2 copy-start.27
  139.3 1.0 copy-start.34
  140.4 1.0 copy-start.41
  142.5 1.0 copy-start.23
  143.4 2.7 collective-permute-start.5
  147.1 1.2 copy-start.7
  155.0 24.0 %all-to-all-start.2 = ((bf16[32,128,128]{2,1,0:T(8,128)(2,1)}), bf16[32,128,128]{2,1,0:T(8,128)(2,1)}, u32[]{:S(2)}, u32[]{:S(2)}) async-start(bf16[32,128,128]{2,1,0:T(8,128)(2,1)} %bitcast.46), calls=%async_computation.2 | async-start | bytes 2097152 | tf_op jit(solution)/shard_map/all_to_all | solution.py:238
  161.7 78.8 %reduce-scatter.5.cloned.1.call-start = ((), (), s32[]{:S(2)}) async-start(), calls=%async_computation.8 | async-start | bytes 1769472 | tf_op jit(solution)/shard_map/reduce_scatter | solution.py:368
  161.8 1.2 copy-start.8
  190.7 22.0 %all-to-all-start.3 = ((bf16[32,128,128]{2,1,0:T(8,128)(2,1)}), bf16[32,128,128]{2,1,0:T(8,128)(2,1)}, u32[]{:S(2)}, u32[]{:S(2)}) async-start(bf16[32,128,128]{2,1,0:T(8,128)(2,1)} %bitcast.45), calls=%async_computation.3 | async-start | bytes 2097152 | tf_op jit(solution)/shard_map/all_to_all | solution.py:238
  195.4 84.4 %reduce-scatter.3.cloned.1.call-start = ((), (), s32[]{:S(2)}) async-start(), calls=%async_computation.7 | async-start | bytes 1769472 | tf_op jit(solution)/shard_map/reduce_scatter | solution.py:368
  195.7 5.0 %copy-start.18 = (f32[8,128,128]{2,1,0:T(8,128)S(1)}, f32[8,128,128]{2,1,0:T(8,128)}, u32[]{:S(2)}) copy-start(f32[8,128,128]{2,1,0:T(8,128)} %copy-done.15) | copy-start | bytes 1572868
  195.7 5.0 %copy-start.22 = (f32[8,128,128]{2,1,0:T(8,128)S(1)}, f32[8,128,128]{2,1,0:T(8,128)}, u32[]{:S(2)}) copy-start(f32[8,128,128]{2,1,0:T(8,128)} %copy-done.19) | copy-start | bytes 1572868
  212.7 1.0 copy-start.30
  224.3 1.2 copy-start.9
  225.4 14.3 %collective-permute-start.6 = (f32[8,128,128]{2,1,0:T(8,128)}, f32[8,128,128]{2,1,0:T(8,128)S(1)}, u32[]{:S(2)}, u32[]{:S(2)}) collective-permute-start(f32[8,128,128]{2,1,0:T(8,128)} %copy-done.45), channel_id=1, source_target_pairs={{0,2},{2,0},{1,3},{3,1},{4,6},{6,4},{5,7},{7,5},{8,10},{10,8},{9,1... | collective-permute-start | bytes 1572872 | tf_op jit(solution)/shard_map/ppermute | solution.py:263
  240.5 1.2 copy-start.5
  241.8 1.0 copy-start.31
  243.7 1.0 copy-start.43
  244.8 35.1 %copy-start.38 = (f32[1,384,128]{2,1,0:T(8,128)S(1)}, f32[1,384,128]{2,1,0:T(8,128)}, u32[]{:S(2)}) copy-start(f32[1,384,128]{2,1,0:T(8,128)} %reduce-scatter.5.cloned.1.call-done.refs_0_) | copy-start | bytes 589828
  248.8 2.7 collective-permute-start.7
  (16 other events, 13.4 us)
Sparse Core Ops, SparseCore 0:
  10.6 112.1 all-gather.4
  137.0 58.6 all-gather.6
  198.3 40.1 reduce-scatter.4
  240.8 38.9 reduce-scatter.2

commit v5 on v3

--- a/solution.py
+++ b/solution.py
@@ -13,7 +13,9 @@
 bf16 = jnp.bfloat16
 PLANE = ("y", "xh", "xl", "core")
 QUAD = ("xl", "core")
-CHAIN = ("z", "xl", "core")
+LINE = ("zh", "zl")
+CHAIN = ("zh", "zl", "xl", "core")
+FINAL = ("y", "xh", "zl")
 
 
 def log_rate(exponent, length):
@@ -69,7 +71,7 @@
         )
 
 
-def quad_kernel(here_ref, exp_ref, mine_ref, other_ref, out_ref, *, length, span):
+def quad_kernel(here_ref, exp_ref, mine_ref, other_ref, after_ref, out_ref, *, length, span):
     for group in range(out_ref.shape[0]):
         rate = log_rate(exp_ref[4 * group + 2 * here_ref[1] + here_ref[2]], length)
         out_ref[group] = weighed(
@@ -77,7 +79,7 @@
         )
 
 
-def scan_kernel(own_ref, parts_ref, out_ref, grad_ref, *, length, span):
+def scan_kernel(own_ref, parts_ref, after_ref, out_ref, grad_ref, *, length, span):
     rate = log_rate(own_ref[0], length)
     decay = power_of(rate, span)
     state = jnp.zeros(grad_ref.shape, f32)
@@ -109,8 +111,9 @@
 
 
 def chip_state_kernel(
-    here_ref, exp_ref, edge_ref, mine_ref, other_ref, keep_ref, send_ref, *, reverse, length, span
-):
+    here_ref, exp_ref, edge_ref, mine_ref, other_ref, *refs, reverse, length, span
+):
+    keep_ref, send_ref = refs[-2:]
     behind = here_ref[1] == (0 if reverse else 1)
     for group in range(edge_ref.shape[0]):
         rate = log_rate(exp_ref[4 * group + 2 * here_ref[1] + here_ref[2]], length)
@@ -121,9 +124,10 @@
 
 
 def core_state_kernel(
-    here_ref, exp_ref, mine_edge_ref, other_edge_ref, mine_ref, other_ref, keep_ref, send_ref,
-    *, reverse, length, span
-):
+    here_ref, exp_ref, mine_edge_ref, other_edge_ref, mine_ref, other_ref, *refs,
+    reverse, length, span
+):
+    keep_ref, send_ref = refs[-2:]
     group = pl.program_id(0)
     behind = here_ref[2] == (0 if reverse else 1)
     for chip, edge_ref in enumerate((mine_edge_ref, other_edge_ref)):
@@ -140,34 +144,45 @@
     return jnp.where(here_ref[2] == slot % 2, mine_ref[0, chip], other_ref[0, chip])
 
 
-def key_value_kernel(
-    here_ref, exp_ref, query_ref, key_ref, value_ref, grad_ref, mine_ref, other_ref,
-    gk_ref, gv_ref, send_ref, *, length
+def inner_kernel(
+    exp_ref, query_ref, key_ref, value_ref, grad_ref, after_ref, gk_ref, gv_ref, *, length
 ):
     group = pl.program_id(0)
     span = query_ref.shape[0]
     source = lax.broadcasted_iota(jnp.int32, (span, span), 0)
     target = lax.broadcasted_iota(jnp.int32, (span, span), 1)
     gap = (target - source).astype(f32)
-    left = span - lax.broadcasted_iota(jnp.int32, (span, WIDTH), 0).astype(f32)
     for slot in range(4):
         rate = log_rate(exp_ref[4 * group + slot], length)
         lanes = pl.ds(slot * WIDTH, WIDTH)
         query, key = query_ref[:, lanes], key_ref[:, lanes]
         value, grad = value_ref[:, lanes], grad_ref[:, lanes]
         mask = jnp.where(gap >= 0.0, jnp.exp(rate * jnp.maximum(gap, 0.0)), 0.0)
-        tail = jnp.exp(rate * left)
         grad_scores = jnp.concatenate(halves(dot(value, grad, ((1,), (1,))) * mask), 1)
         key_scores = jnp.concatenate(halves(dot(key, query, ((1,), (1,))) * mask), 1)
+        gk_ref[:, lanes] = dot(grad_scores, jnp.concatenate((query, query), 0), ((1,), (0,)))
+        gv_ref[:, lanes] = dot(key_scores, jnp.concatenate((grad, grad), 0), ((1,), (0,)))
+
+
+def key_value_kernel(
+    here_ref, exp_ref, key_ref, value_ref, inner_gk_ref, inner_gv_ref, mine_ref, other_ref,
+    gk_ref, gv_ref, send_ref, *, length
+):
+    group = pl.program_id(0)
+    span = key_ref.shape[0]
+    left = span - lax.broadcasted_iota(jnp.int32, (span, WIDTH), 0).astype(f32)
+    for slot in range(4):
+        rate = log_rate(exp_ref[4 * group + slot], length)
+        lanes = pl.ds(slot * WIDTH, WIDTH)
+        key, value = key_ref[:, lanes], value_ref[:, lanes]
+        tail = jnp.exp(rate * left)
         high, low = halves(picked(here_ref, mine_ref, other_ref, slot))
-        gk = tail * dot(
+        gk = inner_gk_ref[:, lanes] + tail * dot(
             jnp.concatenate((value, value), 1), jnp.concatenate((high, low), 1), ((1,), (1,))
         )
-        gk = gk + dot(grad_scores, jnp.concatenate((query, query), 0), ((1,), (0,)))
-        gv = tail * dot(
+        gv = inner_gv_ref[:, lanes] + tail * dot(
             jnp.concatenate((key, key), 1), jnp.concatenate((high, low), 0), ((1,), (0,))
         )
-        gv = gv + dot(key_scores, jnp.concatenate((grad, grad), 0), ((1,), (0,)))
         gk_ref[:, lanes] = gk.astype(bf16)
         gv_ref[:, lanes] = gv.astype(bf16)
         send_ref[slot, 0] = gk.astype(bf16)
@@ -197,12 +212,12 @@
         gq_ref[:, lanes] = gq.astype(bf16)
 
 
-def weight_kernel(cols_ref, rows_ref, out_ref, turned):
-    @pl.when(pl.program_id(0) == 0)
-    def _():
-        turned[...] = cols_ref[...].T
-
-    product = dot(turned[...], rows_ref[...], ((1,), (0,))).T
+def turn_kernel(rows_ref, after_ref, out_ref):
+    out_ref[...] = rows_ref[...].T
+
+
+def weight_kernel(cols_ref, turned_ref, out_ref):
+    product = dot(turned_ref[...], cols_ref[...], ((1,), (0,)))
     out_ref[0] = product[:, :WIDTH]
     out_ref[1] = product[:, WIDTH:]
 
@@ -211,7 +226,24 @@
 FREE = pl.BlockSpec(memory_space=pl.ANY)
 
 
-def call(kernel, grid, in_specs, out_specs, out_shape, args, scratch=(), name=None):
+def exchange(array, axes):
+    return lax.all_to_all(array, axes, split_axis=0, concat_axis=0, tiled=True)
+
+
+def swap(array, axis):
+    return lax.ppermute(array, axis, [(0, 1), (1, 0)])
+
+
+def call(
+    kernel, grid, in_specs, out_specs, out_shape, args, arrived=(), scratch=(), name=None, vmem=8
+):
+    args = [
+        arg
+        if spec is SMEM or any(arg is item for item in arrived)
+        else pltpu.with_memory_space_constraint(arg, pltpu.HBM)
+        for spec, arg in zip(in_specs, args)
+    ]
+    out_shape = jax.tree.map(lambda leaf: pltpu.HBM(leaf.shape, leaf.dtype), out_shape)
     return pl.pallas_call(
         kernel,
         grid=grid,
@@ -220,12 +252,8 @@
         out_shape=out_shape,
         scratch_shapes=scratch,
         name=name,
-        compiler_params=pltpu.CompilerParams(vmem_limit_bytes=48 * 1024 * 1024),
+        compiler_params=pltpu.CompilerParams(vmem_limit_bytes=vmem * 1024 * 1024),
     )(*args)
-
-
-def exchange(array, axes):
-    return lax.all_to_all(array, axes, split_axis=0, concat_axis=0, tiled=True)
 
 
 def per_device(inputs_x, queries, keys, values, grad_out, decay_exp, state_in):
@@ -236,7 +264,7 @@
     tile = (WIDTH, WIDTH)
     query, key, value, grad = queries[0], keys[0], values[0], grad_out[0]
     exps = lax.all_gather(decay_exp, CHAIN, axis=0, tiled=True)
-    here = jnp.stack([lax.axis_index(axis) for axis in CHAIN]).astype(jnp.int32)
+    here = jnp.stack([lax.axis_index(axis) for axis in (LINE, "xl", "core")]).astype(jnp.int32)
     rows = lax.all_gather(inputs_x[0], PLANE, axis=0, tiled=True)
 
     head_cols = pl.BlockSpec((span, 4 * WIDTH), lambda i: (0, i))
@@ -249,15 +277,18 @@
     tile_shape = jax.ShapeDtypeStruct(tile, f32)
     token_shape = jax.ShapeDtypeStruct((span, features), bf16)
 
-    def swap(array, axis):
-        return lax.ppermute(array, axis, [(0, 1), (1, 0)])
-
-    def run(body, grid, in_specs, out_specs, out_shape, args, after=None, scratch=(), name=None, **sizes):
+    arrived = []
+
+    def noted(array):
+        arrived.append(array)
+        return array
+
+    def run(body, grid, in_specs, out_specs, out_shape, args, after=None, name=None, **sizes):
         if after is not None:
             in_specs, args = in_specs + [FREE], args + (after,)
         return call(
             functools.partial(body, length=length, **sizes), grid, in_specs, out_specs, out_shape,
-            args, scratch, name,
+            args, arrived, name=name,
         )
 
     def updates(left, right, reverse, after=None):
@@ -274,67 +305,79 @@
             reverse=reverse, span=float(span), name="chip",
         )
 
-    def chip_state(edges, mine, other, reverse):
+    def chip_state(edges, mine, other, reverse, after=None):
         return run(
             chip_state_kernel, (1,), [SMEM, SMEM, line, line, line], [line, line],
-            [line_shape, line_shape], (here, exps, edges, mine, other),
+            [line_shape, line_shape], (here, exps, edges, mine, other), after,
             reverse=reverse, span=2.0 * span, name="chip_state",
         )
 
-    def core_state(mine_edge, other_edge, mine, other, reverse):
+    def core_state(mine_edge, other_edge, mine, other, reverse, after=None):
         return run(
             core_state_kernel, (groups,),
             [SMEM, SMEM, line_tile, line_tile, pair_tiles, pair_tiles], [pair_tiles, pair_tiles],
-            [pair_shape, pair_shape], (here, exps, mine_edge, other_edge, mine, other),
+            [pair_shape, pair_shape], (here, exps, mine_edge, other_edge, mine, other), after,
             reverse=reverse, span=float(span), name="core_state",
         )
 
     r_mine, sent = updates(query, grad, True)
-    r_other = swap(sent, "core")
+    r_other = noted(swap(sent, "core"))
     r_chip, sent = chip(r_mine, r_other, True)
-    r_next = swap(sent, "xl")
-    f_mine, sent = updates(key, value, False, r_chip)
-    f_other = swap(sent, "core")
-    r_parts = exchange(run(
+    r_next = noted(swap(sent, "xl"))
+    f_mine, sent = updates(key, value, False, r_mine)
+    f_other = noted(swap(sent, "core"))
+    r_quad = run(
         quad_kernel, (1,), [SMEM, SMEM, line, line], line, line_shape,
-        (here, exps, r_chip, r_next), span=2.0 * span, name="quad",
-    ), "z")
-    f_chip, sent = chip(f_mine, f_other, False, r_next)
-    f_next = swap(sent, "xl")
+        (here, exps, r_chip, r_next), r_mine, span=2.0 * span, name="quad",
+    )
+    f_chip, sent = chip(f_mine, f_other, False, r_quad)
+    f_next = noted(swap(sent, "xl"))
+    r_quad, f_chip = lax.optimization_barrier((r_quad, f_chip))
+    r_parts = noted(exchange(r_quad, LINE))
     r_edges, state_grad = run(
         scan_kernel, (1,), [SMEM, line], [line, single], [line_shape, tile_shape],
-        (decay_exp, r_parts), span=4.0 * span, name="scan",
-    )
-    r_edges = exchange(r_edges, "z")
-    r_edge, sent = chip_state(r_edges, r_chip, r_next, True)
-    r_far = swap(sent, "xl")
+        (decay_exp, r_parts), f_next, span=4.0 * span, name="scan",
+    )
+    inner_shape = jax.ShapeDtypeStruct((span, features), f32)
+    inner_gk, inner_gv = run(
+        inner_kernel, (groups,), [SMEM] + 4 * [head_cols], 2 * [head_cols], 2 * [inner_shape],
+        (exps, query, key, value, grad), r_edges, name="inner",
+    )
+    r_edges = noted(exchange(r_edges, LINE))
+    r_edge, sent = chip_state(r_edges, r_chip, r_next, True, inner_gk)
+    r_far = noted(swap(sent, "xl"))
+    mine, sent = core_state(r_edge, r_far, r_mine, r_other, True)
+    other = noted(swap(sent, "core"))
     f_parts = lax.all_gather(run(
         line_kernel, (1,), [SMEM, SMEM, line, line, single],
         pl.BlockSpec((groups + 1,) + tile, lambda i: (0, 0, 0)),
         jax.ShapeDtypeStruct((groups + 1,) + tile, f32),
-        (here, exps, f_chip, f_next, state_in[0, 0]), r_edge, span=2.0 * span, name="line",
-    ), "z")
-    mine, sent = core_state(r_edge, r_far, r_mine, r_other, True)
-    other = swap(sent, "core")
+        (here, exps, f_chip, f_next, state_in[0, 0]), mine, span=2.0 * span, name="line",
+    ), LINE)
     grad_key, grad_value, send = run(
         key_value_kernel, (groups,), [SMEM, SMEM] + 4 * [head_cols] + 2 * [pair_tiles],
         [head_cols, head_cols, pl.BlockSpec((8, 1, span, WIDTH), lambda i: (0, i % 4, 0, i // 4))],
         [token_shape, token_shape, jax.ShapeDtypeStruct((8, 4, span, 2 * WIDTH), bf16)],
-        (here, exps, query, key, value, grad, mine, other), name="key_value",
-    )
-    cols = exchange(send.reshape(32, span, 2 * WIDTH), PLANE).reshape(32 * span, 2 * WIDTH)
+        (here, exps, key, value, inner_gk, inner_gv, mine, other), name="key_value",
+    )
+    cols = exchange(send.reshape(32, span, 2 * WIDTH), PLANE)
+    cols = noted(cols.reshape(32 * span, 2 * WIDTH))
 
     tokens, width = rows.shape
     block = width // 4
+    turned = call(
+        turn_kernel, (width // 256,), [pl.BlockSpec((tokens, 256), lambda i: (0, i)), FREE],
+        pl.BlockSpec((256, tokens), lambda i: (i, 0)),
+        jax.ShapeDtypeStruct((width, tokens), bf16), (rows, send), name="turn", vmem=16,
+    )
     partial = call(
         weight_kernel, (4,),
         [
             pl.BlockSpec((tokens, 2 * WIDTH), lambda i: (0, 0)),
-            pl.BlockSpec((tokens, block), lambda i: (0, i)),
+            pl.BlockSpec((block, tokens), lambda i: (i, 0)),
         ],
         pl.BlockSpec((2, block, WIDTH), lambda i: (i, 0, 0)),
-        jax.ShapeDtypeStruct((8, block, WIDTH), f32),
-        (cols, rows), scratch=[pltpu.VMEM((2 * WIDTH, tokens), bf16)], name="weight",
+        jax.ShapeDtypeStruct((8, block, WIDTH), f32), (cols, turned), arrived, name="weight", vmem=32,
     )
     f_edges = run(
         edge_kernel, (groups,),
@@ -346,14 +389,15 @@
         span=4.0 * span, name="edge",
     )
     f_edge, sent = chip_state(f_edges, f_chip, f_next, False)
-    f_far = swap(sent, "xl")
+    f_far = noted(swap(sent, "xl"))
     mine, sent = core_state(f_edge, f_far, f_mine, f_other, False)
-    other = swap(sent, "core")
+    other = noted(swap(sent, "core"))
     grad_query = run(
         query_kernel, (groups,), [SMEM, SMEM] + 3 * [head_cols] + 2 * [pair_tiles], head_cols,
         token_shape, (here, exps, key, value, grad, mine, other), name="query",
     )
-    summed = lax.psum_scatter(partial, "z", scatter_dimension=0, tiled=True)
+    summed = lax.psum_scatter(partial, LINE, scatter_dimension=0, tiled=True)
+    summed, grad_query = lax.optimization_barrier((summed, grad_query))
     pieces = exchange(summed.reshape(8, block // 8, WIDTH), ("y", "xh"))
     pieces = pieces.reshape(2, 4, block // 8, WIDTH).transpose(0, 2, 1, 3)
     weight_grads = pieces.reshape(2, 1, block // 8, 4 * WIDTH)
@@ -363,7 +407,7 @@
 
 
 def solution(mesh):
-    fine = Mesh(mesh.devices.reshape(4, 2, 8, 2, 2), ("y", "xh", "z", "xl", "core"))
+    fine = Mesh(mesh.devices.reshape(4, 2, 4, 2, 2, 2), ("y", "xh", "zh", "zl", "xl", "core"))
     dp, seq = ("y", "xh"), CHAIN
     tokens = P(dp, seq, None)
     in_specs = (tokens, tokens, tokens, tokens, tokens, P(seq), P(dp, seq, None, None))

time: 275 us -> 281 us (1.022)
  Pallas kernels: 62.8 us -> 114 us
  blocking collectives: 53.4 us -> 34.8 us
  local copies, waits for them, and re-layouts: 22.1 us -> 4.17 us
  waiting for transfers between devices: 96.2 us -> 88.1 us
    pallas_call x15 -> x17, Pallas kernels: 62.8 us -> 114 us  [call(): pl.pallas_call(kernel, grid=grid, in_specs=in_specs, out_specs=out_specs,...]
    all_to_all x1, blocking collectives: 34.9 us -> 16.3 us  [exchange(): return lax.all_to_all(array, axes, split_axis=0, concat_axis=0, tiled=True)]
    unnamed x57 -> x9, local copies, waits for them, and re-layouts: 21 us -> 3.01 us
    ppermute x8, waiting for transfers between devices: 58.8 us -> 70.2 us  [swap(): return lax.ppermute(array, axis, [(0, 1), (1, 0)])]
    all_to_all x3, waiting for transfers between devices: 19.4 us -> 8.45 us  [exchange(): return lax.all_to_all(array, axes, split_axis=0, concat_axis=0, tiled=True)]
    reduce_scatter x1, waiting for transfers between devices: 17.3 us -> 8.7 us  [per_device(): summed = lax.psum_scatter(partial, LINE, scatter_dimension=0, tiled=True)]
  transfers between devices with their start and end apart: 14 -> 14, of which waited for: 10 -> 9; matrix products, arithmetic and copies ran while one was open for 1% -> 1% of each run, Pallas kernels for 23% -> 41%
where the time goes in v5:
time: 281 us; the launch traced here: 278 us
  Pallas kernels  114 us (41%)
  waiting for transfers between devices  88.1 us (31%)
  blocking collectives  34.8 us (12%)
  starting transfers between devices  23.2 us (8%)
  between operations  14.5 us (5%)
  local copies, waits for them, and re-layouts  4.17 us (1%)
    pallas_call x17, Pallas kernels, call(): pl.pallas_call(kernel, grid=grid, in_specs=in_specs, out_specs=out_specs,...  114 us
    ppermute x8, waiting for transfers between devices, swap(): return lax.ppermute(array, axis, [(0, 1), (1, 0)])  70.2 us
    all_to_all x3, starting transfers between devices, exchange(): return lax.all_to_all(array, axes, split_axis=0, concat_axis=0, tiled=True)  19.3 us
    unnamed x1, blocking collectives  18.5 us
    all_to_all x1, blocking collectives, exchange(): return lax.all_to_all(array, axes, split_axis=0, concat_axis=0, tiled=True)  16.3 us
    reduce_scatter x1, waiting for transfers between devices, per_device(): summed = lax.psum_scatter(partial, LINE, scatter_dimension=0, tiled=True)  8.7 us
    all_to_all x3, waiting for transfers between devices, exchange(): return lax.all_to_all(array, axes, split_axis=0, concat_axis=0, tiled=True)  8.45 us
  transfers between devices with their start and end apart: 14, of which 9 were waited for; matrix products, arithmetic and copies ran while one was open for 1% of the time, Pallas kernels for 41%

profile of v5, /device:TPU:32, one launch (start us, length us, event | category | flops | bytes accessed | tf_op | source)
XLA Modules:
  0.0 278.4 jit_solution(12865510408687981368)
XLA Ops:
  7.2 0.0 all-gather.5.cloned.1.call-start
  7.2 0.7 all-gather.5.cloned.1.call-update
  8.6 1.3 dynamic-slice
  9.8 0.8 dynamic-update-slice
  10.6 18.5 %all-reduce.exp_ref = s32[32]{0:T(128)S(1)} all-reduce(s32[32]{0:T(128)S(1)} %dynamic-update-slice), channel_id=1, replica_groups=mesh['y'=4,'xh'=2,'zh'=4,'zl'=2,'xl'=2,'core'=2] {'zh','zl','xl','core'}, use_global_device_ids=true, to_apply=%add | all-reduce | flops 32 | bytes 256
  29.0 0.1 pad_add_fusion.here_ref
  29.1 6.7 %updates.2 = (f32[8,2,128,128]{3,2,1,0:T(8,128)}, f32[8,2,128,128]{3,2,1,0:T(8,128)}) custom-call(s32[3]{0:T(128)S(1)} %pad_add_fusion.here_ref, s32[32]{0:T(128)S(1)} %all-reduce.exp_ref, bf16[128,4096]{1,0:T(8,128)(2,1)} %bitcast.38, bf16[128,4096]{1,0:T(8,128)(2,1)} %bitcast.34), custom_call_target="tpu_custom_call" | custom-call | tf_op jit(solution)/shard_map/updates/pallas_call | solution.py:247
  35.8 6.8 %updates.3 = (f32[8,2,128,128]{3,2,1,0:T(8,128)}, f32[8,2,128,128]{3,2,1,0:T(8,128)}) custom-call(s32[3]{0:T(128)S(1)} %pad_add_fusion.here_ref, s32[32]{0:T(128)S(1)} %all-reduce.exp_ref, bf16[128,4096]{1,0:T(8,128)(2,1)} %bitcast.26, bf16[128,4096]{1,0:T(8,128)(2,1)} %bitcast.30, f32[8,2,128,128]{3,2,1,0:T(8,128)} %get-tuple-element.32.mine_ref.after_ref.refs_0_), custom_call_target="tpu_custom_call" | custom-call | tf_op jit(solution)/shard_map/updates/pallas_call | solution.py:247
  42.6 0.5 collective-permute-start.2
  43.1 5.3 %chip.2 = (f32[8,128,128]{2,1,0:T(8,128)}, f32[8,128,128]{2,1,0:T(8,128)}) custom-call(s32[3]{0:T(128)S(1)} %pad_add_fusion.here_ref, s32[32]{0:T(128)S(1)} %all-reduce.exp_ref, f32[8,2,128,128]{3,2,1,0:T(8,128)} %get-tuple-element.32.mine_ref.after_ref.refs_0_, f32[8,2,128,128]{3,2,1,0:T(8,128)S(1)} %collective-permute-done.other_ref), custom_call_target="tpu_custom_call" | custom-call | tf_op jit(solution)/shard_map/chip/pallas_call | solution.py:247
  48.3 0.9 collective-permute-start.1
  49.2 20.5 %collective-permute-done.1.other_ref = f32[8,128,128]{2,1,0:T(8,128)S(1)} collective-permute-done((f32[8,128,128]{2,1,0:T(8,128)}, f32[8,128,128]{2,1,0:T(8,128)S(1)}, u32[]{:S(2)}, u32[]{:S(2)}) %collective-permute-start.1) | collective-permute-done | bytes 524320 | tf_op jit(solution)/shard_map/ppermute | solution.py:234
  69.7 2.0 quad.1.refs_0_
  71.7 5.3 %chip.3 = (f32[8,128,128]{2,1,0:T(8,128)}, f32[8,128,128]{2,1,0:T(8,128)}) custom-call(s32[3]{0:T(128)S(1)} %pad_add_fusion.here_ref, s32[32]{0:T(128)S(1)} %all-reduce.exp_ref, f32[8,2,128,128]{3,2,1,0:T(8,128)} %get-tuple-element.36.mine_ref, f32[8,2,128,128]{3,2,1,0:T(8,128)S(1)} %collective-permute-done.2.other_ref, f32[8,128,128]{2,1,0:T(8,128)} %quad.1.refs_0_), custom_call_target="tpu_custom_call" | custom-call | tf_op jit(solution)/shard_map/chip/pallas_call | solution.py:247
  77.0 1.0 copy-done
  78.0 5.0 %all-to-all-start = ((f32[8,128,128]{2,1,0:T(8,128)}), f32[8,128,128]{2,1,0:T(8,128)S(1)}, u32[]{:S(2)}, u32[]{:S(2)}) async-start(f32[8,128,128]{2,1,0:T(8,128)} %quad.1.refs_0_), calls=%async_computation | async-start | bytes 1048576 | tf_op jit(solution)/shard_map/all_to_all | solution.py:230
  83.0 1.2 collective-permute-start.3
  84.2 23.7 %collective-permute-done.3.after_ref.other_ref = f32[8,128,128]{2,1,0:T(8,128)S(1)} collective-permute-done((f32[8,128,128]{2,1,0:T(8,128)}, f32[8,128,128]{2,1,0:T(8,128)S(1)}, u32[]{:S(2)}, u32[]{:S(2)}) %collective-permute-start.3) | collective-permute-done | bytes 524320 | tf_op jit(solution)/shard_map/ppermute | solution.py:234
  108.0 0.9 scan.1
  108.8 7.2 %all-to-all-start.1 = ((f32[8,128,128]{2,1,0:T(8,128)}), f32[8,128,128]{2,1,0:T(8,128)S(1)}, u32[]{:S(2)}, u32[]{:S(2)}) async-start(f32[8,128,128]{2,1,0:T(8,128)} %get-tuple-element.41.after_ref), calls=%async_computation.1 | async-start | bytes 1048576 | tf_op jit(solution)/shard_map/all_to_all | solution.py:230
  116.0 10.3 %inner.1 = (f32[128,4096]{1,0:T(8,128)}, f32[128,4096]{1,0:T(8,128)}) custom-call(s32[32]{0:T(128)S(1)} %all-reduce.exp_ref, bf16[128,4096]{1,0:T(8,128)(2,1)} %bitcast.39, bf16[128,4096]{1,0:T(8,128)(2,1)} %bitcast.27, bf16[128,4096]{1,0:T(8,128)(2,1)} %bitcast.31, bf16[128,4096]{1,0:T(8,128)(2,1)} %bitcast.35, f32[8,128,128]{2,1,0:T(8,128)} %get-tuple-element.41.after_ref), custom_call_target="tpu_custom_call" | custom-call | tf_op jit(solution)/shard_map/inner/pallas_call | solution.py:247
  126.3 1.6 all-to-all-done.1.edge_ref
  128.0 2.2 chip_state.2
  130.2 1.1 collective-permute-start.4
  131.3 8.3 %collective-permute-done.4.other_edge_ref = f32[8,128,128]{2,1,0:T(8,128)S(1)} collective-permute-done((f32[8,128,128]{2,1,0:T(8,128)}, f32[8,128,128]{2,1,0:T(8,128)S(1)}, u32[]{:S(2)}, u32[]{:S(2)}) %collective-permute-start.4) | collective-permute-done | bytes 524320 | tf_op jit(solution)/shard_map/ppermute | solution.py:234
  139.6 5.7 %core_state.2 = (f32[8,2,128,128]{3,2,1,0:T(8,128)}, f32[8,2,128,128]{3,2,1,0:T(8,128)}) custom-call(s32[3]{0:T(128)S(1)} %pad_add_fusion.here_ref, s32[32]{0:T(128)S(1)} %all-reduce.exp_ref, f32[8,128,128]{2,1,0:T(8,128)} %get-tuple-element.44.mine_edge_ref, f32[8,128,128]{2,1,0:T(8,128)S(1)} %collective-permute-done.4.other_edge_ref, ...), custom_call_target="tpu_custom_call" | custom-call | tf_op jit(solution)/shard_map/core_state/pallas_call | solution.py:247
  145.3 2.1 line.1
  147.4 0.0 all-gather.7.cloned.1.call-update
  147.4 0.1 collective-permute-start.5
  147.5 2.6 collective-permute-done.5.other_ref
  150.1 8.3 %key_value.1 = (bf16[128,4096]{1,0:T(8,128)(2,1)}, bf16[128,4096]{1,0:T(8,128)(2,1)}, bf16[8,4,128,256]{3,2,1,0:T(8,128)(2,1)}) custom-call(s32[3]{0:T(128)S(1)} %pad_add_fusion.here_ref, s32[32]{0:T(128)S(1)} %all-reduce.exp_ref, bf16[128,4096]{1,0:T(8,128)(2,1)} %bitcast.28, bf16[128,4096]{1,0:T(8,128)(2,1)} %bitcast.32, ...), custom_call_target="tpu_custom_call" | custom-call | tf_op jit(solution)/shard_map/key_value/pallas_call | solution.py:247
  158.5 7.1 %all-to-all-start.2 = ((bf16[32,128,256]{2,1,0:T(8,128)(2,1)}), bf16[32,128,256]{2,1,0:T(8,128)(2,1)S(1)}, u32[]{:S(2)}, u32[]{:S(2)}) async-start(bf16[32,128,256]{2,1,0:T(8,128)(2,1)} %bitcast.37), calls=%async_computation.2 | async-start | bytes 4194304 | tf_op jit(solution)/shard_map/all_to_all | solution.py:230
  165.6 0.0 reduce-scatter.2.cloned.1.call-start
  165.6 0.0 all-gather.5.cloned.1.call-done
  165.7 23.1 %turn.1.turned_ref = bf16[3072,4096]{1,0:T(8,128)(2,1)} custom-call(bf16[4096,3072]{1,0:T(8,128)(2,1)} %bitcast.23, bf16[8,4,128,256]{3,2,1,0:T(8,128)(2,1)} %get-tuple-element.48.after_ref), custom_call_target="tpu_custom_call" | custom-call | tf_op jit(solution)/shard_map/turn/pallas_call | solution.py:247
  188.8 6.8 %all-to-all-done.2 = bf16[32,128,256]{2,1,0:T(8,128)(2,1)S(1)} async-done(((bf16[32,128,256]{2,1,0:T(8,128)(2,1)}), bf16[32,128,256]{2,1,0:T(8,128)(2,1)S(1)}, u32[]{:S(2)}, u32[]{:S(2)}) %all-to-all-start.2) | async-done | bytes 2097184 | tf_op jit(solution)/shard_map/all_to_all | solution.py:230
  195.6 12.7 %weight.1.after_ref = f32[8,768,128]{2,1,0:T(8,128)} custom-call(bf16[4096,256]{1,0:T(8,128)(2,1)S(1)} %bitcast.22, bf16[3072,4096]{1,0:T(8,128)(2,1)} %turn.1.turned_ref), custom_call_target="tpu_custom_call" | custom-call | tf_op jit(solution)/shard_map/weight/pallas_call | solution.py:247
  208.3 0.0 all-gather.7.cloned.1.call-done
  208.4 6.1 %edge.1.edge_ref = f32[8,128,128]{2,1,0:T(8,128)} custom-call(s32[3]{0:T(128)S(1)} %pad_add_fusion.here_ref, s32[32]{0:T(128)S(1)} %all-reduce.exp_ref, f32[8,9,128,128]{3,2,1,0:T(8,128)} %bitcast.24, f32[8,9,128,128]{3,2,1,0:T(8,128)} %bitcast.25, f32[8,768,128]{2,1,0:T(8,128)} %weight.1.after_ref), custom_call_target="tpu_custom_call" | custom-call | tf_op jit(solution)/shard_map/edge/pallas_call | solution.py:247
  214.4 2.4 chip_state.3
  216.8 12.2 %collective-permute-done.6.other_edge_ref = f32[8,128,128]{2,1,0:T(8,128)S(1)} collective-permute-done((f32[8,128,128]{2,1,0:T(8,128)}, f32[8,128,128]{2,1,0:T(8,128)S(1)}, u32[]{:S(2)}, u32[]{:S(2)}) %collective-permute-start.6) | collective-permute-done | bytes 524320 | tf_op jit(solution)/shard_map/ppermute | solution.py:234
  229.0 5.7 %core_state.3 = (f32[8,2,128,128]{3,2,1,0:T(8,128)}, f32[8,2,128,128]{3,2,1,0:T(8,128)}) custom-call(s32[3]{0:T(128)S(1)} %pad_add_fusion.here_ref, s32[32]{0:T(128)S(1)} %all-reduce.exp_ref, f32[8,128,128]{2,1,0:T(8,128)} %get-tuple-element.50.mine_edge_ref, f32[8,128,128]{2,1,0:T(8,128)S(1)} %collective-permute-done.6.other_edge_ref, ...), custom_call_target="tpu_custom_call" | custom-call | tf_op jit(solution)/shard_map/core_state/pallas_call | solution.py:247
  234.7 2.9 %collective-permute-done.7.other_ref = f32[8,2,128,128]{3,2,1,0:T(8,128)S(1)} collective-permute-done((f32[8,2,128,128]{3,2,1,0:T(8,128)}, f32[8,2,128,128]{3,2,1,0:T(8,128)S(1)}, u32[]{:S(2)}, u32[]{:S(2)}) %collective-permute-start.7) | collective-permute-done | bytes 1048608 | tf_op jit(solution)/shard_map/ppermute | solution.py:234
  237.6 8.1 %query.1 = bf16[128,4096]{1,0:T(8,128)(2,1)} custom-call(s32[3]{0:T(128)S(1)} %pad_add_fusion.here_ref, s32[32]{0:T(128)S(1)} %all-reduce.exp_ref, bf16[128,4096]{1,0:T(8,128)(2,1)} %bitcast.29, bf16[128,4096]{1,0:T(8,128)(2,1)} %bitcast.33, bf16[128,4096]{1,0:T(8,128)(2,1)} %bitcast.36, f32[8,2,128,128]{3,2,1,0:T(8,128)} %get-tuple-element.52.mine_ref, ...), custom_call_target="tpu_custom_call" | custom-call | tf_op jit(solution)/shard_map/query/pallas_call | solution.py:247
  245.7 8.7 %reduce-scatter.2.cloned.1.call-done = f32[1,768,128]{2,1,0:T(8,128)} async-done(((f32[8,768,128]{2,1,0:T(8,128)}), f32[1,768,128]{2,1,0:T(8,128)}) %reduce-scatter.2.cloned.1.call-update) | async-done | bytes 393232 | tf_op jit(solution)/shard_map/reduce_scatter | solution.py:399
  254.4 16.3 %all_to_all.20 = f32[8,96,128]{2,1,0:T(8,128)S(1)} all-to-all(f32[8,96,128]{2,1,0:T(8,128)} %bitcast.43), channel_id=1, replica_groups=mesh['y'=4,'xh'=2,'zh'=4,'zl'=2,'xl'=2,'core'=2] {'y','xh'}, dimensions={0} | all-to-all | bytes 786432 | tf_op jit(solution)/shard_map/all_to_all | solution.py:230
  270.7 0.3 copy.15
  270.9 0.9 reshape.29
  (14 shorter events, 0.0 us)
Async XLA Ops:
  7.2 158.5 %all-gather.5.cloned.1.call-start = ((), (), s32[]{:S(2)}) async-start(), calls=%async_computation.6 | async-start | bytes 25952256 | tf_op jit(solution)/shard_map/all_gather | solution.py:268
  35.8 7.2 %collective-permute-start = (f32[8,2,128,128]{3,2,1,0:T(8,128)}, f32[8,2,128,128]{3,2,1,0:T(8,128)S(1)}, u32[]{:S(2)}, u32[]{:S(2)}) collective-permute-start(f32[8,2,128,128]{3,2,1,0:T(8,128)} %get-tuple-element.33), channel_id=1, source_target_pairs={{0,1},{1,0},{2,3},{3,2},{4,5},{5,4},{6,7},{7,6},{8,9},{9,8},{10,11... | collective-permute-start | bytes 3145736 | tf_op jit(solution)/shard_map/ppermute | solution.py:234
  42.6 29.1 %collective-permute-start.2 = (f32[8,2,128,128]{3,2,1,0:T(8,128)}, f32[8,2,128,128]{3,2,1,0:T(8,128)S(1)}, u32[]{:S(2)}, u32[]{:S(2)}) collective-permute-start(f32[8,2,128,128]{3,2,1,0:T(8,128)} %get-tuple-element.37), channel_id=1, source_target_pairs={{0,1},{1,0},{2,3},{3,2},{4,5},{5,4},{6,7},{7,6},{8,9},{9,8},{10,11... | collective-permute-start | bytes 3145736 | tf_op jit(solution)/shard_map/ppermute | solution.py:234
  48.3 21.4 %collective-permute-start.1 = (f32[8,128,128]{2,1,0:T(8,128)}, f32[8,128,128]{2,1,0:T(8,128)S(1)}, u32[]{:S(2)}, u32[]{:S(2)}) collective-permute-start(f32[8,128,128]{2,1,0:T(8,128)} %get-tuple-element.35), channel_id=1, source_target_pairs={{0,2},{2,0},{1,3},{3,1},{4,6},{6,4},{5,7},{7,5},{8,10},{10,8},{9,1... | collective-permute-start | bytes 1572872 | tf_op jit(solution)/shard_map/ppermute | solution.py:234
  77.0 1.0 copy-start
  78.0 29.9 %all-to-all-start = ((f32[8,128,128]{2,1,0:T(8,128)}), f32[8,128,128]{2,1,0:T(8,128)S(1)}, u32[]{:S(2)}, u32[]{:S(2)}) async-start(f32[8,128,128]{2,1,0:T(8,128)} %quad.1.refs_0_), calls=%async_computation | async-start | bytes 1048576 | tf_op jit(solution)/shard_map/all_to_all | solution.py:230
  83.0 25.0 %collective-permute-start.3 = (f32[8,128,128]{2,1,0:T(8,128)}, f32[8,128,128]{2,1,0:T(8,128)S(1)}, u32[]{:S(2)}, u32[]{:S(2)}) collective-permute-start(f32[8,128,128]{2,1,0:T(8,128)} %get-tuple-element.40), channel_id=1, source_target_pairs={{0,2},{2,0},{1,3},{3,1},{4,6},{6,4},{5,7},{7,5},{8,10},{10,8},{9,1... | collective-permute-start | bytes 1572872 | tf_op jit(solution)/shard_map/ppermute | solution.py:234
  108.8 19.2 %all-to-all-start.1 = ((f32[8,128,128]{2,1,0:T(8,128)}), f32[8,128,128]{2,1,0:T(8,128)S(1)}, u32[]{:S(2)}, u32[]{:S(2)}) async-start(f32[8,128,128]{2,1,0:T(8,128)} %get-tuple-element.41.after_ref), calls=%async_computation.1 | async-start | bytes 1048576 | tf_op jit(solution)/shard_map/all_to_all | solution.py:230
  116.0 92.3 %all-gather.7.cloned.1.call-start = ((), (), s32[]{:S(2)}) async-start(), calls=%async_computation.7 | async-start | bytes 5308416 | tf_op jit(solution)/shard_map/all_gather | solution.py:351
  130.2 9.4 %collective-permute-start.4 = (f32[8,128,128]{2,1,0:T(8,128)}, f32[8,128,128]{2,1,0:T(8,128)S(1)}, u32[]{:S(2)}, u32[]{:S(2)}) collective-permute-start(f32[8,128,128]{2,1,0:T(8,128)} %get-tuple-element.45), channel_id=1, source_target_pairs={{0,2},{2,0},{1,3},{3,1},{4,6},{6,4},{5,7},{7,5},{8,10},{10,8},{9,1... | collective-permute-start | bytes 1572872 | tf_op jit(solution)/shard_map/ppermute | solution.py:234
  145.3 2.1 copy-start.2
  147.4 2.7 collective-permute-start.5
  158.5 37.1 %all-to-all-start.2 = ((bf16[32,128,256]{2,1,0:T(8,128)(2,1)}), bf16[32,128,256]{2,1,0:T(8,128)(2,1)S(1)}, u32[]{:S(2)}, u32[]{:S(2)}) async-start(bf16[32,128,256]{2,1,0:T(8,128)(2,1)} %bitcast.37), calls=%async_computation.2 | async-start | bytes 4194304 | tf_op jit(solution)/shard_map/all_to_all | solution.py:230
  165.6 88.8 %reduce-scatter.2.cloned.1.call-start = ((), (), s32[]{:S(2)}) async-start(), calls=%async_computation.5 | async-start | bytes 3538944 | tf_op jit(solution)/shard_map/reduce_scatter | solution.py:399
  208.4 20.6 %copy-start.1 = (f32[8,2,128,128]{3,2,1,0:T(8,128)S(1)}, f32[8,2,128,128]{3,2,1,0:T(8,128)}, u32[]{:S(2)}) copy-start(f32[8,2,128,128]{3,2,1,0:T(8,128)} %copy-done) | copy-start | bytes 3145732
  216.8 12.2 %collective-permute-start.6 = (f32[8,128,128]{2,1,0:T(8,128)}, f32[8,128,128]{2,1,0:T(8,128)S(1)}, u32[]{:S(2)}, u32[]{:S(2)}) collective-permute-start(f32[8,128,128]{2,1,0:T(8,128)} %get-tuple-element.51), channel_id=1, source_target_pairs={{0,2},{2,0},{1,3},{3,1},{4,6},{6,4},{5,7},{7,5},{8,10},{10,8},{9,1... | collective-permute-start | bytes 1572872 | tf_op jit(solution)/shard_map/ppermute | solution.py:234
  234.7 2.9 %collective-permute-start.7 = (f32[8,2,128,128]{3,2,1,0:T(8,128)}, f32[8,2,128,128]{3,2,1,0:T(8,128)S(1)}, u32[]{:S(2)}, u32[]{:S(2)}) collective-permute-start(f32[8,2,128,128]{3,2,1,0:T(8,128)} %get-tuple-element.53), channel_id=1, source_target_pairs={{0,1},{1,0},{2,3},{3,2},{4,5},{5,4},{6,7},{7,6},{8,9},{9,8},{10,11... | collective-permute-start | bytes 3145736 | tf_op jit(solution)/shard_map/ppermute | solution.py:234
Sparse Core Ops, SparseCore 0:
  10.5 115.4 all-gather.4
  147.5 57.7 all-gather.6
  208.4 45.8 reduce-scatter.1

commit v6 on v5

v6 whole, which is shorter than its diff:
```python
import functools

import jax
import jax.numpy as jnp
from jax import lax
from jax.experimental import pallas as pl
from jax.experimental.pallas import tpu as pltpu
from jax.sharding import Mesh
from jax.sharding import PartitionSpec as P

WIDTH = 128
f32 = jnp.float32
bf16 = jnp.bfloat16
PLANE = ("y", "xh", "xl", "core")
QUAD = ("xl", "core")
LINE = ("zh", "zl")
CHIPS = ("zh", "zl", "xl")
CHAIN = ("zh", "zl", "xl", "core")
OWNERS = ("y", "xh", "zh", "zl")


def log_rate(exponent, length):
    return -(jnp.left_shift(1, exponent).astype(f32)) * (1.0 / length)


def power_of(rate, steps):
    return jnp.exp(jnp.full((1, WIDTH), rate * steps, f32))


def halves(wide):
    high = wide.astype(bf16)
    return high, (wide - high.astype(f32)).astype(bf16)


def dot(left, right, dims):
    return lax.dot_general(left, right, (dims, ((), ())), preferred_element_type=f32)


def groups_of(ref):
    count = ref.shape[0]
    return [(item, pl.program_id(0) * count + item) for item in range(count)]


def update_kernel(here_ref, exp_ref, left_ref, right_ref, *refs, reverse, length):
    keep_ref, send_ref = refs[-2:]
    span = left_ref.shape[0]
    rows = lax.broadcasted_iota(jnp.int32, (span, WIDTH), 0).astype(f32)
    steps = rows if reverse else (span - 1.0) - rows
    for item, group in groups_of(keep_ref):
        for core, out_ref in enumerate((keep_ref, send_ref)):
            for chip in range(2):
                slot = 2 * jnp.bitwise_xor(here_ref[1], chip) + jnp.bitwise_xor(here_ref[2], core)
                rate = log_rate(exp_ref[4 * group + slot], length)
                start = pl.multiple_of((4 * item + slot) * WIDTH, WIDTH)
                lanes = pl.ds(start, WIDTH)
                high, low = halves(left_ref[:, lanes].astype(f32) * jnp.exp(rate * steps))
                right = right_ref[:, lanes]
                out_ref[item, chip] = dot(
                    jnp.concatenate((high, low), 0), jnp.concatenate((right, right), 0),
                    ((0,), (0,)),
                )


def weighed(mine, other, position, reverse, rate, span):
    position = position.astype(f32)
    later = position if reverse else 1.0 - position
    return power_of(rate, span * later) * mine + power_of(rate, span * (1.0 - later)) * other


def chip_kernel(here_ref, exp_ref, mine_ref, other_ref, *refs, reverse, length, span):
    keep_ref, send_ref = refs[-2:]
    for item, group in groups_of(keep_ref):
        for chip, out_ref in enumerate((keep_ref, send_ref)):
            head = 4 * group + 2 * jnp.bitwise_xor(here_ref[1], chip) + here_ref[2]
            out_ref[item] = weighed(
                mine_ref[item, chip], other_ref[item, chip], here_ref[2], reverse,
                log_rate(exp_ref[head], length), span,
            )


def pair_kernel(here_ref, exp_ref, mine_ref, other_ref, out_ref, *, length, span):
    for item, group in groups_of(out_ref):
        for chip in range(2):
            rate = log_rate(exp_ref[4 * group + 2 * chip + here_ref[2]], length)
            out_ref[item, chip] = weighed(
                mine_ref[item, chip], other_ref[item, chip], here_ref[2], True, rate, span
            )


def scan_kernel(own_ref, parts_ref, after_ref, out_ref, grad_ref, *, length, span):
    rate = log_rate(own_ref[0], length)
    decay = power_of(rate, span)
    state = jnp.zeros(grad_ref.shape, f32)
    for group in reversed(range(parts_ref.shape[0])):
        for chip in (1, 0):
            out_ref[group, chip] = state
            state = decay * state + parts_ref[group, chip]
    grad_ref[...] = power_of(rate, 1.0) * state


def line_kernel(
    here_ref, exp_ref, mine_ref, other_ref, after_ref, keep_ref, send_ref, *, length, span
):
    parity = here_ref[0] % 2
    for half, out_ref in enumerate((keep_ref, send_ref)):
        for item in range(out_ref.shape[0]):
            group = 2 * item + jnp.bitwise_xor(parity, half)
            rate = log_rate(exp_ref[4 * group + 2 * here_ref[1] + here_ref[2]], length)
            out_ref[item] = weighed(
                mine_ref[group], other_ref[group], here_ref[1], False, rate, span
            )


def own_rate(here_ref, exp_ref, item, length):
    group = 2 * item + here_ref[0] % 2
    return log_rate(exp_ref[4 * group + 2 * here_ref[1] + here_ref[2]], length)


def line_pair_kernel(
    here_ref, exp_ref, mine_ref, other_ref, first_ref, out_ref, *, length, span
):
    count = mine_ref.shape[0]
    for item in range(count):
        rate = own_rate(here_ref, exp_ref, item, length)
        out_ref[item] = weighed(
            mine_ref[item], other_ref[item], here_ref[0] % 2, False, rate, span
        )
    out_ref[count] = first_ref[...]


def edge_kernel(
    here_ref, exp_ref, parts_ref, mine_ref, other_ref, after_ref, keep_ref, send_ref,
    *, length, span
):
    count = mine_ref.shape[0]
    behind = here_ref[0] % 2 == 1
    for item in range(count):
        rate = own_rate(here_ref, exp_ref, item, length)
        decay = power_of(rate, 2.0 * span)
        state = parts_ref[item, count]
        for before in range(count - 1):
            update = decay * state + parts_ref[before, item]
            state = jnp.where(here_ref[0] // 2 > before, update, state)
        past = power_of(rate, span) * state
        keep_ref[item] = jnp.where(behind, past + other_ref[item], state)
        send_ref[item] = jnp.where(behind, state, past + mine_ref[item])


def chip_state_kernel(
    here_ref, exp_ref, mine_edge_ref, other_edge_ref, mine_ref, other_ref, keep_ref, send_ref,
    *, length, span
):
    behind = here_ref[1] == 1
    for group in range(keep_ref.shape[0]):
        rate = log_rate(exp_ref[4 * group + 2 * here_ref[1] + here_ref[2]], length)
        edge = jnp.where(
            here_ref[0] % 2 == group % 2, mine_edge_ref[group // 2], other_edge_ref[group // 2]
        )
        past = power_of(rate, span) * edge
        keep_ref[group] = jnp.where(behind, past + other_ref[group], edge)
        send_ref[group] = jnp.where(behind, edge, past + mine_ref[group])


def core_state_kernel(here_ref, exp_ref, mine_ref, other_ref, *refs, reverse, count, length, span):
    edge_refs, (keep_ref, send_ref) = refs[:count], refs[-2:]
    behind = here_ref[2] == (0 if reverse else 1)
    for item, group in groups_of(keep_ref):
        for chip in range(2):
            head = 4 * group + 2 * jnp.bitwise_xor(here_ref[1], chip) + here_ref[2]
            rate = log_rate(exp_ref[head], length)
            edge = edge_refs[0][item, chip] if count == 1 else edge_refs[chip][item]
            past = power_of(rate, span) * edge
            keep_ref[item, chip] = jnp.where(behind, past + other_ref[item, chip], edge)
            send_ref[item, chip] = jnp.where(behind, edge, past + mine_ref[item, chip])


def picked(here_ref, mine_ref, other_ref, item, slot):
    chip = jnp.bitwise_xor(here_ref[1], slot // 2)
    return jnp.where(here_ref[2] == slot % 2, mine_ref[item, chip], other_ref[item, chip])


def heads_of(ref):
    count = ref.shape[1] // (4 * WIDTH)
    first = pl.program_id(0) * count
    return [
        (item, slot, 4 * (first + item) + slot, pl.ds((4 * item + slot) * WIDTH, WIDTH))
        for item in range(count)
        for slot in range(4)
    ]


def inner_kernel(
    exp_ref, query_ref, key_ref, value_ref, grad_ref, after_ref, gk_ref, gv_ref, *, length
):
    span = query_ref.shape[0]
    source = lax.broadcasted_iota(jnp.int32, (span, span), 0)
    target = lax.broadcasted_iota(jnp.int32, (span, span), 1)
    gap = (target - source).astype(f32)
    for item, slot, head, lanes in heads_of(query_ref):
        rate = log_rate(exp_ref[head], length)
        query, key = query_ref[:, lanes], key_ref[:, lanes]
        value, grad = value_ref[:, lanes], grad_ref[:, lanes]
        mask = jnp.where(gap >= 0.0, jnp.exp(rate * jnp.maximum(gap, 0.0)), 0.0)
        grad_scores = jnp.concatenate(halves(dot(value, grad, ((1,), (1,))) * mask), 1)
        key_scores = jnp.concatenate(halves(dot(key, query, ((1,), (1,))) * mask), 1)
        gk_ref[:, lanes] = dot(grad_scores, jnp.concatenate((query, query), 0), ((1,), (0,)))
        gv_ref[:, lanes] = dot(key_scores, jnp.concatenate((grad, grad), 0), ((1,), (0,)))


def key_value_kernel(
    here_ref, exp_ref, key_ref, value_ref, inner_gk_ref, inner_gv_ref, mine_ref, other_ref,
    gk_ref, gv_ref, send_ref, *, length
):
    span = key_ref.shape[0]
    left = span - lax.broadcasted_iota(jnp.int32, (span, WIDTH), 0).astype(f32)
    for item, slot, head, lanes in heads_of(key_ref):
        rate = log_rate(exp_ref[head], length)
        key, value = key_ref[:, lanes], value_ref[:, lanes]
        tail = jnp.exp(rate * left)
        high, low = halves(picked(here_ref, mine_ref, other_ref, item, slot))
        gk = inner_gk_ref[:, lanes] + tail * dot(
            jnp.concatenate((value, value), 1), jnp.concatenate((high, low), 1), ((1,), (1,))
        )
        gv = inner_gv_ref[:, lanes] + tail * dot(
            jnp.concatenate((key, key), 1), jnp.concatenate((high, low), 0), ((1,), (0,))
        )
        gk_ref[:, lanes] = gk.astype(bf16)
        gv_ref[:, lanes] = gv.astype(bf16)
        send_ref[slot, item] = gk.astype(bf16)
        send_ref[4 + slot, item] = gv.astype(bf16)


def query_kernel(
    here_ref, exp_ref, key_ref, value_ref, grad_ref, mine_ref, other_ref, gq_ref, *, length
):
    span = key_ref.shape[0]
    target = lax.broadcasted_iota(jnp.int32, (span, span), 0)
    source = lax.broadcasted_iota(jnp.int32, (span, span), 1)
    gap = (target - source).astype(f32)
    done = 1.0 + lax.broadcasted_iota(jnp.int32, (span, WIDTH), 0).astype(f32)
    for item, slot, head, lanes in heads_of(key_ref):
        rate = log_rate(exp_ref[head], length)
        key, value, grad = key_ref[:, lanes], value_ref[:, lanes], grad_ref[:, lanes]
        mask = jnp.where(gap >= 0.0, jnp.exp(rate * jnp.maximum(gap, 0.0)), 0.0)
        scores = jnp.concatenate(halves(dot(grad, value, ((1,), (1,))) * mask), 1)
        high, low = halves(picked(here_ref, mine_ref, other_ref, item, slot))
        gq = jnp.exp(rate * done) * dot(
            jnp.concatenate((grad, grad), 1), jnp.concatenate((high, low), 1), ((1,), (1,))
        )
        gq = gq + dot(scores, jnp.concatenate((key, key), 0), ((1,), (0,)))
        gq_ref[:, lanes] = gq.astype(bf16)


def weight_kernel(cols_ref, rows_ref, out_ref, turned):
    @pl.when(pl.program_id(0) == 0)
    def _():
        turned[...] = cols_ref[...].T

    product = dot(turned[...], rows_ref[...], ((1,), (0,))).T.astype(bf16)
    count = out_ref.shape[2]
    for item in range(out_ref.shape[0]):
        rows = product[item * count : (item + 1) * count]
        out_ref[item, 0] = rows[:, :WIDTH]
        out_ref[item, 1] = rows[:, WIDTH:]


def total_kernel(parts_ref, out_ref):
    for owner in range(parts_ref.shape[0]):
        total = parts_ref[owner, 0].astype(f32)
        for item in range(1, parts_ref.shape[1]):
            total = total + parts_ref[owner, item].astype(f32)
        out_ref[0, 0, :, owner * WIDTH : (owner + 1) * WIDTH] = total


SMEM = pl.BlockSpec(memory_space=pltpu.SMEM)
FREE = pl.BlockSpec(memory_space=pl.ANY)


def exchange(array, axes):
    return lax.all_to_all(array, axes, split_axis=0, concat_axis=0, tiled=True)


def swap(array, axis):
    return lax.ppermute(array, axis, [(0, 1), (1, 0)])


def far(array):
    return pltpu.with_memory_space_constraint(array, pltpu.HBM)


def call(kernel, grid, in_specs, out_specs, out_shape, args, scratch=(), name=None, vmem=24):
    return pl.pallas_call(
        kernel,
        grid=grid,
        in_specs=in_specs,
        out_specs=out_specs,
        out_shape=out_shape,
        scratch_shapes=scratch,
        name=name,
        compiler_params=pltpu.CompilerParams(vmem_limit_bytes=vmem * 1024 * 1024),
    )(*args)


def per_device(inputs_x, queries, keys, values, grad_out, decay_exp, state_in):
    span = queries.shape[1]
    features = queries.shape[2]
    groups = features // (4 * WIDTH)
    length = span * lax.axis_size(CHAIN)
    tile = (WIDTH, WIDTH)
    query, key, value, grad = queries[0], keys[0], values[0], grad_out[0]
    exps = lax.all_gather(decay_exp, CHAIN, axis=0, tiled=True)
    here = jnp.stack([lax.axis_index(axis) for axis in (LINE, "xl", "core")]).astype(jnp.int32)
    rows = lax.all_gather(inputs_x[0], PLANE, axis=0, tiled=True)

    head_cols = pl.BlockSpec((span, features // 2), lambda i: (0, i))
    pair_tiles = pl.BlockSpec((groups // 2, 2) + tile, lambda i: (i, 0, 0, 0))
    line_tile = pl.BlockSpec((groups // 2,) + tile, lambda i: (i, 0, 0))
    line = pl.BlockSpec((groups,) + tile, lambda i: (0, 0, 0))
    single = pl.BlockSpec(tile, lambda i: (0, 0))
    pair_kept, pair_sent = pltpu.HBM((groups, 2) + tile, f32), pltpu.HBM((groups, 2) + tile, f32)
    line_kept, line_sent = pltpu.HBM((groups,) + tile, f32), pltpu.HBM((groups,) + tile, f32)
    tile_shape = pltpu.HBM(tile, f32)
    token_shape = pltpu.HBM((span, features), bf16)

    arrived = []

    def noted(array):
        arrived.append(array)
        return array

    def run(body, grid, in_specs, out_specs, out_shape, args, after=None, name=None, **sizes):
        if after is not None:
            in_specs, args = in_specs + [FREE], args + (after,)
        args = [
            arg
            if spec is SMEM or any(arg is item for item in arrived)
            else far(arg)
            for spec, arg in zip(in_specs, args)
        ]
        return call(
            functools.partial(body, length=length, **sizes), grid, in_specs, out_specs, out_shape,
            args, name=name,
        )

    def updates(left, right, where, reverse, after=None):
        return run(
            update_kernel, (2,), [SMEM, SMEM, head_cols, head_cols], [pair_tiles, pair_tiles],
            [pair_kept, pair_sent], (where, exps, left, right), after,
            reverse=reverse, name="updates",
        )

    def chip(mine, other, reverse, after=None):
        return run(
            chip_kernel, (2,), [SMEM, SMEM, pair_tiles, pair_tiles], [line_tile, line_tile],
            [line_kept, line_sent], (here, exps, mine, other), after,
            reverse=reverse, span=float(span), name="chip",
        )

    def core_state(edges, mine, other, where, reverse, after=None):
        specs = [pair_tiles] if len(edges) == 1 else [line_tile, line_tile]
        return run(
            core_state_kernel, (2,), [SMEM, SMEM, pair_tiles, pair_tiles] + specs,
            [pair_tiles, pair_tiles], [pair_kept, pair_sent],
            (where, exps, mine, other, *edges), after,
            reverse=reverse, count=len(edges), span=float(span), name="core_state",
        )

    inner_shape = pltpu.HBM((span, features), f32)
    even = here * jnp.array([1, 0, 1], jnp.int32)
    r_mine, sent = updates(query, grad, even, True)
    r_other = noted(swap(sent, "core"))
    r_pair = run(
        pair_kernel, (2,), [SMEM, SMEM, pair_tiles, pair_tiles], pair_tiles, pair_sent,
        (here, exps, r_mine, r_other), span=float(span), name="pair",
    )
    f_mine, sent = updates(key, value, here, False, r_mine)
    f_other = noted(swap(sent, "core"))
    r_parts = exchange(r_pair.reshape((2 * groups,) + tile), CHIPS)
    r_parts = noted(r_parts.reshape((groups, 2) + tile))
    f_chip, sent = chip(f_mine, f_other, False, r_pair)
    f_next = noted(swap(sent, "xl"))
    all_pairs = pl.BlockSpec((groups, 2) + tile, lambda i: (0, 0, 0, 0))
    r_edges, state_grad = run(
        scan_kernel, (1,), [SMEM, all_pairs], [all_pairs, single], [pair_sent, tile_shape],
        (decay_exp, r_parts), f_chip, span=2.0 * span, name="scan",
    )
    inner_gk, inner_gv = run(
        inner_kernel, (2,), [SMEM] + 4 * [head_cols], 2 * [head_cols], 2 * [inner_shape],
        (exps, query, key, value, grad), r_edges, name="inner",
    )
    r_edges = exchange(r_edges.reshape((2 * groups,) + tile), CHIPS)
    r_edges = noted(r_edges.reshape((groups, 2) + tile))
    mine, sent = core_state([r_edges], r_mine, r_other, even, True, inner_gk)
    other = noted(swap(sent, "core"))
    quarter = pl.BlockSpec((4,) + tile, lambda i: (0, 0, 0))
    quarter_shape = pltpu.HBM((4,) + tile, f32)
    f_line, sent = run(
        line_kernel, (1,), [SMEM, SMEM, line, line], [quarter, quarter],
        [quarter_shape, quarter_shape], (here, exps, f_chip, f_next), mine,
        span=2.0 * span, name="line",
    )
    f_beside = noted(swap(sent, "zl"))
    f_parts = lax.all_gather(run(
        line_pair_kernel, (1,), [SMEM, SMEM, quarter, quarter, single],
        pl.BlockSpec((5,) + tile, lambda i: (0, 0, 0)), pltpu.HBM((5,) + tile, f32),
        (here, exps, f_line, f_beside, state_in[0, 0]), span=4.0 * span, name="line_pair",
    ), "zh")
    grad_key, grad_value, send = run(
        key_value_kernel, (2,), [SMEM, SMEM] + 4 * [head_cols] + 2 * [pair_tiles],
        [head_cols, head_cols, pl.BlockSpec((8, 4, span, WIDTH), lambda i: (0, 0, 0, i))],
        [token_shape, token_shape, pltpu.HBM((8, 4, span, 2 * WIDTH), bf16)],
        (even, exps, key, value, inner_gk, inner_gv, mine, other), name="key_value",
    )
    cols = exchange(send.reshape(32, span, 2 * WIDTH), PLANE)
    cols = cols.reshape(32 * span, 2 * WIDTH)

    tokens, width = rows.shape
    block = width // 4
    partial = call(
        weight_kernel, (4,),
        [
            pl.BlockSpec((tokens, 2 * WIDTH), lambda i: (0, 0)),
            pl.BlockSpec((tokens, block), lambda i: (0, i)),
        ],
        pl.BlockSpec((8, 2, block // 8, WIDTH), lambda i: (0, i, 0, 0)),
        pltpu.HBM((8, 8, block // 8, WIDTH), bf16), (cols, far(rows)), scratch=[pltpu.VMEM((2 * WIDTH, tokens), bf16)], name="weight", vmem=40,
    )
    f_edge, sent = run(
        edge_kernel, (1,),
        [SMEM, SMEM, pl.BlockSpec((4, 5) + tile, lambda i: (0, 0, 0, 0)), quarter, quarter],
        [quarter, quarter], [quarter_shape, quarter_shape],
        (here, exps, f_parts, f_line, f_beside), partial, span=4.0 * span, name="edge",
    )
    f_side = noted(swap(sent, "zl"))
    f_edge, sent = run(
        chip_state_kernel, (1,), [SMEM, SMEM, quarter, quarter, line, line], [line, line],
        [line_kept, line_sent], (here, exps, f_edge, f_side, f_chip, f_next),
        span=2.0 * span, name="chip_state",
    )
    f_far = noted(swap(sent, "xl"))
    mine, sent = core_state([f_edge, f_far], f_mine, f_other, here, False)
    other = noted(swap(sent, "core"))
    grad_query = run(
        query_kernel, (2,), [SMEM, SMEM] + 3 * [head_cols] + 2 * [pair_tiles], head_cols,
        token_shape, (here, exps, key, value, grad, mine, other), name="query",
    )
    share = block // 8
    pieces = exchange(partial.reshape(64, share, WIDTH), OWNERS).reshape(8, 8, share, WIDTH)
    weight_grads = call(
        total_kernel, (2,), [pl.BlockSpec((4, 8, share, WIDTH), lambda i: (i, 0, 0, 0))],
        pl.BlockSpec((1, 1, share, 4 * WIDTH), lambda i: (i, 0, 0, 0)),
        pltpu.HBM((2, 1, share, 4 * WIDTH), f32), (pieces,), name="total",
    )
    return (
        grad_query[None], grad_key[None], grad_value[None], weight_grads, state_grad[None, None]
    )


def solution(mesh):
    fine = Mesh(mesh.devices.reshape(4, 2, 4, 2, 2, 2), ("y", "xh", "zh", "zl", "xl", "core"))
    dp, seq = ("y", "xh"), CHAIN
    tokens = P(dp, seq, None)
    in_specs = (tokens, tokens, tokens, tokens, tokens, P(seq), P(dp, seq, None, None))
    out_specs = (tokens, tokens, tokens, P(None, seq, dp, None), P(dp, seq, None, None))
    return jax.shard_map(
        per_device, mesh=fine, in_specs=in_specs, out_specs=out_specs, check_vma=False
    )
```

time: 281 us -> 288 us (1.025)
  waiting for transfers between devices: 88.1 us -> 152 us
  Pallas kernels: 114 us -> 59.3 us
  blocking collectives: 34.8 us -> 18.5 us
  starting transfers between devices: 23.2 us -> 37.7 us
    pallas_call x17 -> x16, Pallas kernels: 114 us -> 59.3 us  [call(): pl.pallas_call(kernel, grid=grid, in_specs=in_specs, out_specs=out_specs,...]
    all_gather x1, waiting for transfers between devices: 0.02 us -> 26.7 us  [per_device(): lax.all_gather(run(line_pair_kernel, (1,), [SMEM, SMEM, quarter, quarter,...]
    all_to_all x3 -> x4, waiting for transfers between devices: 8.45 us -> 33.3 us  [exchange(): return lax.all_to_all(array, axes, split_axis=0, concat_axis=0, tiled=True)]
    ppermute x8, waiting for transfers between devices: 70.2 us -> 91.2 us  [swap(): return lax.ppermute(array, axis, [(0, 1), (1, 0)])]
    all_to_all x1 -> x0, blocking collectives: 16.3 us -> none  [exchange(): return lax.all_to_all(array, axes, split_axis=0, concat_axis=0, tiled=True)]
    all_to_all x3 -> x4, starting transfers between devices: 19.3 us -> 31.4 us  [exchange(): return lax.all_to_all(array, axes, split_axis=0, concat_axis=0, tiled=True)]
    reduce_scatter x1 -> x0, waiting for transfers between devices: 8.7 us -> none  [per_device(): summed = lax.psum_scatter(partial, LINE, scatter_dimension=0, tiled=True)]
  transfers between devices with their start and end apart: 14 -> 14, of which waited for: 9 -> 11; matrix products, arithmetic and copies ran while one was open for 1% -> 1% of each run, Pallas kernels for 41% -> 20%
where the time goes in v6:
time: 288 us; the launch traced here: 286 us
  waiting for transfers between devices  152 us (53%)
  Pallas kernels  59.3 us (21%)
  starting transfers between devices  37.7 us (13%)
  blocking collectives  18.5 us (6%)
  between operations  14.8 us (5%)
    ppermute x8, waiting for transfers between devices, swap(): return lax.ppermute(array, axis, [(0, 1), (1, 0)])  91.2 us
    pallas_call x16, Pallas kernels, call(): pl.pallas_call(kernel, grid=grid, in_specs=in_specs, out_specs=out_specs,...  59.3 us
    all_to_all x4, waiting for transfers between devices, exchange(): return lax.all_to_all(array, axes, split_axis=0, concat_axis=0, tiled=True)  33.3 us
    all_to_all x4, starting transfers between devices, exchange(): return lax.all_to_all(array, axes, split_axis=0, concat_axis=0, tiled=True)  31.4 us
    all_gather x1, waiting for transfers between devices, per_device(): lax.all_gather(run(line_pair_kernel, (1,), [SMEM, SMEM, quarter, quarter,...  26.7 us
    unnamed x1, blocking collectives  18.5 us
    ppermute x8, starting transfers between devices, swap(): return lax.ppermute(array, axis, [(0, 1), (1, 0)])  6.3 us
  transfers between devices with their start and end apart: 14, of which 11 were waited for; matrix products, arithmetic and copies ran while one was open for 1% of the time, Pallas kernels for 20%

profile of v6, /device:TPU:32, one launch (start us, length us, event | category | flops | bytes accessed | tf_op | source)
XLA Modules:
  0.0 285.7 jit_solution(3705596317480232122)
XLA Ops:
  7.2 0.0 all-gather.7.cloned.1.call-start
  7.2 0.7 all-gather.7.cloned.1.call-update
  8.6 1.3 dynamic-slice
  9.8 0.8 dynamic-update-slice
  10.6 18.5 %all-reduce.exp_ref = s32[32]{0:T(128)S(1)} all-reduce(s32[32]{0:T(128)S(1)} %dynamic-update-slice), channel_id=1, replica_groups=mesh['y'=4,'xh'=2,'zh'=4,'zl'=2,'xl'=2,'core'=2] {'zh','zl','xl','core'}, use_global_device_ids=true, to_apply=%add | all-reduce | flops 32 | bytes 256
  29.0 0.7 fusion
  29.8 3.4 %updates.2 = (f32[8,2,128,128]{3,2,1,0:T(8,128)}, f32[8,2,128,128]{3,2,1,0:T(8,128)}) custom-call(s32[3]{0:T(128)S(1)} %get-tuple-element.51.here_ref, s32[32]{0:T(128)S(1)} %all-reduce.exp_ref, bf16[128,4096]{1,0:T(8,128)(2,1)} %bitcast.42, bf16[128,4096]{1,0:T(8,128)(2,1)} %bitcast.38), custom_call_target="tpu_custom_call" | custom-call | tf_op jit(solution)/shard_map/updates/pallas_call | solution.py:292
  33.2 0.0 collective-permute-start.1
  33.2 2.9 %collective-permute-done.1.other_ref = f32[8,2,128,128]{3,2,1,0:T(8,128)S(1)} collective-permute-done((f32[8,2,128,128]{3,2,1,0:T(8,128)}, f32[8,2,128,128]{3,2,1,0:T(8,128)S(1)}, u32[]{:S(2)}, u32[]{:S(2)}) %collective-permute-start.1) | collective-permute-done | bytes 1048608 | tf_op jit(solution)/shard_map/ppermute | solution.py:284
  36.0 2.1 pair.1.refs_0_
  38.1 4.5 %all-to-all-start = ((f32[16,128,128]{2,1,0:T(8,128)}), f32[16,128,128]{2,1,0:T(8,128)S(1)}, u32[]{:S(2)}, u32[]{:S(2)}) async-start(f32[16,128,128]{2,1,0:T(8,128)} %bitcast.37), calls=%async_computation | async-start | bytes 2097152 | tf_op jit(solution)/shard_map/all_to_all | solution.py:280
  42.7 3.4 %updates.3 = (f32[8,2,128,128]{3,2,1,0:T(8,128)}, f32[8,2,128,128]{3,2,1,0:T(8,128)}) custom-call(s32[3]{0:T(128)S(1)} %get-tuple-element.52.here_ref, s32[32]{0:T(128)S(1)} %all-reduce.exp_ref, bf16[128,4096]{1,0:T(8,128)(2,1)} %bitcast.28, bf16[128,4096]{1,0:T(8,128)(2,1)} %bitcast.32, f32[8,2,128,128]{3,2,1,0:T(8,128)} %get-tuple-element.28.refs_0_.mine_ref), custom_call_target="tpu_custom_call" | custom-call | tf_op jit(solution)/shard_map/updates/pallas_call | solution.py:292
  46.0 0.0 collective-permute-start
  46.0 2.9 %collective-permute-done.other_ref = f32[8,2,128,128]{3,2,1,0:T(8,128)S(1)} collective-permute-done((f32[8,2,128,128]{3,2,1,0:T(8,128)}, f32[8,2,128,128]{3,2,1,0:T(8,128)S(1)}, u32[]{:S(2)}, u32[]{:S(2)}) %collective-permute-start) | collective-permute-done | bytes 1048608 | tf_op jit(solution)/shard_map/ppermute | solution.py:284
  48.9 2.1 chip.1
  51.0 17.5 %all-to-all-done = f32[16,128,128]{2,1,0:T(8,128)S(1)} async-done(((f32[16,128,128]{2,1,0:T(8,128)}), f32[16,128,128]{2,1,0:T(8,128)S(1)}, u32[]{:S(2)}, u32[]{:S(2)}) %all-to-all-start) | async-done | bytes 1048608 | tf_op jit(solution)/shard_map/all_to_all | solution.py:280
  68.5 1.1 scan.1
  69.6 7.2 %all-to-all-start.1 = ((f32[16,128,128]{2,1,0:T(8,128)}), f32[16,128,128]{2,1,0:T(8,128)S(1)}, u32[]{:S(2)}, u32[]{:S(2)}) async-start(f32[16,128,128]{2,1,0:T(8,128)} %bitcast.41), calls=%async_computation.1 | async-start | bytes 2097152 | tf_op jit(solution)/shard_map/all_to_all | solution.py:280
  76.8 8.8 %inner.1 = (f32[128,4096]{1,0:T(8,128)}, f32[128,4096]{1,0:T(8,128)}) custom-call(s32[32]{0:T(128)S(1)} %all-reduce.exp_ref, bf16[128,4096]{1,0:T(8,128)(2,1)} %bitcast.43, bf16[128,4096]{1,0:T(8,128)(2,1)} %bitcast.29, bf16[128,4096]{1,0:T(8,128)(2,1)} %bitcast.33, bf16[128,4096]{1,0:T(8,128)(2,1)} %bitcast.39, f32[8,2,128,128]{3,2,1,0:T(8,128)} %get-tuple-element.34.after_ref), custom_call_target="tpu_custom_call" | custom-call | tf_op jit(solution)/shard_map/inner/pallas_call | solution.py:292
  85.5 15.8 %all-to-all-done.1 = f32[16,128,128]{2,1,0:T(8,128)S(1)} async-done(((f32[16,128,128]{2,1,0:T(8,128)}), f32[16,128,128]{2,1,0:T(8,128)S(1)}, u32[]{:S(2)}, u32[]{:S(2)}) %all-to-all-start.1) | async-done | bytes 1048608 | tf_op jit(solution)/shard_map/all_to_all | solution.py:280
  101.4 2.5 core_state.2
  103.9 2.9 %collective-permute-done.4.other_ref = f32[8,2,128,128]{3,2,1,0:T(8,128)S(1)} collective-permute-done((f32[8,2,128,128]{3,2,1,0:T(8,128)}, f32[8,2,128,128]{3,2,1,0:T(8,128)S(1)}, u32[]{:S(2)}, u32[]{:S(2)}) %collective-permute-start.4) | collective-permute-done | bytes 1048608 | tf_op jit(solution)/shard_map/ppermute | solution.py:284
  106.7 5.4 %key_value.1 = (bf16[128,4096]{1,0:T(8,128)(2,1)}, bf16[128,4096]{1,0:T(8,128)(2,1)}, bf16[8,4,128,256]{3,2,1,0:T(8,128)(2,1)}) custom-call(s32[3]{0:T(128)S(1)} %get-tuple-element.51.here_ref, s32[32]{0:T(128)S(1)} %all-reduce.exp_ref, bf16[128,4096]{1,0:T(8,128)(2,1)} %bitcast.30, bf16[128,4096]{1,0:T(8,128)(2,1)} %bitcast.34, ...), custom_call_target="tpu_custom_call" | custom-call | tf_op jit(solution)/shard_map/key_value/pallas_call | solution.py:292
  112.1 7.1 %all-to-all-start.2 = ((bf16[32,128,256]{2,1,0:T(8,128)(2,1)}), bf16[32,128,256]{2,1,0:T(8,128)(2,1)S(1)}, u32[]{:S(2)}, u32[]{:S(2)}) async-start(bf16[32,128,256]{2,1,0:T(8,128)(2,1)} %bitcast.44), calls=%async_computation.2 | async-start | bytes 4194304 | tf_op jit(solution)/shard_map/all_to_all | solution.py:280
  119.2 0.0 all-gather.5.cloned.1.call-start
  119.2 1.9 collective-permute-start.2
  121.1 39.0 %collective-permute-done.2.other_ref = f32[8,128,128]{2,1,0:T(8,128)S(1)} collective-permute-done((f32[8,128,128]{2,1,0:T(8,128)}, f32[8,128,128]{2,1,0:T(8,128)S(1)}, u32[]{:S(2)}, u32[]{:S(2)}) %collective-permute-start.2) | collective-permute-done | bytes 524320 | tf_op jit(solution)/shard_map/ppermute | solution.py:284
  160.2 1.9 line.1
  162.1 0.8 copy-done
  162.8 1.1 collective-permute-start.3
  164.0 7.2 %collective-permute-done.3.other_ref = f32[4,128,128]{2,1,0:T(8,128)S(1)} collective-permute-done((f32[4,128,128]{2,1,0:T(8,128)}, f32[4,128,128]{2,1,0:T(8,128)S(1)}, u32[]{:S(2)}, u32[]{:S(2)}) %collective-permute-start.3) | collective-permute-done | bytes 262176 | tf_op jit(solution)/shard_map/ppermute | solution.py:284
  171.2 1.7 line_pair.1
  172.9 0.0 all-gather.5.cloned.1.call-update
  173.0 0.0 all-gather.7.cloned.1.call-done
  173.0 13.1 %weight.1.after_ref = bf16[8,8,96,128]{3,2,1,0:T(8,128)(2,1)} custom-call(bf16[4096,256]{1,0:T(8,128)(2,1)S(1)} %bitcast.23, bf16[4096,3072]{1,0:T(8,128)(2,1)} %bitcast.27), custom_call_target="tpu_custom_call" | custom-call | tf_op jit(solution)/shard_map/weight/pallas_call | solution.py:292
  186.1 12.6 %all-to-all-start.3 = ((bf16[64,96,128]{2,1,0:T(8,128)(2,1)}), bf16[64,96,128]{2,1,0:T(8,128)(2,1)S(1)}, u32[]{:S(2)}, u32[]{:S(2)}) async-start(bf16[64,96,128]{2,1,0:T(8,128)(2,1)} %bitcast.36), calls=%async_computation.3 | async-start | bytes 3145728 | tf_op jit(solution)/shard_map/all_to_all | solution.py:280
  198.7 0.0 copy-start.1
  198.7 26.7 %all-gather.5.cloned.1.call-done = f32[20,128,128]{2,1,0:T(8,128)} async-done(((f32[5,128,128]{2,1,0:T(8,128)}), f32[20,128,128]{2,1,0:T(8,128)}) %all-gather.5.cloned.1.call-update) | async-done | bytes 1310736 | tf_op jit(solution)/shard_map/all_gather | solution.py:403
  225.4 2.3 edge.1
  227.8 1.8 collective-permute-start.5
  229.6 20.9 %collective-permute-done.5.other_edge_ref = f32[4,128,128]{2,1,0:T(8,128)S(1)} collective-permute-done((f32[4,128,128]{2,1,0:T(8,128)}, f32[4,128,128]{2,1,0:T(8,128)S(1)}, u32[]{:S(2)}, u32[]{:S(2)}) %collective-permute-start.5) | collective-permute-done | bytes 262176 | tf_op jit(solution)/shard_map/ppermute | solution.py:284
  250.5 2.2 chip_state.1
  252.7 1.5 collective-permute-start.6
  254.2 12.5 %collective-permute-done.6.refs_1_ = f32[8,128,128]{2,1,0:T(8,128)S(1)} collective-permute-done((f32[8,128,128]{2,1,0:T(8,128)}, f32[8,128,128]{2,1,0:T(8,128)S(1)}, u32[]{:S(2)}, u32[]{:S(2)}) %collective-permute-start.6) | collective-permute-done | bytes 524320 | tf_op jit(solution)/shard_map/ppermute | solution.py:284
  266.7 2.6 core_state.3
  269.3 2.9 %collective-permute-done.7.other_ref = f32[8,2,128,128]{3,2,1,0:T(8,128)S(1)} collective-permute-done((f32[8,2,128,128]{3,2,1,0:T(8,128)}, f32[8,2,128,128]{3,2,1,0:T(8,128)S(1)}, u32[]{:S(2)}, u32[]{:S(2)}) %collective-permute-start.7) | collective-permute-done | bytes 1048608 | tf_op jit(solution)/shard_map/ppermute | solution.py:284
  272.1 5.8 %query.1 = bf16[128,4096]{1,0:T(8,128)(2,1)} custom-call(s32[3]{0:T(128)S(1)} %get-tuple-element.52.here_ref, s32[32]{0:T(128)S(1)} %all-reduce.exp_ref, bf16[128,4096]{1,0:T(8,128)(2,1)} %bitcast.31, bf16[128,4096]{1,0:T(8,128)(2,1)} %bitcast.35, bf16[128,4096]{1,0:T(8,128)(2,1)} %bitcast.40, f32[8,2,128,128]{3,2,1,0:T(8,128)} %get-tuple-element.46.mine_ref, ...), custom_call_target="tpu_custom_call" | custom-call | tf_op jit(solution)/shard_map/query/pallas_call | solution.py:292
  278.0 0.9 total.1
  (7 shorter events, 0.0 us)
Async XLA Ops:
  7.2 165.8 %all-gather.7.cloned.1.call-start = ((), (), s32[]{:S(2)}) async-start(), calls=%async_computation.5 | async-start | bytes 25952256 | tf_op jit(solution)/shard_map/all_gather | solution.py:313
  33.2 2.9 %collective-permute-start.1 = (f32[8,2,128,128]{3,2,1,0:T(8,128)}, f32[8,2,128,128]{3,2,1,0:T(8,128)S(1)}, u32[]{:S(2)}, u32[]{:S(2)}) collective-permute-start(f32[8,2,128,128]{3,2,1,0:T(8,128)} %get-tuple-element.31), channel_id=1, source_target_pairs={{0,1},{1,0},{2,3},{3,2},{4,5},{5,4},{6,7},{7,6},{8,9},{9,8},{10,11... | collective-permute-start | bytes 3145736 | tf_op jit(solution)/shard_map/ppermute | solution.py:284
  38.1 30.4 %all-to-all-start = ((f32[16,128,128]{2,1,0:T(8,128)}), f32[16,128,128]{2,1,0:T(8,128)S(1)}, u32[]{:S(2)}, u32[]{:S(2)}) async-start(f32[16,128,128]{2,1,0:T(8,128)} %bitcast.37), calls=%async_computation | async-start | bytes 2097152 | tf_op jit(solution)/shard_map/all_to_all | solution.py:280
  46.0 2.9 %collective-permute-start = (f32[8,2,128,128]{3,2,1,0:T(8,128)}, f32[8,2,128,128]{3,2,1,0:T(8,128)S(1)}, u32[]{:S(2)}, u32[]{:S(2)}) collective-permute-start(f32[8,2,128,128]{3,2,1,0:T(8,128)} %get-tuple-element.30), channel_id=1, source_target_pairs={{0,1},{1,0},{2,3},{3,2},{4,5},{5,4},{6,7},{7,6},{8,9},{9,8},{10,11... | collective-permute-start | bytes 3145736 | tf_op jit(solution)/shard_map/ppermute | solution.py:284
  69.6 31.8 %all-to-all-start.1 = ((f32[16,128,128]{2,1,0:T(8,128)}), f32[16,128,128]{2,1,0:T(8,128)S(1)}, u32[]{:S(2)}, u32[]{:S(2)}) async-start(f32[16,128,128]{2,1,0:T(8,128)} %bitcast.41), calls=%async_computation.1 | async-start | bytes 2097152 | tf_op jit(solution)/shard_map/all_to_all | solution.py:280
  103.8 2.9 %collective-permute-start.4 = (f32[8,2,128,128]{3,2,1,0:T(8,128)}, f32[8,2,128,128]{3,2,1,0:T(8,128)S(1)}, u32[]{:S(2)}, u32[]{:S(2)}) collective-permute-start(f32[8,2,128,128]{3,2,1,0:T(8,128)} %get-tuple-element.40), channel_id=1, source_target_pairs={{0,1},{1,0},{2,3},{3,2},{4,5},{5,4},{6,7},{7,6},{8,9},{9,8},{10,11... | collective-permute-start | bytes 3145736 | tf_op jit(solution)/shard_map/ppermute | solution.py:284
  112.1 60.9 %all-to-all-start.2 = ((bf16[32,128,256]{2,1,0:T(8,128)(2,1)}), bf16[32,128,256]{2,1,0:T(8,128)(2,1)S(1)}, u32[]{:S(2)}, u32[]{:S(2)}) async-start(bf16[32,128,256]{2,1,0:T(8,128)(2,1)} %bitcast.44), calls=%async_computation.2 | async-start | bytes 4194304 | tf_op jit(solution)/shard_map/all_to_all | solution.py:280
  119.2 106.2 %all-gather.5.cloned.1.call-start = ((), (), s32[]{:S(2)}) async-start(), calls=%async_computation.4 | async-start | bytes 1638400 | tf_op jit(solution)/shard_map/all_gather | solution.py:403
  119.2 40.9 %collective-permute-start.2 = (f32[8,128,128]{2,1,0:T(8,128)}, f32[8,128,128]{2,1,0:T(8,128)S(1)}, u32[]{:S(2)}, u32[]{:S(2)}) collective-permute-start(f32[8,128,128]{2,1,0:T(8,128)} %get-tuple-element.33), channel_id=1, source_target_pairs={{0,2},{2,0},{1,3},{3,1},{4,6},{6,4},{5,7},{7,5},{8,10},{10,8},{9,1... | collective-permute-start | bytes 1572872 | tf_op jit(solution)/shard_map/ppermute | solution.py:284
  162.1 0.8 copy-start
  162.8 8.4 %collective-permute-start.3 = (f32[4,128,128]{2,1,0:T(8,128)}, f32[4,128,128]{2,1,0:T(8,128)S(1)}, u32[]{:S(2)}, u32[]{:S(2)}) collective-permute-start(f32[4,128,128]{2,1,0:T(8,128)} %get-tuple-element.38), channel_id=1, source_target_pairs={{0,4},{4,0},{1,5},{5,1},{2,6},{6,2},{3,7},{7,3},{8,12},{12,8},{9,1... | collective-permute-start | bytes 786440 | tf_op jit(solution)/shard_map/ppermute | solution.py:284
  186.1 91.9 %all-to-all-start.3 = ((bf16[64,96,128]{2,1,0:T(8,128)(2,1)}), bf16[64,96,128]{2,1,0:T(8,128)(2,1)S(1)}, u32[]{:S(2)}, u32[]{:S(2)}) async-start(bf16[64,96,128]{2,1,0:T(8,128)(2,1)} %bitcast.36), calls=%async_computation.3 | async-start | bytes 3145728 | tf_op jit(solution)/shard_map/all_to_all | solution.py:280
  198.7 51.8 %copy-start.1 = (f32[8,128,128]{2,1,0:T(8,128)S(1)}, f32[8,128,128]{2,1,0:T(8,128)}, u32[]{:S(2)}) copy-start(f32[8,128,128]{2,1,0:T(8,128)} %copy-done) | copy-start | bytes 1572868
  227.8 22.7 %collective-permute-start.5 = (f32[4,128,128]{2,1,0:T(8,128)}, f32[4,128,128]{2,1,0:T(8,128)S(1)}, u32[]{:S(2)}, u32[]{:S(2)}) collective-permute-start(f32[4,128,128]{2,1,0:T(8,128)} %get-tuple-element.43), channel_id=1, source_target_pairs={{0,4},{4,0},{1,5},{5,1},{2,6},{6,2},{3,7},{7,3},{8,12},{12,8},{9,1... | collective-permute-start | bytes 786440 | tf_op jit(solution)/shard_map/ppermute | solution.py:284
  252.7 14.0 %collective-permute-start.6 = (f32[8,128,128]{2,1,0:T(8,128)}, f32[8,128,128]{2,1,0:T(8,128)S(1)}, u32[]{:S(2)}, u32[]{:S(2)}) collective-permute-start(f32[8,128,128]{2,1,0:T(8,128)} %get-tuple-element.45), channel_id=1, source_target_pairs={{0,2},{2,0},{1,3},{3,1},{4,6},{6,4},{5,7},{7,5},{8,10},{10,8},{9,1... | collective-permute-start | bytes 1572872 | tf_op jit(solution)/shard_map/ppermute | solution.py:284
  269.3 2.9 %collective-permute-start.7 = (f32[8,2,128,128]{3,2,1,0:T(8,128)}, f32[8,2,128,128]{3,2,1,0:T(8,128)S(1)}, u32[]{:S(2)}, u32[]{:S(2)}) collective-permute-start(f32[8,2,128,128]{3,2,1,0:T(8,128)} %get-tuple-element.47), channel_id=1, source_target_pairs={{0,1},{1,0},{2,3},{3,2},{4,5},{5,4},{6,7},{7,6},{8,9},{9,8},{10,11... | collective-permute-start | bytes 3145736 | tf_op jit(solution)/shard_map/ppermute | solution.py:284
Sparse Core Ops, SparseCore 0:
  10.5 121.8 all-gather.6
  173.1 52.2 all-gather.4

commit v7 on v6

--- a/solution.py
+++ b/solution.py
@@ -117,8 +117,9 @@
 
 
 def line_pair_kernel(
-    here_ref, exp_ref, mine_ref, other_ref, first_ref, out_ref, *, length, span
-):
+    here_ref, exp_ref, mine_ref, other_ref, first_ref, *refs, length, span
+):
+    out_ref = refs[-1]
     count = mine_ref.shape[0]
     for item in range(count):
         rate = own_rate(here_ref, exp_ref, item, length)
@@ -382,8 +383,16 @@
     all_pairs = pl.BlockSpec((groups, 2) + tile, lambda i: (0, 0, 0, 0))
     r_edges, state_grad = run(
         scan_kernel, (1,), [SMEM, all_pairs], [all_pairs, single], [pair_sent, tile_shape],
-        (decay_exp, r_parts), f_chip, span=2.0 * span, name="scan",
-    )
+        (decay_exp, r_parts), f_next, span=2.0 * span, name="scan",
+    )
+    quarter = pl.BlockSpec((4,) + tile, lambda i: (0, 0, 0))
+    quarter_shape = pltpu.HBM((4,) + tile, f32)
+    f_line, sent = run(
+        line_kernel, (1,), [SMEM, SMEM, line, line], [quarter, quarter],
+        [quarter_shape, quarter_shape], (here, exps, f_chip, f_next), r_edges,
+        span=2.0 * span, name="line",
+    )
+    f_beside = noted(swap(sent, "zl"))
     inner_gk, inner_gv = run(
         inner_kernel, (2,), [SMEM] + 4 * [head_cols], 2 * [head_cols], 2 * [inner_shape],
         (exps, query, key, value, grad), r_edges, name="inner",
@@ -392,19 +401,6 @@
     r_edges = noted(r_edges.reshape((groups, 2) + tile))
     mine, sent = core_state([r_edges], r_mine, r_other, even, True, inner_gk)
     other = noted(swap(sent, "core"))
-    quarter = pl.BlockSpec((4,) + tile, lambda i: (0, 0, 0))
-    quarter_shape = pltpu.HBM((4,) + tile, f32)
-    f_line, sent = run(
-        line_kernel, (1,), [SMEM, SMEM, line, line], [quarter, quarter],
-        [quarter_shape, quarter_shape], (here, exps, f_chip, f_next), mine,
-        span=2.0 * span, name="line",
-    )
-    f_beside = noted(swap(sent, "zl"))
-    f_parts = lax.all_gather(run(
-        line_pair_kernel, (1,), [SMEM, SMEM, quarter, quarter, single],
-        pl.BlockSpec((5,) + tile, lambda i: (0, 0, 0)), pltpu.HBM((5,) + tile, f32),
-        (here, exps, f_line, f_beside, state_in[0, 0]), span=4.0 * span, name="line_pair",
-    ), "zh")
     grad_key, grad_value, send = run(
         key_value_kernel, (2,), [SMEM, SMEM] + 4 * [head_cols] + 2 * [pair_tiles],
         [head_cols, head_cols, pl.BlockSpec((8, 4, span, WIDTH), lambda i: (0, 0, 0, i))],
@@ -414,6 +410,13 @@
     cols = exchange(send.reshape(32, span, 2 * WIDTH), PLANE)
     cols = cols.reshape(32 * span, 2 * WIDTH)
 
+    f_lines = run(
+        line_pair_kernel, (1,), [SMEM, SMEM, quarter, quarter, single, FREE],
+        pl.BlockSpec((5,) + tile, lambda i: (0, 0, 0)), pltpu.HBM((5,) + tile, f32),
+        (here, exps, f_line, f_beside, state_in[0, 0], rows), send, span=4.0 * span,
+        name="line_pair",
+    )
+    f_parts = lax.all_gather(f_lines, "zh")
     tokens, width = rows.shape
     block = width // 4
     partial = call(
@@ -425,13 +428,14 @@
         pl.BlockSpec((8, 2, block // 8, WIDTH), lambda i: (0, i, 0, 0)),
         pltpu.HBM((8, 8, block // 8, WIDTH), bf16), (cols, far(rows)), scratch=[pltpu.VMEM((2 * WIDTH, tokens), bf16)], name="weight", vmem=40,
     )
-    f_edge, sent = run(
+    f_edge, f_sent = run(
         edge_kernel, (1,),
         [SMEM, SMEM, pl.BlockSpec((4, 5) + tile, lambda i: (0, 0, 0, 0)), quarter, quarter],
         [quarter, quarter], [quarter_shape, quarter_shape],
         (here, exps, f_parts, f_line, f_beside), partial, span=4.0 * span, name="edge",
     )
-    f_side = noted(swap(sent, "zl"))
+    partial, f_sent = lax.optimization_barrier((partial, f_sent))
+    f_side = noted(swap(f_sent, "zl"))
     f_edge, sent = run(
         chip_state_kernel, (1,), [SMEM, SMEM, quarter, quarter, line, line], [line, line],
         [line_kept, line_sent], (here, exps, f_edge, f_side, f_chip, f_next),

time: 288 us -> 271 us (0.941)
  waiting for transfers between devices: 152 us -> 138 us
  starting transfers between devices: 37.7 us -> 33.8 us
    all_gather x1, waiting for transfers between devices: 26.7 us -> 0.01 us  [per_device(): f_parts = lax.all_gather(f_lines, 'zh')]
    all_to_all x4, waiting for transfers between devices: 33.3 us -> 44.3 us  [exchange(): return lax.all_to_all(array, axes, split_axis=0, concat_axis=0, tiled=True)]
    all_to_all x4, starting transfers between devices: 31.4 us -> 27.9 us  [exchange(): return lax.all_to_all(array, axes, split_axis=0, concat_axis=0, tiled=True)]
  transfers between devices with their start and end apart: 14 -> 14, of which waited for: 11 -> 8; matrix products, arithmetic and copies ran while one was open for 1% -> 1% of each run, Pallas kernels for 20% -> 21%
where the time goes in v7:
time: 271 us; the launch traced here: 267 us
  waiting for transfers between devices  138 us (51%)
  Pallas kernels  59.9 us (22%)
  starting transfers between devices  33.8 us (12%)
  blocking collectives  18.5 us (7%)
  between operations  14.8 us (5%)
    ppermute x8, waiting for transfers between devices, swap(): return lax.ppermute(array, axis, [(0, 1), (1, 0)])  92.8 us
    pallas_call x16, Pallas kernels, call(): pl.pallas_call(kernel, grid=grid, in_specs=in_specs, out_specs=out_specs,...  59.9 us
    all_to_all x4, waiting for transfers between devices, exchange(): return lax.all_to_all(array, axes, split_axis=0, concat_axis=0, tiled=True)  44.3 us
    all_to_all x4, starting transfers between devices, exchange(): return lax.all_to_all(array, axes, split_axis=0, concat_axis=0, tiled=True)  27.9 us
    unnamed x1, blocking collectives  18.5 us
    ppermute x8, starting transfers between devices, swap(): return lax.ppermute(array, axis, [(0, 1), (1, 0)])  5.81 us
  transfers between devices with their start and end apart: 14, of which 8 were waited for; matrix products, arithmetic and copies ran while one was open for 1% of the time, Pallas kernels for 21%

profile of v7, /device:TPU:32, one launch (start us, length us, event | category | flops | bytes accessed | tf_op | source)
XLA Modules:
  0.0 267.4 jit_solution(9951368824579820320)
XLA Ops:
  7.2 0.0 all-gather.5.cloned.1.call-start
  7.2 0.7 all-gather.5.cloned.1.call-update
  8.6 1.3 dynamic-slice
  9.8 0.8 dynamic-update-slice
  10.6 18.5 %all-reduce.exp_ref = s32[32]{0:T(128)S(1)} all-reduce(s32[32]{0:T(128)S(1)} %dynamic-update-slice), channel_id=1, replica_groups=mesh['y'=4,'xh'=2,'zh'=4,'zl'=2,'xl'=2,'core'=2] {'zh','zl','xl','core'}, use_global_device_ids=true, to_apply=%add | all-reduce | flops 32 | bytes 256
  29.0 0.7 fusion
  29.8 3.3 %updates.2 = (f32[8,2,128,128]{3,2,1,0:T(8,128)}, f32[8,2,128,128]{3,2,1,0:T(8,128)}) custom-call(s32[3]{0:T(128)S(1)} %get-tuple-element.55.here_ref, s32[32]{0:T(128)S(1)} %all-reduce.exp_ref, bf16[128,4096]{1,0:T(8,128)(2,1)} %bitcast.44, bf16[128,4096]{1,0:T(8,128)(2,1)} %bitcast.40), custom_call_target="tpu_custom_call" | custom-call | tf_op jit(solution)/shard_map/updates/pallas_call | solution.py:293
  33.1 0.0 collective-permute-start.1
  33.1 2.9 %collective-permute-done.1.other_ref = f32[8,2,128,128]{3,2,1,0:T(8,128)S(1)} collective-permute-done((f32[8,2,128,128]{3,2,1,0:T(8,128)}, f32[8,2,128,128]{3,2,1,0:T(8,128)S(1)}, u32[]{:S(2)}, u32[]{:S(2)}) %collective-permute-start.1) | collective-permute-done | bytes 1048608 | tf_op jit(solution)/shard_map/ppermute | solution.py:285
  36.0 2.1 pair.1.refs_0_
  38.1 4.5 %all-to-all-start = ((f32[16,128,128]{2,1,0:T(8,128)}), f32[16,128,128]{2,1,0:T(8,128)S(1)}, u32[]{:S(2)}, u32[]{:S(2)}) async-start(f32[16,128,128]{2,1,0:T(8,128)} %bitcast.38), calls=%async_computation | async-start | bytes 2097152 | tf_op jit(solution)/shard_map/all_to_all | solution.py:281
  42.6 3.4 %updates.3 = (f32[8,2,128,128]{3,2,1,0:T(8,128)}, f32[8,2,128,128]{3,2,1,0:T(8,128)}) custom-call(s32[3]{0:T(128)S(1)} %get-tuple-element.56.here_ref, s32[32]{0:T(128)S(1)} %all-reduce.exp_ref, bf16[128,4096]{1,0:T(8,128)(2,1)} %bitcast.29, bf16[128,4096]{1,0:T(8,128)(2,1)} %bitcast.33, f32[8,2,128,128]{3,2,1,0:T(8,128)} %get-tuple-element.30.refs_0_.mine_ref), custom_call_target="tpu_custom_call" | custom-call | tf_op jit(solution)/shard_map/updates/pallas_call | solution.py:293
  46.0 0.0 collective-permute-start
  46.0 2.9 %collective-permute-done.other_ref = f32[8,2,128,128]{3,2,1,0:T(8,128)S(1)} collective-permute-done((f32[8,2,128,128]{3,2,1,0:T(8,128)}, f32[8,2,128,128]{3,2,1,0:T(8,128)S(1)}, u32[]{:S(2)}, u32[]{:S(2)}) %collective-permute-start) | collective-permute-done | bytes 1048608 | tf_op jit(solution)/shard_map/ppermute | solution.py:285
  48.9 2.5 chip.1
  51.3 1.5 collective-permute-start.2
  52.8 32.5 %collective-permute-done.2.after_ref.other_ref = f32[8,128,128]{2,1,0:T(8,128)S(1)} collective-permute-done((f32[8,128,128]{2,1,0:T(8,128)}, f32[8,128,128]{2,1,0:T(8,128)S(1)}, u32[]{:S(2)}, u32[]{:S(2)}) %collective-permute-start.2) | collective-permute-done | bytes 524320 | tf_op jit(solution)/shard_map/ppermute | solution.py:285
  85.3 0.0 all-to-all-done
  85.3 1.1 scan.1
  86.4 8.8 %all-to-all-start.1 = ((f32[16,128,128]{2,1,0:T(8,128)}), f32[16,128,128]{2,1,0:T(8,128)S(1)}, u32[]{:S(2)}, u32[]{:S(2)}) async-start(f32[16,128,128]{2,1,0:T(8,128)} %bitcast.39), calls=%async_computation.1 | async-start | bytes 2097152 | tf_op jit(solution)/shard_map/all_to_all | solution.py:281
  95.2 8.8 %inner.1 = (f32[128,4096]{1,0:T(8,128)}, f32[128,4096]{1,0:T(8,128)}) custom-call(s32[32]{0:T(128)S(1)} %all-reduce.exp_ref, bf16[128,4096]{1,0:T(8,128)(2,1)} %bitcast.45, bf16[128,4096]{1,0:T(8,128)(2,1)} %bitcast.30, bf16[128,4096]{1,0:T(8,128)(2,1)} %bitcast.34, bf16[128,4096]{1,0:T(8,128)(2,1)} %bitcast.41, f32[8,2,128,128]{3,2,1,0:T(8,128)} %get-tuple-element.36.after_ref), custom_call_target="tpu_custom_call" | custom-call | tf_op jit(solution)/shard_map/inner/pallas_call | solution.py:293
  104.0 16.1 %all-to-all-done.1 = f32[16,128,128]{2,1,0:T(8,128)S(1)} async-done(((f32[16,128,128]{2,1,0:T(8,128)}), f32[16,128,128]{2,1,0:T(8,128)S(1)}, u32[]{:S(2)}, u32[]{:S(2)}) %all-to-all-start.1) | async-done | bytes 1048608 | tf_op jit(solution)/shard_map/all_to_all | solution.py:281
  120.1 2.5 core_state.2
  122.6 0.0 collective-permute-start.4
  122.6 1.9 line.1
  124.5 3.0 %collective-permute-start.3 = (f32[4,128,128]{2,1,0:T(8,128)}, f32[4,128,128]{2,1,0:T(8,128)S(1)}, u32[]{:S(2)}, u32[]{:S(2)}) collective-permute-start(f32[4,128,128]{2,1,0:T(8,128)} %get-tuple-element.38), channel_id=1, source_target_pairs={{0,4},{4,0},{1,5},{5,1},{2,6},{6,2},{3,7},{7,3},{8,12},{12,8},{9,1... | collective-permute-start | bytes 786440 | tf_op jit(solution)/shard_map/ppermute | solution.py:285
  127.5 0.0 collective-permute-done.4.other_ref
  127.5 5.5 %key_value.1 = (bf16[128,4096]{1,0:T(8,128)(2,1)}, bf16[128,4096]{1,0:T(8,128)(2,1)}, bf16[8,4,128,256]{3,2,1,0:T(8,128)(2,1)}) custom-call(s32[3]{0:T(128)S(1)} %get-tuple-element.55.here_ref, s32[32]{0:T(128)S(1)} %all-reduce.exp_ref, bf16[128,4096]{1,0:T(8,128)(2,1)} %bitcast.31, bf16[128,4096]{1,0:T(8,128)(2,1)} %bitcast.35, ...), custom_call_target="tpu_custom_call" | custom-call | tf_op jit(solution)/shard_map/key_value/pallas_call | solution.py:293
  133.1 7.1 %all-to-all-start.2 = ((bf16[32,128,256]{2,1,0:T(8,128)(2,1)}), bf16[32,128,256]{2,1,0:T(8,128)(2,1)S(1)}, u32[]{:S(2)}, u32[]{:S(2)}) async-start(bf16[32,128,256]{2,1,0:T(8,128)(2,1)} %bitcast.43), calls=%async_computation.2 | async-start | bytes 4194304 | tf_op jit(solution)/shard_map/all_to_all | solution.py:281
  140.2 0.0 all-gather.7.cloned.1.call-start
  140.3 0.0 collective-permute-done.3.other_ref
  140.3 0.0 all-gather.5.cloned.1.call-done
  140.3 1.7 line_pair.1
  142.0 0.0 all-gather.7.cloned.1.call-update
  142.1 28.1 %all-to-all-done.2 = bf16[32,128,256]{2,1,0:T(8,128)(2,1)S(1)} async-done(((bf16[32,128,256]{2,1,0:T(8,128)(2,1)}), bf16[32,128,256]{2,1,0:T(8,128)(2,1)S(1)}, u32[]{:S(2)}, u32[]{:S(2)}) %all-to-all-start.2) | async-done | bytes 2097184 | tf_op jit(solution)/shard_map/all_to_all | solution.py:281
  170.2 13.2 %weight.1.after_ref = bf16[8,8,96,128]{3,2,1,0:T(8,128)(2,1)} custom-call(bf16[4096,256]{1,0:T(8,128)(2,1)S(1)} %bitcast.23, bf16[4096,3072]{1,0:T(8,128)(2,1)} %bitcast.28), custom_call_target="tpu_custom_call" | custom-call | tf_op jit(solution)/shard_map/weight/pallas_call | solution.py:293
  183.4 2.3 edge.1
  185.7 7.5 %all-to-all-start.3 = ((bf16[64,96,128]{2,1,0:T(8,128)(2,1)}), bf16[64,96,128]{2,1,0:T(8,128)(2,1)S(1)}, u32[]{:S(2)}, u32[]{:S(2)}) async-start(bf16[64,96,128]{2,1,0:T(8,128)(2,1)} %bitcast.37), calls=%async_computation.3 | async-start | bytes 3145728 | tf_op jit(solution)/shard_map/all_to_all | solution.py:281
  193.2 0.7 collective-permute-start.5
  193.9 39.2 %collective-permute-done.5.other_edge_ref = f32[4,128,128]{2,1,0:T(8,128)S(1)} collective-permute-done((f32[4,128,128]{2,1,0:T(8,128)S(1)}, f32[4,128,128]{2,1,0:T(8,128)S(1)}, u32[]{:S(2)}, u32[]{:S(2)}) %collective-permute-start.5) | collective-permute-done | bytes 262176 | tf_op jit(solution)/shard_map/ppermute | solution.py:285
  233.1 2.2 chip_state.1
  235.4 0.6 collective-permute-start.6
  235.9 12.5 %collective-permute-done.6.refs_1_ = f32[8,128,128]{2,1,0:T(8,128)S(1)} collective-permute-done((f32[8,128,128]{2,1,0:T(8,128)}, f32[8,128,128]{2,1,0:T(8,128)S(1)}, u32[]{:S(2)}, u32[]{:S(2)}) %collective-permute-start.6) | collective-permute-done | bytes 524320 | tf_op jit(solution)/shard_map/ppermute | solution.py:285
  248.4 2.6 core_state.3
  251.0 0.0 collective-permute-start.7
  251.0 2.9 %collective-permute-done.7.other_ref = f32[8,2,128,128]{3,2,1,0:T(8,128)S(1)} collective-permute-done((f32[8,2,128,128]{3,2,1,0:T(8,128)}, f32[8,2,128,128]{3,2,1,0:T(8,128)S(1)}, u32[]{:S(2)}, u32[]{:S(2)}) %collective-permute-start.7) | collective-permute-done | bytes 1048608 | tf_op jit(solution)/shard_map/ppermute | solution.py:285
  253.9 5.8 %query.1 = bf16[128,4096]{1,0:T(8,128)(2,1)} custom-call(s32[3]{0:T(128)S(1)} %get-tuple-element.56.here_ref, s32[32]{0:T(128)S(1)} %all-reduce.exp_ref, bf16[128,4096]{1,0:T(8,128)(2,1)} %bitcast.32, bf16[128,4096]{1,0:T(8,128)(2,1)} %bitcast.36, bf16[128,4096]{1,0:T(8,128)(2,1)} %bitcast.42, f32[8,2,128,128]{3,2,1,0:T(8,128)} %get-tuple-element.49.mine_ref, ...), custom_call_target="tpu_custom_call" | custom-call | tf_op jit(solution)/shard_map/query/pallas_call | solution.py:293
  259.7 0.9 total.1
  (9 shorter events, 0.0 us)
Async XLA Ops:
  7.2 133.1 %all-gather.5.cloned.1.call-start = ((), (), s32[]{:S(2)}) async-start(), calls=%async_computation.4 | async-start | bytes 25952256 | tf_op jit(solution)/shard_map/all_gather | solution.py:314
  33.1 2.9 %collective-permute-start.1 = (f32[8,2,128,128]{3,2,1,0:T(8,128)}, f32[8,2,128,128]{3,2,1,0:T(8,128)S(1)}, u32[]{:S(2)}, u32[]{:S(2)}) collective-permute-start(f32[8,2,128,128]{3,2,1,0:T(8,128)} %get-tuple-element.33), channel_id=1, source_target_pairs={{0,1},{1,0},{2,3},{3,2},{4,5},{5,4},{6,7},{7,6},{8,9},{9,8},{10,11... | collective-permute-start | bytes 3145736 | tf_op jit(solution)/shard_map/ppermute | solution.py:285
  38.1 47.2 %all-to-all-start = ((f32[16,128,128]{2,1,0:T(8,128)}), f32[16,128,128]{2,1,0:T(8,128)S(1)}, u32[]{:S(2)}, u32[]{:S(2)}) async-start(f32[16,128,128]{2,1,0:T(8,128)} %bitcast.38), calls=%async_computation | async-start | bytes 2097152 | tf_op jit(solution)/shard_map/all_to_all | solution.py:281
  46.0 2.9 %collective-permute-start = (f32[8,2,128,128]{3,2,1,0:T(8,128)}, f32[8,2,128,128]{3,2,1,0:T(8,128)S(1)}, u32[]{:S(2)}, u32[]{:S(2)}) collective-permute-start(f32[8,2,128,128]{3,2,1,0:T(8,128)} %get-tuple-element.32), channel_id=1, source_target_pairs={{0,1},{1,0},{2,3},{3,2},{4,5},{5,4},{6,7},{7,6},{8,9},{9,8},{10,11... | collective-permute-start | bytes 3145736 | tf_op jit(solution)/shard_map/ppermute | solution.py:285
  48.9 2.5 copy-start
  51.3 34.0 %collective-permute-start.2 = (f32[8,128,128]{2,1,0:T(8,128)}, f32[8,128,128]{2,1,0:T(8,128)S(1)}, u32[]{:S(2)}, u32[]{:S(2)}) collective-permute-start(f32[8,128,128]{2,1,0:T(8,128)} %get-tuple-element.35), channel_id=1, source_target_pairs={{0,2},{2,0},{1,3},{3,1},{4,6},{6,4},{5,7},{7,5},{8,10},{10,8},{9,1... | collective-permute-start | bytes 1572872 | tf_op jit(solution)/shard_map/ppermute | solution.py:285
  86.4 33.7 %all-to-all-start.1 = ((f32[16,128,128]{2,1,0:T(8,128)}), f32[16,128,128]{2,1,0:T(8,128)S(1)}, u32[]{:S(2)}, u32[]{:S(2)}) async-start(f32[16,128,128]{2,1,0:T(8,128)} %bitcast.39), calls=%async_computation.1 | async-start | bytes 2097152 | tf_op jit(solution)/shard_map/all_to_all | solution.py:281
  122.6 5.0 %collective-permute-start.4 = (f32[8,2,128,128]{3,2,1,0:T(8,128)}, f32[8,2,128,128]{3,2,1,0:T(8,128)S(1)}, u32[]{:S(2)}, u32[]{:S(2)}) collective-permute-start(f32[8,2,128,128]{3,2,1,0:T(8,128)} %get-tuple-element.42), channel_id=1, source_target_pairs={{0,1},{1,0},{2,3},{3,2},{4,5},{5,4},{6,7},{7,6},{8,9},{9,8},{10,11... | collective-permute-start | bytes 3145736 | tf_op jit(solution)/shard_map/ppermute | solution.py:285
  124.5 15.8 %collective-permute-start.3 = (f32[4,128,128]{2,1,0:T(8,128)}, f32[4,128,128]{2,1,0:T(8,128)S(1)}, u32[]{:S(2)}, u32[]{:S(2)}) collective-permute-start(f32[4,128,128]{2,1,0:T(8,128)} %get-tuple-element.38), channel_id=1, source_target_pairs={{0,4},{4,0},{1,5},{5,1},{2,6},{6,2},{3,7},{7,3},{8,12},{12,8},{9,1... | collective-permute-start | bytes 786440 | tf_op jit(solution)/shard_map/ppermute | solution.py:285
  133.1 37.1 %all-to-all-start.2 = ((bf16[32,128,256]{2,1,0:T(8,128)(2,1)}), bf16[32,128,256]{2,1,0:T(8,128)(2,1)S(1)}, u32[]{:S(2)}, u32[]{:S(2)}) async-start(bf16[32,128,256]{2,1,0:T(8,128)(2,1)} %bitcast.43), calls=%async_computation.2 | async-start | bytes 4194304 | tf_op jit(solution)/shard_map/all_to_all | solution.py:281
  140.2 43.2 %all-gather.7.cloned.1.call-start = ((), (), s32[]{:S(2)}) async-start(), calls=%async_computation.5 | async-start | bytes 1638400 | tf_op jit(solution)/shard_map/all_gather | solution.py:419
  185.7 7.5 %copy-start.2 = (f32[4,128,128]{2,1,0:T(8,128)S(1)}, f32[4,128,128]{2,1,0:T(8,128)}, u32[]{:S(2)}) copy-start(f32[4,128,128]{2,1,0:T(8,128)} %get-tuple-element.46) | copy-start | bytes 786436
  185.7 74.0 %all-to-all-start.3 = ((bf16[64,96,128]{2,1,0:T(8,128)(2,1)}), bf16[64,96,128]{2,1,0:T(8,128)(2,1)S(1)}, u32[]{:S(2)}, u32[]{:S(2)}) async-start(bf16[64,96,128]{2,1,0:T(8,128)(2,1)} %bitcast.37), calls=%async_computation.3 | async-start | bytes 3145728 | tf_op jit(solution)/shard_map/all_to_all | solution.py:281
  193.2 55.2 %copy-start.1 = (f32[8,2,128,128]{3,2,1,0:T(8,128)S(1)}, f32[8,2,128,128]{3,2,1,0:T(8,128)}, u32[]{:S(2)}) copy-start(f32[8,2,128,128]{3,2,1,0:T(8,128)} %copy-done) | copy-start | bytes 3145732
  193.2 39.9 %collective-permute-start.5 = (f32[4,128,128]{2,1,0:T(8,128)S(1)}, f32[4,128,128]{2,1,0:T(8,128)S(1)}, u32[]{:S(2)}, u32[]{:S(2)}) collective-permute-start(f32[4,128,128]{2,1,0:T(8,128)S(1)} %copy-done.2), channel_id=1, source_target_pairs={{0,4},{4,0},{1,5},{5,1},{2,6},{6,2},{3,7},{7,3},{8,12},{12,8},{9,1... | collective-permute-start | bytes 786440 | tf_op jit(solution)/shard_map/ppermute | solution.py:285
  235.4 13.0 %collective-permute-start.6 = (f32[8,128,128]{2,1,0:T(8,128)}, f32[8,128,128]{2,1,0:T(8,128)S(1)}, u32[]{:S(2)}, u32[]{:S(2)}) collective-permute-start(f32[8,128,128]{2,1,0:T(8,128)} %get-tuple-element.48), channel_id=1, source_target_pairs={{0,2},{2,0},{1,3},{3,1},{4,6},{6,4},{5,7},{7,5},{8,10},{10,8},{9,1... | collective-permute-start | bytes 1572872 | tf_op jit(solution)/shard_map/ppermute | solution.py:285
  251.0 2.9 %collective-permute-start.7 = (f32[8,2,128,128]{3,2,1,0:T(8,128)}, f32[8,2,128,128]{3,2,1,0:T(8,128)S(1)}, u32[]{:S(2)}, u32[]{:S(2)}) collective-permute-start(f32[8,2,128,128]{3,2,1,0:T(8,128)} %get-tuple-element.50), channel_id=1, source_target_pairs={{0,1},{1,0},{2,3},{3,2},{4,5},{5,4},{6,7},{7,6},{8,9},{9,8},{10,11... | collective-permute-start | bytes 3145736 | tf_op jit(solution)/shard_map/ppermute | solution.py:285
Sparse Core Ops, SparseCore 0:
  10.5 127.6 all-gather.4
  143.4 35.0 all-gather.6

commit v8 on v7

--- a/solution.py
+++ b/solution.py
@@ -98,68 +98,56 @@
     grad_ref[...] = power_of(rate, 1.0) * state
 
 
+def group_rate(here_ref, exp_ref, group, length):
+    return log_rate(exp_ref[4 * group + 2 * here_ref[1] + here_ref[2]], length)
+
+
 def line_kernel(
-    here_ref, exp_ref, mine_ref, other_ref, after_ref, keep_ref, send_ref, *, length, span
+    here_ref, exp_ref, mine_ref, other_ref, first_ref, after_ref, out_ref, *, length, span
 ):
-    parity = here_ref[0] % 2
-    for half, out_ref in enumerate((keep_ref, send_ref)):
-        for item in range(out_ref.shape[0]):
-            group = 2 * item + jnp.bitwise_xor(parity, half)
-            rate = log_rate(exp_ref[4 * group + 2 * here_ref[1] + here_ref[2]], length)
-            out_ref[item] = weighed(
-                mine_ref[group], other_ref[group], here_ref[1], False, rate, span
-            )
-
-
-def own_rate(here_ref, exp_ref, item, length):
-    group = 2 * item + here_ref[0] % 2
-    return log_rate(exp_ref[4 * group + 2 * here_ref[1] + here_ref[2]], length)
-
-
-def line_pair_kernel(
-    here_ref, exp_ref, mine_ref, other_ref, first_ref, *refs, length, span
-):
+    count = mine_ref.shape[0]
+    for group in range(count):
+        rate = group_rate(here_ref, exp_ref, group, length)
+        out_ref[group] = weighed(
+            mine_ref[group], other_ref[group], here_ref[1], False, rate, span
+        )
+    out_ref[count] = first_ref[...]
+
+
+def line_pair_kernel(here_ref, exp_ref, mine_ref, other_ref, *refs, length, span):
     out_ref = refs[-1]
-    count = mine_ref.shape[0]
-    for item in range(count):
-        rate = own_rate(here_ref, exp_ref, item, length)
-        out_ref[item] = weighed(
-            mine_ref[item], other_ref[item], here_ref[0] % 2, False, rate, span
-        )
-    out_ref[count] = first_ref[...]
+    count = mine_ref.shape[0] - 1
+    for group in range(count):
+        rate = group_rate(here_ref, exp_ref, group, length)
+        out_ref[group] = weighed(
+            mine_ref[group], other_ref[group], here_ref[0] % 2, False, rate, span
+        )
+    out_ref[count] = mine_ref[count]
+    out_ref[count + 1] = other_ref[count]
 
 
 def edge_kernel(
-    here_ref, exp_ref, parts_ref, mine_ref, other_ref, after_ref, keep_ref, send_ref,
+    here_ref, exp_ref, parts_ref, beside_ref, mine_ref, other_ref, after_ref, keep_ref, send_ref,
     *, length, span
 ):
     count = mine_ref.shape[0]
-    behind = here_ref[0] % 2 == 1
-    for item in range(count):
-        rate = own_rate(here_ref, exp_ref, item, length)
-        decay = power_of(rate, 2.0 * span)
-        state = parts_ref[item, count]
-        for before in range(count - 1):
-            update = decay * state + parts_ref[before, item]
+    for group in range(count):
+        rate = group_rate(here_ref, exp_ref, group, length)
+        decay = power_of(rate, 4.0 * span)
+        state = jnp.where(
+            here_ref[0] % 2 == group % 2,
+            parts_ref[group // 2, count],
+            parts_ref[group // 2, count + 1],
+        )
+        for before in range(parts_ref.shape[0] - 1):
+            update = decay * state + parts_ref[before, group]
             state = jnp.where(here_ref[0] // 2 > before, update, state)
+        update = power_of(rate, 2.0 * span) * state + beside_ref[group]
+        state = jnp.where(here_ref[0] % 2 == 1, update, state)
         past = power_of(rate, span) * state
-        keep_ref[item] = jnp.where(behind, past + other_ref[item], state)
-        send_ref[item] = jnp.where(behind, state, past + mine_ref[item])
-
-
-def chip_state_kernel(
-    here_ref, exp_ref, mine_edge_ref, other_edge_ref, mine_ref, other_ref, keep_ref, send_ref,
-    *, length, span
-):
-    behind = here_ref[1] == 1
-    for group in range(keep_ref.shape[0]):
-        rate = log_rate(exp_ref[4 * group + 2 * here_ref[1] + here_ref[2]], length)
-        edge = jnp.where(
-            here_ref[0] % 2 == group % 2, mine_edge_ref[group // 2], other_edge_ref[group // 2]
-        )
-        past = power_of(rate, span) * edge
-        keep_ref[group] = jnp.where(behind, past + other_ref[group], edge)
-        send_ref[group] = jnp.where(behind, edge, past + mine_ref[group])
+        behind = here_ref[1] == 1
+        keep_ref[group] = jnp.where(behind, past + other_ref[group], state)
+        send_ref[group] = jnp.where(behind, state, past + mine_ref[group])
 
 
 def core_state_kernel(here_ref, exp_ref, mine_ref, other_ref, *refs, reverse, count, length, span):
@@ -210,7 +198,7 @@
 
 def key_value_kernel(
     here_ref, exp_ref, key_ref, value_ref, inner_gk_ref, inner_gv_ref, mine_ref, other_ref,
-    gk_ref, gv_ref, send_ref, *, length
+    after_ref, gk_ref, gv_ref, send_ref, *, length
 ):
     span = key_ref.shape[0]
     left = span - lax.broadcasted_iota(jnp.int32, (span, WIDTH), 0).astype(f32)
@@ -383,16 +371,15 @@
     all_pairs = pl.BlockSpec((groups, 2) + tile, lambda i: (0, 0, 0, 0))
     r_edges, state_grad = run(
         scan_kernel, (1,), [SMEM, all_pairs], [all_pairs, single], [pair_sent, tile_shape],
-        (decay_exp, r_parts), f_next, span=2.0 * span, name="scan",
-    )
-    quarter = pl.BlockSpec((4,) + tile, lambda i: (0, 0, 0))
-    quarter_shape = pltpu.HBM((4,) + tile, f32)
-    f_line, sent = run(
-        line_kernel, (1,), [SMEM, SMEM, line, line], [quarter, quarter],
-        [quarter_shape, quarter_shape], (here, exps, f_chip, f_next), r_edges,
+        (decay_exp, r_parts), f_chip, span=2.0 * span, name="scan",
+    )
+    nine = pl.BlockSpec((groups + 1,) + tile, lambda i: (0, 0, 0))
+    f_line = run(
+        line_kernel, (1,), [SMEM, SMEM, line, line, single], nine,
+        pltpu.HBM((groups + 1,) + tile, f32), (here, exps, f_chip, f_next, state_in[0, 0]), r_edges,
         span=2.0 * span, name="line",
     )
-    f_beside = noted(swap(sent, "zl"))
+    f_beside = noted(swap(f_line, "zl"))
     inner_gk, inner_gv = run(
         inner_kernel, (2,), [SMEM] + 4 * [head_cols], 2 * [head_cols], 2 * [inner_shape],
         (exps, query, key, value, grad), r_edges, name="inner",
@@ -405,16 +392,16 @@
         key_value_kernel, (2,), [SMEM, SMEM] + 4 * [head_cols] + 2 * [pair_tiles],
         [head_cols, head_cols, pl.BlockSpec((8, 4, span, WIDTH), lambda i: (0, 0, 0, i))],
         [token_shape, token_shape, pltpu.HBM((8, 4, span, 2 * WIDTH), bf16)],
-        (even, exps, key, value, inner_gk, inner_gv, mine, other), name="key_value",
+        (even, exps, key, value, inner_gk, inner_gv, mine, other), f_line, name="key_value",
     )
     cols = exchange(send.reshape(32, span, 2 * WIDTH), PLANE)
     cols = cols.reshape(32 * span, 2 * WIDTH)
 
     f_lines = run(
-        line_pair_kernel, (1,), [SMEM, SMEM, quarter, quarter, single, FREE],
-        pl.BlockSpec((5,) + tile, lambda i: (0, 0, 0)), pltpu.HBM((5,) + tile, f32),
-        (here, exps, f_line, f_beside, state_in[0, 0], rows), send, span=4.0 * span,
-        name="line_pair",
+        line_pair_kernel, (1,), [SMEM, SMEM, nine, nine],
+        pl.BlockSpec((groups + 2,) + tile, lambda i: (0, 0, 0)),
+        pltpu.HBM((groups + 2,) + tile, f32), (here, exps, f_line, f_beside), send,
+        span=4.0 * span, name="line_pair",
     )
     f_parts = lax.all_gather(f_lines, "zh")
     tokens, width = rows.shape
@@ -428,18 +415,14 @@
         pl.BlockSpec((8, 2, block // 8, WIDTH), lambda i: (0, i, 0, 0)),
         pltpu.HBM((8, 8, block // 8, WIDTH), bf16), (cols, far(rows)), scratch=[pltpu.VMEM((2 * WIDTH, tokens), bf16)], name="weight", vmem=40,
     )
-    f_edge, f_sent = run(
+    f_edge, sent = run(
         edge_kernel, (1,),
-        [SMEM, SMEM, pl.BlockSpec((4, 5) + tile, lambda i: (0, 0, 0, 0)), quarter, quarter],
-        [quarter, quarter], [quarter_shape, quarter_shape],
-        (here, exps, f_parts, f_line, f_beside), partial, span=4.0 * span, name="edge",
-    )
-    partial, f_sent = lax.optimization_barrier((partial, f_sent))
-    f_side = noted(swap(f_sent, "zl"))
-    f_edge, sent = run(
-        chip_state_kernel, (1,), [SMEM, SMEM, quarter, quarter, line, line], [line, line],
-        [line_kept, line_sent], (here, exps, f_edge, f_side, f_chip, f_next),
-        span=2.0 * span, name="chip_state",
+        [
+            SMEM, SMEM, pl.BlockSpec((4, groups + 2) + tile, lambda i: (0, 0, 0, 0)), nine, line,
+            line,
+        ],
+        [line, line], [line_kept, line_sent], (here, exps, f_parts, f_beside, f_chip, f_next),
+        partial, span=2.0 * span, name="edge",
     )
     f_far = noted(swap(sent, "xl"))
     mine, sent = core_state([f_edge, f_far], f_mine, f_other, here, False)

time: 271 us -> 261 us (0.963)
  waiting for transfers between devices: 138 us -> 102 us
  blocking collectives: 18.5 us -> 54.2 us
  starting transfers between devices: 33.8 us -> 24.2 us
    ppermute x8 -> x7, waiting for transfers between devices: 92.8 us -> 44.6 us  [swap(): return lax.ppermute(array, axis, [(0, 1), (1, 0)])]
    all_to_all x0 -> x1, blocking collectives: none -> 35.7 us  [exchange(): return lax.all_to_all(array, axes, split_axis=0, concat_axis=0, tiled=True)]
    all_gather x1, waiting for transfers between devices: 0.01 us -> 24.7 us  [per_device(): f_parts = lax.all_gather(f_lines, 'zh')]
    all_to_all x4 -> x3, waiting for transfers between devices: 44.3 us -> 31.5 us  [exchange(): return lax.all_to_all(array, axes, split_axis=0, concat_axis=0, tiled=True)]
    all_to_all x4 -> x3, starting transfers between devices: 27.9 us -> 20.5 us  [exchange(): return lax.all_to_all(array, axes, split_axis=0, concat_axis=0, tiled=True)]
    ppermute x8 -> x7, starting transfers between devices: 5.81 us -> 3.63 us  [swap(): return lax.ppermute(array, axis, [(0, 1), (1, 0)])]
    pallas_call x16 -> x15, Pallas kernels: 59.9 us -> 59.1 us  [call(): pl.pallas_call(kernel, grid=grid, in_specs=in_specs, out_specs=out_specs,...]
  transfers between devices with their start and end apart: 14 -> 12, of which waited for: 8 -> 9; matrix products, arithmetic and copies ran while one was open for 1% -> 1% of each run, Pallas kernels for 21% -> 23%
where the time goes in v8:
time: 261 us; the launch traced here: 258 us
  waiting for transfers between devices  102 us (39%)
  Pallas kernels  59.1 us (23%)
  blocking collectives  54.2 us (21%)
  starting transfers between devices  24.2 us (9%)
  between operations  14.7 us (6%)
  local copies, waits for them, and re-layouts  3.92 us (2%)
    pallas_call x15, Pallas kernels, call(): pl.pallas_call(kernel, grid=grid, in_specs=in_specs, out_specs=out_specs,...  59.1 us
    ppermute x7, waiting for transfers between devices, swap(): return lax.ppermute(array, axis, [(0, 1), (1, 0)])  44.6 us
    all_to_all x1, blocking collectives, exchange(): return lax.all_to_all(array, axes, split_axis=0, concat_axis=0, tiled=True)  35.7 us
    all_to_all x3, waiting for transfers between devices, exchange(): return lax.all_to_all(array, axes, split_axis=0, concat_axis=0, tiled=True)  31.5 us
    all_gather x1, waiting for transfers between devices, per_device(): f_parts = lax.all_gather(f_lines, 'zh')  24.7 us
    all_to_all x3, starting transfers between devices, exchange(): return lax.all_to_all(array, axes, split_axis=0, concat_axis=0, tiled=True)  20.5 us
    unnamed x1, blocking collectives  18.5 us
  transfers between devices with their start and end apart: 12, of which 9 were waited for; matrix products, arithmetic and copies ran while one was open for 1% of the time, Pallas kernels for 23%

profile of v8, /device:TPU:32, one launch (start us, length us, event | category | flops | bytes accessed | tf_op | source)
XLA Modules:
  0.0 258.4 jit_solution(13510758508903725457)
XLA Ops:
  7.2 0.0 all-gather.7.cloned.1.call-start
  7.2 0.7 all-gather.7.cloned.1.call-update
  8.6 1.3 dynamic-slice
  9.8 0.8 dynamic-update-slice
  10.6 18.5 %all-reduce.exp_ref = s32[32]{0:T(128)S(1)} all-reduce(s32[32]{0:T(128)S(1)} %dynamic-update-slice), channel_id=1, replica_groups=mesh['y'=4,'xh'=2,'zh'=4,'zl'=2,'xl'=2,'core'=2] {'zh','zl','xl','core'}, use_global_device_ids=true, to_apply=%add | all-reduce | flops 32 | bytes 256
  29.0 0.7 fusion
  29.8 3.3 %updates.2 = (f32[8,2,128,128]{3,2,1,0:T(8,128)}, f32[8,2,128,128]{3,2,1,0:T(8,128)}) custom-call(s32[3]{0:T(128)S(1)} %get-tuple-element.43.here_ref, s32[32]{0:T(128)S(1)} %all-reduce.exp_ref, bf16[128,4096]{1,0:T(8,128)(2,1)} %bitcast.43, bf16[128,4096]{1,0:T(8,128)(2,1)} %bitcast.39), custom_call_target="tpu_custom_call" | custom-call | tf_op jit(solution)/shard_map/updates/pallas_call | solution.py:281
  33.1 0.0 collective-permute-start.1
  33.1 2.9 %collective-permute-done.1.other_ref = f32[8,2,128,128]{3,2,1,0:T(8,128)S(1)} collective-permute-done((f32[8,2,128,128]{3,2,1,0:T(8,128)}, f32[8,2,128,128]{3,2,1,0:T(8,128)S(1)}, u32[]{:S(2)}, u32[]{:S(2)}) %collective-permute-start.1) | collective-permute-done | bytes 1048608 | tf_op jit(solution)/shard_map/ppermute | solution.py:273
  36.0 2.1 pair.1.refs_0_
  38.1 4.5 %all-to-all-start = ((f32[16,128,128]{2,1,0:T(8,128)}), f32[16,128,128]{2,1,0:T(8,128)S(1)}, u32[]{:S(2)}, u32[]{:S(2)}) async-start(f32[16,128,128]{2,1,0:T(8,128)} %bitcast.38), calls=%async_computation | async-start | bytes 2097152 | tf_op jit(solution)/shard_map/all_to_all | solution.py:269
  42.6 3.4 %updates.3 = (f32[8,2,128,128]{3,2,1,0:T(8,128)}, f32[8,2,128,128]{3,2,1,0:T(8,128)}) custom-call(s32[3]{0:T(128)S(1)} %get-tuple-element.44.here_ref, s32[32]{0:T(128)S(1)} %all-reduce.exp_ref, bf16[128,4096]{1,0:T(8,128)(2,1)} %bitcast.28, bf16[128,4096]{1,0:T(8,128)(2,1)} %bitcast.32, f32[8,2,128,128]{3,2,1,0:T(8,128)} %get-tuple-element.24.refs_0_.mine_ref), custom_call_target="tpu_custom_call" | custom-call | tf_op jit(solution)/shard_map/updates/pallas_call | solution.py:281
  46.0 0.0 collective-permute-start
  46.0 2.9 %collective-permute-done.other_ref = f32[8,2,128,128]{3,2,1,0:T(8,128)S(1)} collective-permute-done((f32[8,2,128,128]{3,2,1,0:T(8,128)}, f32[8,2,128,128]{3,2,1,0:T(8,128)S(1)}, u32[]{:S(2)}, u32[]{:S(2)}) %collective-permute-start) | collective-permute-done | bytes 1048608 | tf_op jit(solution)/shard_map/ppermute | solution.py:273
  48.9 2.1 chip.1
  51.0 17.5 %all-to-all-done = f32[16,128,128]{2,1,0:T(8,128)S(1)} async-done(((f32[16,128,128]{2,1,0:T(8,128)}), f32[16,128,128]{2,1,0:T(8,128)S(1)}, u32[]{:S(2)}, u32[]{:S(2)}) %all-to-all-start) | async-done | bytes 1048608 | tf_op jit(solution)/shard_map/all_to_all | solution.py:269
  68.5 1.1 scan.1
  69.6 7.2 %all-to-all-start.1 = ((f32[16,128,128]{2,1,0:T(8,128)}), f32[16,128,128]{2,1,0:T(8,128)S(1)}, u32[]{:S(2)}, u32[]{:S(2)}) async-start(f32[16,128,128]{2,1,0:T(8,128)} %bitcast.37), calls=%async_computation.1 | async-start | bytes 2097152 | tf_op jit(solution)/shard_map/all_to_all | solution.py:269
  76.8 0.0 all-gather.5.cloned.1.call-start
  76.8 1.6 collective-permute-start.2
  78.4 8.9 %inner.1 = (f32[128,4096]{1,0:T(8,128)}, f32[128,4096]{1,0:T(8,128)}) custom-call(s32[32]{0:T(128)S(1)} %all-reduce.exp_ref, bf16[128,4096]{1,0:T(8,128)(2,1)} %bitcast.44, bf16[128,4096]{1,0:T(8,128)(2,1)} %bitcast.29, bf16[128,4096]{1,0:T(8,128)(2,1)} %bitcast.33, bf16[128,4096]{1,0:T(8,128)(2,1)} %bitcast.40, f32[8,2,128,128]{3,2,1,0:T(8,128)} %get-tuple-element.30.after_ref), custom_call_target="tpu_custom_call" | custom-call | tf_op jit(solution)/shard_map/inner/pallas_call | solution.py:281
  87.3 14.0 %all-to-all-done.1 = f32[16,128,128]{2,1,0:T(8,128)S(1)} async-done(((f32[16,128,128]{2,1,0:T(8,128)}), f32[16,128,128]{2,1,0:T(8,128)S(1)}, u32[]{:S(2)}, u32[]{:S(2)}) %all-to-all-start.1) | async-done | bytes 1048608 | tf_op jit(solution)/shard_map/all_to_all | solution.py:269
  101.3 2.5 core_state.2
  103.8 0.0 collective-permute-start.4
  103.8 10.6 %collective-permute-done.2.other_ref = f32[8,128,128]{2,1,0:T(8,128)} collective-permute-done((f32[8,128,128]{2,1,0:T(8,128)}, f32[8,128,128]{2,1,0:T(8,128)}, u32[]{:S(2)}, u32[]{:S(2)}) %collective-permute-start.2) | collective-permute-done | bytes 524320 | tf_op jit(solution)/shard_map/ppermute | solution.py:273
  114.4 2.1 line.1.after_ref.mine_ref
  116.6 0.6 collective-permute-start.3
  117.1 0.0 collective-permute-done.4.other_ref
  117.1 5.7 %key_value.1 = (bf16[128,4096]{1,0:T(8,128)(2,1)}, bf16[128,4096]{1,0:T(8,128)(2,1)}, bf16[8,4,128,256]{3,2,1,0:T(8,128)(2,1)}) custom-call(s32[3]{0:T(128)S(1)} %get-tuple-element.43.here_ref, s32[32]{0:T(128)S(1)} %all-reduce.exp_ref, bf16[128,4096]{1,0:T(8,128)(2,1)} %bitcast.30, bf16[128,4096]{1,0:T(8,128)(2,1)} %bitcast.34, ...), custom_call_target="tpu_custom_call" | custom-call | tf_op jit(solution)/shard_map/key_value/pallas_call | solution.py:281
  122.9 7.2 %collective-permute-done.3.other_ref.beside_ref = f32[9,128,128]{2,1,0:T(8,128)S(1)} collective-permute-done((f32[9,128,128]{2,1,0:T(8,128)}, f32[9,128,128]{2,1,0:T(8,128)S(1)}, u32[]{:S(2)}, u32[]{:S(2)}) %collective-permute-start.3) | collective-permute-done | bytes 589856 | tf_op jit(solution)/shard_map/ppermute | solution.py:273
  130.0 2.0 line_pair.1
  132.0 0.0 copy-start
  132.0 0.8 copy-done
  132.9 0.0 all-gather.5.cloned.1.call-update
  132.9 35.7 %all_to_all.20 = bf16[32,128,256]{2,1,0:T(8,128)(2,1)S(1)} all-to-all(bf16[32,128,256]{2,1,0:T(8,128)(2,1)} %bitcast.42), channel_id=1, replica_groups=mesh['y'=4,'xh'=2,'zh'=4,'zl'=2,'xl'=2,'core'=2] {'y','xh','xl','core'}, dimensions={0} | all-to-all | bytes 4194304 | tf_op jit(solution)/shard_map/all_to_all | solution.py:269
  168.6 13.1 %weight.1.after_ref = bf16[8,8,96,128]{3,2,1,0:T(8,128)(2,1)} custom-call(bf16[4096,256]{1,0:T(8,128)(2,1)S(1)} %bitcast.23, bf16[4096,3072]{1,0:T(8,128)(2,1)} %bitcast.27), custom_call_target="tpu_custom_call" | custom-call | tf_op jit(solution)/shard_map/weight/pallas_call | solution.py:281
  181.7 8.8 %all-to-all-start.3 = ((bf16[64,96,128]{2,1,0:T(8,128)(2,1)}), bf16[64,96,128]{2,1,0:T(8,128)(2,1)S(1)}, u32[]{:S(2)}, u32[]{:S(2)}) async-start(bf16[64,96,128]{2,1,0:T(8,128)(2,1)} %bitcast.36), calls=%async_computation.3 | async-start | bytes 3145728 | tf_op jit(solution)/shard_map/all_to_all | solution.py:269
  190.5 24.7 %all-gather.5.cloned.1.call-done = f32[40,128,128]{2,1,0:T(8,128)} async-done(((f32[10,128,128]{2,1,0:T(8,128)}), f32[40,128,128]{2,1,0:T(8,128)}) %all-gather.5.cloned.1.call-update) | async-done | bytes 2621456 | tf_op jit(solution)/shard_map/all_gather | solution.py:406
  215.2 1.1 copy-done.1
  216.3 3.3 %edge.1 = (f32[8,128,128]{2,1,0:T(8,128)}, f32[8,128,128]{2,1,0:T(8,128)}) custom-call(s32[3]{0:T(128)S(1)} %get-tuple-element.44.here_ref, s32[32]{0:T(128)S(1)} %all-reduce.exp_ref, f32[4,10,128,128]{3,2,1,0:T(8,128)} %bitcast.45, f32[9,128,128]{2,1,0:T(8,128)S(1)} %copy-done.1, f32[8,128,128]{2,1,0:T(8,128)} %get-tuple-element.28.after_ref.mine_ref, ...), custom_call_target="tpu_custom_call" | custom-call | tf_op jit(solution)/shard_map/edge/pallas_call | solution.py:281
  219.6 1.5 collective-permute-start.5
  221.1 18.3 %collective-permute-done.5.refs_1_ = f32[8,128,128]{2,1,0:T(8,128)S(1)} collective-permute-done((f32[8,128,128]{2,1,0:T(8,128)}, f32[8,128,128]{2,1,0:T(8,128)S(1)}, u32[]{:S(2)}, u32[]{:S(2)}) %collective-permute-start.5) | collective-permute-done | bytes 524320 | tf_op jit(solution)/shard_map/ppermute | solution.py:273
  239.3 2.6 core_state.3
  241.9 0.0 collective-permute-start.6
  241.9 2.9 %collective-permute-done.6.other_ref = f32[8,2,128,128]{3,2,1,0:T(8,128)S(1)} collective-permute-done((f32[8,2,128,128]{3,2,1,0:T(8,128)}, f32[8,2,128,128]{3,2,1,0:T(8,128)S(1)}, u32[]{:S(2)}, u32[]{:S(2)}) %collective-permute-start.6) | collective-permute-done | bytes 1048608 | tf_op jit(solution)/shard_map/ppermute | solution.py:273
  244.8 5.8 %query.1 = bf16[128,4096]{1,0:T(8,128)(2,1)} custom-call(s32[3]{0:T(128)S(1)} %get-tuple-element.44.here_ref, s32[32]{0:T(128)S(1)} %all-reduce.exp_ref, bf16[128,4096]{1,0:T(8,128)(2,1)} %bitcast.31, bf16[128,4096]{1,0:T(8,128)(2,1)} %bitcast.35, bf16[128,4096]{1,0:T(8,128)(2,1)} %bitcast.41, f32[8,2,128,128]{3,2,1,0:T(8,128)} %get-tuple-element.38.mine_ref, ...), custom_call_target="tpu_custom_call" | custom-call | tf_op jit(solution)/shard_map/query/pallas_call | solution.py:281
  250.6 0.0 all-to-all-done.3
  250.6 0.9 total.1
  (3 shorter events, 0.0 us)
Async XLA Ops:
  7.2 161.4 %all-gather.7.cloned.1.call-start = ((), (), s32[]{:S(2)}) async-start(), calls=%async_computation.5 | async-start | bytes 25952256 | tf_op jit(solution)/shard_map/all_gather | solution.py:302
  33.1 2.9 %collective-permute-start.1 = (f32[8,2,128,128]{3,2,1,0:T(8,128)}, f32[8,2,128,128]{3,2,1,0:T(8,128)S(1)}, u32[]{:S(2)}, u32[]{:S(2)}) collective-permute-start(f32[8,2,128,128]{3,2,1,0:T(8,128)} %get-tuple-element.27), channel_id=1, source_target_pairs={{0,1},{1,0},{2,3},{3,2},{4,5},{5,4},{6,7},{7,6},{8,9},{9,8},{10,11... | collective-permute-start | bytes 3145736 | tf_op jit(solution)/shard_map/ppermute | solution.py:273
  38.1 30.4 %all-to-all-start = ((f32[16,128,128]{2,1,0:T(8,128)}), f32[16,128,128]{2,1,0:T(8,128)S(1)}, u32[]{:S(2)}, u32[]{:S(2)}) async-start(f32[16,128,128]{2,1,0:T(8,128)} %bitcast.38), calls=%async_computation | async-start | bytes 2097152 | tf_op jit(solution)/shard_map/all_to_all | solution.py:269
  46.0 2.9 %collective-permute-start = (f32[8,2,128,128]{3,2,1,0:T(8,128)}, f32[8,2,128,128]{3,2,1,0:T(8,128)S(1)}, u32[]{:S(2)}, u32[]{:S(2)}) collective-permute-start(f32[8,2,128,128]{3,2,1,0:T(8,128)} %get-tuple-element.26), channel_id=1, source_target_pairs={{0,1},{1,0},{2,3},{3,2},{4,5},{5,4},{6,7},{7,6},{8,9},{9,8},{10,11... | collective-permute-start | bytes 3145736 | tf_op jit(solution)/shard_map/ppermute | solution.py:273
  69.6 31.8 %all-to-all-start.1 = ((f32[16,128,128]{2,1,0:T(8,128)}), f32[16,128,128]{2,1,0:T(8,128)S(1)}, u32[]{:S(2)}, u32[]{:S(2)}) async-start(f32[16,128,128]{2,1,0:T(8,128)} %bitcast.37), calls=%async_computation.1 | async-start | bytes 2097152 | tf_op jit(solution)/shard_map/all_to_all | solution.py:269
  76.8 138.5 %all-gather.5.cloned.1.call-start = ((), (), s32[]{:S(2)}) async-start(), calls=%async_computation.4 | async-start | bytes 3276800 | tf_op jit(solution)/shard_map/all_gather | solution.py:406
  76.8 37.6 %collective-permute-start.2 = (f32[8,128,128]{2,1,0:T(8,128)}, f32[8,128,128]{2,1,0:T(8,128)}, u32[]{:S(2)}, u32[]{:S(2)}) collective-permute-start(f32[8,128,128]{2,1,0:T(8,128)} %get-tuple-element.29), channel_id=1, source_target_pairs={{0,2},{2,0},{1,3},{3,1},{4,6},{6,4},{5,7},{7,5},{8,10},{10,8},{9,1... | collective-permute-start | bytes 1572872 | tf_op jit(solution)/shard_map/ppermute | solution.py:273
  103.8 13.3 %collective-permute-start.4 = (f32[8,2,128,128]{3,2,1,0:T(8,128)}, f32[8,2,128,128]{3,2,1,0:T(8,128)S(1)}, u32[]{:S(2)}, u32[]{:S(2)}) collective-permute-start(f32[8,2,128,128]{3,2,1,0:T(8,128)} %get-tuple-element.34), channel_id=1, source_target_pairs={{0,1},{1,0},{2,3},{3,2},{4,5},{5,4},{6,7},{7,6},{8,9},{9,8},{10,11... | collective-permute-start | bytes 3145736 | tf_op jit(solution)/shard_map/ppermute | solution.py:273
  116.6 13.5 %collective-permute-start.3 = (f32[9,128,128]{2,1,0:T(8,128)}, f32[9,128,128]{2,1,0:T(8,128)S(1)}, u32[]{:S(2)}, u32[]{:S(2)}) collective-permute-start(f32[9,128,128]{2,1,0:T(8,128)} %line.1.after_ref.mine_ref), channel_id=1, source_target_pairs={{0,4},{4,0},{1,5},{5,1},{2,6},{6,2},{3,7},{7,3},{8,12},{12,8},{9,1... | collective-permute-start | bytes 1769480 | tf_op jit(solution)/shard_map/ppermute | solution.py:273
  132.0 0.8 copy-start
  181.7 68.9 %all-to-all-start.3 = ((bf16[64,96,128]{2,1,0:T(8,128)(2,1)}), bf16[64,96,128]{2,1,0:T(8,128)(2,1)S(1)}, u32[]{:S(2)}, u32[]{:S(2)}) async-start(bf16[64,96,128]{2,1,0:T(8,128)(2,1)} %bitcast.36), calls=%async_computation.3 | async-start | bytes 3145728 | tf_op jit(solution)/shard_map/all_to_all | solution.py:269
  215.2 1.1 copy-start.1
  219.6 19.7 %collective-permute-start.5 = (f32[8,128,128]{2,1,0:T(8,128)}, f32[8,128,128]{2,1,0:T(8,128)S(1)}, u32[]{:S(2)}, u32[]{:S(2)}) collective-permute-start(f32[8,128,128]{2,1,0:T(8,128)} %get-tuple-element.37), channel_id=1, source_target_pairs={{0,2},{2,0},{1,3},{3,1},{4,6},{6,4},{5,7},{7,5},{8,10},{10,8},{9,1... | collective-permute-start | bytes 1572872 | tf_op jit(solution)/shard_map/ppermute | solution.py:273
  241.9 2.9 %collective-permute-start.6 = (f32[8,2,128,128]{3,2,1,0:T(8,128)}, f32[8,2,128,128]{3,2,1,0:T(8,128)S(1)}, u32[]{:S(2)}, u32[]{:S(2)}) collective-permute-start(f32[8,2,128,128]{3,2,1,0:T(8,128)} %get-tuple-element.39), channel_id=1, source_target_pairs={{0,1},{1,0},{2,3},{3,2},{4,5},{5,4},{6,7},{7,6},{8,9},{9,8},{10,11... | collective-permute-start | bytes 3145736 | tf_op jit(solution)/shard_map/ppermute | solution.py:273
Sparse Core Ops, SparseCore 0:
  10.5 128.8 all-gather.6
  141.8 73.3 all-gather.4

commit v9 on v7

--- a/solution.py
+++ b/solution.py
@@ -210,7 +210,7 @@
 
 def key_value_kernel(
     here_ref, exp_ref, key_ref, value_ref, inner_gk_ref, inner_gv_ref, mine_ref, other_ref,
-    gk_ref, gv_ref, send_ref, *, length
+    after_ref, gk_ref, gv_ref, send_ref, *, length
 ):
     span = key_ref.shape[0]
     left = span - lax.broadcasted_iota(jnp.int32, (span, WIDTH), 0).astype(f32)
@@ -383,7 +383,7 @@
     all_pairs = pl.BlockSpec((groups, 2) + tile, lambda i: (0, 0, 0, 0))
     r_edges, state_grad = run(
         scan_kernel, (1,), [SMEM, all_pairs], [all_pairs, single], [pair_sent, tile_shape],
-        (decay_exp, r_parts), f_next, span=2.0 * span, name="scan",
+        (decay_exp, r_parts), f_chip, span=2.0 * span, name="scan",
     )
     quarter = pl.BlockSpec((4,) + tile, lambda i: (0, 0, 0))
     quarter_shape = pltpu.HBM((4,) + tile, f32)
@@ -405,15 +405,15 @@
         key_value_kernel, (2,), [SMEM, SMEM] + 4 * [head_cols] + 2 * [pair_tiles],
         [head_cols, head_cols, pl.BlockSpec((8, 4, span, WIDTH), lambda i: (0, 0, 0, i))],
         [token_shape, token_shape, pltpu.HBM((8, 4, span, 2 * WIDTH), bf16)],
-        (even, exps, key, value, inner_gk, inner_gv, mine, other), name="key_value",
+        (even, exps, key, value, inner_gk, inner_gv, mine, other), f_line, name="key_value",
     )
     cols = exchange(send.reshape(32, span, 2 * WIDTH), PLANE)
     cols = cols.reshape(32 * span, 2 * WIDTH)
 
     f_lines = run(
-        line_pair_kernel, (1,), [SMEM, SMEM, quarter, quarter, single, FREE],
+        line_pair_kernel, (1,), [SMEM, SMEM, quarter, quarter, single],
         pl.BlockSpec((5,) + tile, lambda i: (0, 0, 0)), pltpu.HBM((5,) + tile, f32),
-        (here, exps, f_line, f_beside, state_in[0, 0], rows), send, span=4.0 * span,
+        (here, exps, f_line, f_beside, state_in[0, 0]), send, span=4.0 * span,
         name="line_pair",
     )
     f_parts = lax.all_gather(f_lines, "zh")
@@ -434,13 +434,13 @@
         [quarter, quarter], [quarter_shape, quarter_shape],
         (here, exps, f_parts, f_line, f_beside), partial, span=4.0 * span, name="edge",
     )
-    partial, f_sent = lax.optimization_barrier((partial, f_sent))
     f_side = noted(swap(f_sent, "zl"))
     f_edge, sent = run(
         chip_state_kernel, (1,), [SMEM, SMEM, quarter, quarter, line, line], [line, line],
         [line_kept, line_sent], (here, exps, f_edge, f_side, f_chip, f_next),
         span=2.0 * span, name="chip_state",
     )
+    partial, sent = lax.optimization_barrier((partial, sent))
     f_far = noted(swap(sent, "xl"))
     mine, sent = core_state([f_edge, f_far], f_mine, f_other, here, False)
     other = noted(swap(sent, "core"))

time: 271 us -> 260 us (0.959); the launches traced: 267 us -> 259 us
  waiting for transfers between devices: 138 us -> 131 us
    ppermute x8, waiting for transfers between devices: 92.8 us -> 61.4 us  [swap(): return lax.ppermute(array, axis, [(0, 1), (1, 0)])]
    all_to_all x4, waiting for transfers between devices: 44.3 us -> 69.4 us  [exchange(): return lax.all_to_all(array, axes, split_axis=0, concat_axis=0, tiled=True)]
  transfers between devices with their start and end apart: 14 -> 14, of which waited for: 8 -> 10; matrix products, arithmetic and copies ran while one was open for 1% -> 1% of each run, Pallas kernels for 21% -> 21%
where the time goes in v9:
time: 260 us; the launch traced here: 259 us
  waiting for transfers between devices  131 us (50%)
  Pallas kernels  59.3 us (23%)
  starting transfers between devices  31.9 us (12%)
  blocking collectives  18.5 us (7%)
  between operations  14.8 us (6%)
  local copies, waits for them, and re-layouts  2.83 us (1%)
    all_to_all x4, waiting for transfers between devices, exchange(): return lax.all_to_all(array, axes, split_axis=0, concat_axis=0, tiled=True)  69.4 us
    ppermute x8, waiting for transfers between devices, swap(): return lax.ppermute(array, axis, [(0, 1), (1, 0)])  61.4 us
    pallas_call x16, Pallas kernels, call(): pl.pallas_call(kernel, grid=grid, in_specs=in_specs, out_specs=out_specs,...  59.3 us
    all_to_all x4, starting transfers between devices, exchange(): return lax.all_to_all(array, axes, split_axis=0, concat_axis=0, tiled=True)  27.3 us
    unnamed x1, blocking collectives  18.5 us
  transfers between devices with their start and end apart: 14, of which 10 were waited for; matrix products, arithmetic and copies ran while one was open for 1% of the time, Pallas kernels for 21%

profile of v9, /device:TPU:32, one launch (start us, length us, event | category | flops | bytes accessed | tf_op | source)
XLA Modules:
  0.0 259.4 jit_solution(15785906577676404453)
XLA Ops:
  7.2 0.0 all-gather.7.cloned.1.call-start
  7.2 0.7 all-gather.7.cloned.1.call-update
  8.6 1.3 dynamic-slice
  9.8 0.8 dynamic-update-slice
  10.6 18.5 %all-reduce.exp_ref = s32[32]{0:T(128)S(1)} all-reduce(s32[32]{0:T(128)S(1)} %dynamic-update-slice), channel_id=1, replica_groups=mesh['y'=4,'xh'=2,'zh'=4,'zl'=2,'xl'=2,'core'=2] {'zh','zl','xl','core'}, use_global_device_ids=true, to_apply=%add | all-reduce | flops 32 | bytes 256
  29.1 0.7 fusion
  29.8 3.4 %updates.2 = (f32[8,2,128,128]{3,2,1,0:T(8,128)}, f32[8,2,128,128]{3,2,1,0:T(8,128)}) custom-call(s32[3]{0:T(128)S(1)} %get-tuple-element.55.here_ref, s32[32]{0:T(128)S(1)} %all-reduce.exp_ref, bf16[128,4096]{1,0:T(8,128)(2,1)} %bitcast.43, bf16[128,4096]{1,0:T(8,128)(2,1)} %bitcast.39), custom_call_target="tpu_custom_call" | custom-call | tf_op jit(solution)/shard_map/updates/pallas_call | solution.py:293
  33.2 0.0 collective-permute-start.1
  33.2 2.9 %collective-permute-done.1.other_ref = f32[8,2,128,128]{3,2,1,0:T(8,128)S(1)} collective-permute-done((f32[8,2,128,128]{3,2,1,0:T(8,128)}, f32[8,2,128,128]{3,2,1,0:T(8,128)S(1)}, u32[]{:S(2)}, u32[]{:S(2)}) %collective-permute-start.1) | collective-permute-done | bytes 1048608 | tf_op jit(solution)/shard_map/ppermute | solution.py:285
  36.0 2.1 pair.1.refs_0_
  38.1 4.5 %all-to-all-start = ((f32[16,128,128]{2,1,0:T(8,128)}), f32[16,128,128]{2,1,0:T(8,128)S(1)}, u32[]{:S(2)}, u32[]{:S(2)}) async-start(f32[16,128,128]{2,1,0:T(8,128)} %bitcast.37), calls=%async_computation | async-start | bytes 2097152 | tf_op jit(solution)/shard_map/all_to_all | solution.py:281
  42.7 3.4 %updates.3 = (f32[8,2,128,128]{3,2,1,0:T(8,128)}, f32[8,2,128,128]{3,2,1,0:T(8,128)}) custom-call(s32[3]{0:T(128)S(1)} %get-tuple-element.56.here_ref, s32[32]{0:T(128)S(1)} %all-reduce.exp_ref, bf16[128,4096]{1,0:T(8,128)(2,1)} %bitcast.28, bf16[128,4096]{1,0:T(8,128)(2,1)} %bitcast.32, f32[8,2,128,128]{3,2,1,0:T(8,128)} %get-tuple-element.30.refs_0_.mine_ref), custom_call_target="tpu_custom_call" | custom-call | tf_op jit(solution)/shard_map/updates/pallas_call | solution.py:293
  46.0 0.0 collective-permute-start
  46.0 2.9 %collective-permute-done.other_ref = f32[8,2,128,128]{3,2,1,0:T(8,128)S(1)} collective-permute-done((f32[8,2,128,128]{3,2,1,0:T(8,128)}, f32[8,2,128,128]{3,2,1,0:T(8,128)S(1)}, u32[]{:S(2)}, u32[]{:S(2)}) %collective-permute-start) | collective-permute-done | bytes 1048608 | tf_op jit(solution)/shard_map/ppermute | solution.py:285
  48.9 2.2 chip.1
  51.1 17.4 %all-to-all-done = f32[16,128,128]{2,1,0:T(8,128)S(1)} async-done(((f32[16,128,128]{2,1,0:T(8,128)}), f32[16,128,128]{2,1,0:T(8,128)S(1)}, u32[]{:S(2)}, u32[]{:S(2)}) %all-to-all-start) | async-done | bytes 1048608 | tf_op jit(solution)/shard_map/all_to_all | solution.py:281
  68.5 1.1 scan.1
  69.6 7.2 %all-to-all-start.1 = ((f32[16,128,128]{2,1,0:T(8,128)}), f32[16,128,128]{2,1,0:T(8,128)S(1)}, u32[]{:S(2)}, u32[]{:S(2)}) async-start(f32[16,128,128]{2,1,0:T(8,128)} %bitcast.38), calls=%async_computation.1 | async-start | bytes 2097152 | tf_op jit(solution)/shard_map/all_to_all | solution.py:281
  76.8 8.8 %inner.1 = (f32[128,4096]{1,0:T(8,128)}, f32[128,4096]{1,0:T(8,128)}) custom-call(s32[32]{0:T(128)S(1)} %all-reduce.exp_ref, bf16[128,4096]{1,0:T(8,128)(2,1)} %bitcast.44, bf16[128,4096]{1,0:T(8,128)(2,1)} %bitcast.29, bf16[128,4096]{1,0:T(8,128)(2,1)} %bitcast.33, bf16[128,4096]{1,0:T(8,128)(2,1)} %bitcast.40, f32[8,2,128,128]{3,2,1,0:T(8,128)} %get-tuple-element.36.after_ref), custom_call_target="tpu_custom_call" | custom-call | tf_op jit(solution)/shard_map/inner/pallas_call | solution.py:293
  85.6 15.8 %all-to-all-done.1 = f32[16,128,128]{2,1,0:T(8,128)S(1)} async-done(((f32[16,128,128]{2,1,0:T(8,128)}), f32[16,128,128]{2,1,0:T(8,128)S(1)}, u32[]{:S(2)}, u32[]{:S(2)}) %all-to-all-start.1) | async-done | bytes 1048608 | tf_op jit(solution)/shard_map/all_to_all | solution.py:281
  101.4 2.5 core_state.2
  103.9 0.0 collective-permute-start.4
  103.9 0.7 collective-permute-start.2
  104.6 25.2 %collective-permute-done.2.other_ref = f32[8,128,128]{2,1,0:T(8,128)S(1)} collective-permute-done((f32[8,128,128]{2,1,0:T(8,128)S(1)}, f32[8,128,128]{2,1,0:T(8,128)S(1)}, u32[]{:S(2)}, u32[]{:S(2)}) %collective-permute-start.2) | collective-permute-done | bytes 524320 | tf_op jit(solution)/shard_map/ppermute | solution.py:285
  129.8 1.9 line.1
  131.7 0.8 copy-done
  132.5 3.1 %collective-permute-start.3 = (f32[4,128,128]{2,1,0:T(8,128)}, f32[4,128,128]{2,1,0:T(8,128)S(1)}, u32[]{:S(2)}, u32[]{:S(2)}) collective-permute-start(f32[4,128,128]{2,1,0:T(8,128)} %get-tuple-element.38), channel_id=1, source_target_pairs={{0,4},{4,0},{1,5},{5,1},{2,6},{6,2},{3,7},{7,3},{8,12},{12,8},{9,1... | collective-permute-start | bytes 786440 | tf_op jit(solution)/shard_map/ppermute | solution.py:285
  135.6 0.0 collective-permute-done.4.other_ref
  135.6 5.2 %key_value.1 = (bf16[128,4096]{1,0:T(8,128)(2,1)}, bf16[128,4096]{1,0:T(8,128)(2,1)}, bf16[8,4,128,256]{3,2,1,0:T(8,128)(2,1)}) custom-call(s32[3]{0:T(128)S(1)} %get-tuple-element.55.here_ref, s32[32]{0:T(128)S(1)} %all-reduce.exp_ref, bf16[128,4096]{1,0:T(8,128)(2,1)} %bitcast.30, bf16[128,4096]{1,0:T(8,128)(2,1)} %bitcast.34, ...), custom_call_target="tpu_custom_call" | custom-call | tf_op jit(solution)/shard_map/key_value/pallas_call | solution.py:293
  140.9 7.0 %all-to-all-start.2 = ((bf16[32,128,256]{2,1,0:T(8,128)(2,1)}), bf16[32,128,256]{2,1,0:T(8,128)(2,1)S(1)}, u32[]{:S(2)}, u32[]{:S(2)}) async-start(bf16[32,128,256]{2,1,0:T(8,128)(2,1)} %bitcast.42), calls=%async_computation.2 | async-start | bytes 4194304 | tf_op jit(solution)/shard_map/all_to_all | solution.py:281
  147.9 0.0 all-gather.5.cloned.1.call-start
  148.0 1.7 line_pair.1
  149.7 0.0 all-gather.5.cloned.1.call-update
  149.7 28.2 %all-to-all-done.2 = bf16[32,128,256]{2,1,0:T(8,128)(2,1)S(1)} async-done(((bf16[32,128,256]{2,1,0:T(8,128)(2,1)}), bf16[32,128,256]{2,1,0:T(8,128)(2,1)S(1)}, u32[]{:S(2)}, u32[]{:S(2)}) %all-to-all-start.2) | async-done | bytes 2097184 | tf_op jit(solution)/shard_map/all_to_all | solution.py:281
  177.9 13.1 %weight.1.after_ref = bf16[8,8,96,128]{3,2,1,0:T(8,128)(2,1)} custom-call(bf16[4096,256]{1,0:T(8,128)(2,1)S(1)} %bitcast.23, bf16[4096,3072]{1,0:T(8,128)(2,1)} %bitcast.27), custom_call_target="tpu_custom_call" | custom-call | tf_op jit(solution)/shard_map/weight/pallas_call | solution.py:293
  191.0 2.4 edge.1
  193.3 0.0 collective-permute-start.5
  193.4 6.6 %collective-permute-done.5.other_edge_ref = f32[4,128,128]{2,1,0:T(8,128)S(1)} collective-permute-done((f32[4,128,128]{2,1,0:T(8,128)}, f32[4,128,128]{2,1,0:T(8,128)S(1)}, u32[]{:S(2)}, u32[]{:S(2)}) %collective-permute-start.5) | collective-permute-done | bytes 262176 | tf_op jit(solution)/shard_map/ppermute | solution.py:285
  200.0 2.3 chip_state.1
  202.2 8.5 %all-to-all-start.3 = ((bf16[64,96,128]{2,1,0:T(8,128)(2,1)}), bf16[64,96,128]{2,1,0:T(8,128)(2,1)S(1)}, u32[]{:S(2)}, u32[]{:S(2)}) async-start(bf16[64,96,128]{2,1,0:T(8,128)(2,1)} %bitcast.36), calls=%async_computation.3 | async-start | bytes 3145728 | tf_op jit(solution)/shard_map/all_to_all | solution.py:281
  210.8 0.7 collective-permute-start.6
  211.4 21.0 %collective-permute-done.6.refs_1_ = f32[8,128,128]{2,1,0:T(8,128)S(1)} collective-permute-done((f32[8,128,128]{2,1,0:T(8,128)S(1)}, f32[8,128,128]{2,1,0:T(8,128)S(1)}, u32[]{:S(2)}, u32[]{:S(2)}) %collective-permute-start.6) | collective-permute-done | bytes 524320 | tf_op jit(solution)/shard_map/ppermute | solution.py:285
  232.4 2.6 core_state.3
  235.0 0.0 collective-permute-start.7
  235.0 2.9 %collective-permute-done.7.other_ref = f32[8,2,128,128]{3,2,1,0:T(8,128)S(1)} collective-permute-done((f32[8,2,128,128]{3,2,1,0:T(8,128)}, f32[8,2,128,128]{3,2,1,0:T(8,128)S(1)}, u32[]{:S(2)}, u32[]{:S(2)}) %collective-permute-start.7) | collective-permute-done | bytes 1048608 | tf_op jit(solution)/shard_map/ppermute | solution.py:285
  237.9 5.8 %query.1 = bf16[128,4096]{1,0:T(8,128)(2,1)} custom-call(s32[3]{0:T(128)S(1)} %get-tuple-element.56.here_ref, s32[32]{0:T(128)S(1)} %all-reduce.exp_ref, bf16[128,4096]{1,0:T(8,128)(2,1)} %bitcast.31, bf16[128,4096]{1,0:T(8,128)(2,1)} %bitcast.35, bf16[128,4096]{1,0:T(8,128)(2,1)} %bitcast.41, f32[8,2,128,128]{3,2,1,0:T(8,128)} %get-tuple-element.49.mine_ref, ...), custom_call_target="tpu_custom_call" | custom-call | tf_op jit(solution)/shard_map/query/pallas_call | solution.py:293
  243.7 8.0 %all-to-all-done.3 = bf16[64,96,128]{2,1,0:T(8,128)(2,1)S(1)} async-done(((bf16[64,96,128]{2,1,0:T(8,128)(2,1)}), bf16[64,96,128]{2,1,0:T(8,128)(2,1)S(1)}, u32[]{:S(2)}, u32[]{:S(2)}) %all-to-all-start.3) | async-done | bytes 1572896 | tf_op jit(solution)/shard_map/all_to_all | solution.py:281
  251.7 0.9 total.1
  (11 shorter events, 0.0 us)
Async XLA Ops:
  7.2 170.7 %all-gather.7.cloned.1.call-start = ((), (), s32[]{:S(2)}) async-start(), calls=%async_computation.5 | async-start | bytes 25952256 | tf_op jit(solution)/shard_map/all_gather | solution.py:314
  33.2 2.9 %collective-permute-start.1 = (f32[8,2,128,128]{3,2,1,0:T(8,128)}, f32[8,2,128,128]{3,2,1,0:T(8,128)S(1)}, u32[]{:S(2)}, u32[]{:S(2)}) collective-permute-start(f32[8,2,128,128]{3,2,1,0:T(8,128)} %get-tuple-element.33), channel_id=1, source_target_pairs={{0,1},{1,0},{2,3},{3,2},{4,5},{5,4},{6,7},{7,6},{8,9},{9,8},{10,11... | collective-permute-start | bytes 3145736 | tf_op jit(solution)/shard_map/ppermute | solution.py:285
  38.1 30.4 %all-to-all-start = ((f32[16,128,128]{2,1,0:T(8,128)}), f32[16,128,128]{2,1,0:T(8,128)S(1)}, u32[]{:S(2)}, u32[]{:S(2)}) async-start(f32[16,128,128]{2,1,0:T(8,128)} %bitcast.37), calls=%async_computation | async-start | bytes 2097152 | tf_op jit(solution)/shard_map/all_to_all | solution.py:281
  46.0 2.9 %collective-permute-start = (f32[8,2,128,128]{3,2,1,0:T(8,128)}, f32[8,2,128,128]{3,2,1,0:T(8,128)S(1)}, u32[]{:S(2)}, u32[]{:S(2)}) collective-permute-start(f32[8,2,128,128]{3,2,1,0:T(8,128)} %get-tuple-element.32), channel_id=1, source_target_pairs={{0,1},{1,0},{2,3},{3,2},{4,5},{5,4},{6,7},{7,6},{8,9},{9,8},{10,11... | collective-permute-start | bytes 3145736 | tf_op jit(solution)/shard_map/ppermute | solution.py:285
  69.6 31.8 %all-to-all-start.1 = ((f32[16,128,128]{2,1,0:T(8,128)}), f32[16,128,128]{2,1,0:T(8,128)S(1)}, u32[]{:S(2)}, u32[]{:S(2)}) async-start(f32[16,128,128]{2,1,0:T(8,128)} %bitcast.38), calls=%async_computation.1 | async-start | bytes 2097152 | tf_op jit(solution)/shard_map/all_to_all | solution.py:281
  101.4 2.6 copy-start.2
  103.9 31.7 %collective-permute-start.4 = (f32[8,2,128,128]{3,2,1,0:T(8,128)}, f32[8,2,128,128]{3,2,1,0:T(8,128)S(1)}, u32[]{:S(2)}, u32[]{:S(2)}) collective-permute-start(f32[8,2,128,128]{3,2,1,0:T(8,128)} %get-tuple-element.42), channel_id=1, source_target_pairs={{0,1},{1,0},{2,3},{3,2},{4,5},{5,4},{6,7},{7,6},{8,9},{9,8},{10,11... | collective-permute-start | bytes 3145736 | tf_op jit(solution)/shard_map/ppermute | solution.py:285
  103.9 25.9 %collective-permute-start.2 = (f32[8,128,128]{2,1,0:T(8,128)S(1)}, f32[8,128,128]{2,1,0:T(8,128)S(1)}, u32[]{:S(2)}, u32[]{:S(2)}) collective-permute-start(f32[8,128,128]{2,1,0:T(8,128)S(1)} %copy-done.2), channel_id=1, source_target_pairs={{0,2},{2,0},{1,3},{3,1},{4,6},{6,4},{5,7},{7,5},{8,10},{10,8},{9,1... | collective-permute-start | bytes 1572872 | tf_op jit(solution)/shard_map/ppermute | solution.py:285
  131.7 0.8 copy-start
  132.5 15.5 %collective-permute-start.3 = (f32[4,128,128]{2,1,0:T(8,128)}, f32[4,128,128]{2,1,0:T(8,128)S(1)}, u32[]{:S(2)}, u32[]{:S(2)}) collective-permute-start(f32[4,128,128]{2,1,0:T(8,128)} %get-tuple-element.38), channel_id=1, source_target_pairs={{0,4},{4,0},{1,5},{5,1},{2,6},{6,2},{3,7},{7,3},{8,12},{12,8},{9,1... | collective-permute-start | bytes 786440 | tf_op jit(solution)/shard_map/ppermute | solution.py:285
  140.9 37.0 %all-to-all-start.2 = ((bf16[32,128,256]{2,1,0:T(8,128)(2,1)}), bf16[32,128,256]{2,1,0:T(8,128)(2,1)S(1)}, u32[]{:S(2)}, u32[]{:S(2)}) async-start(bf16[32,128,256]{2,1,0:T(8,128)(2,1)} %bitcast.42), calls=%async_computation.2 | async-start | bytes 4194304 | tf_op jit(solution)/shard_map/all_to_all | solution.py:281
  147.9 43.1 %all-gather.5.cloned.1.call-start = ((), (), s32[]{:S(2)}) async-start(), calls=%async_computation.4 | async-start | bytes 1638400 | tf_op jit(solution)/shard_map/all_gather | solution.py:419
  191.0 9.0 %copy-start.1 = (f32[8,128,128]{2,1,0:T(8,128)S(1)}, f32[8,128,128]{2,1,0:T(8,128)}, u32[]{:S(2)}) copy-start(f32[8,128,128]{2,1,0:T(8,128)} %copy-done) | copy-start | bytes 1572868
  193.3 6.6 %collective-permute-start.5 = (f32[4,128,128]{2,1,0:T(8,128)}, f32[4,128,128]{2,1,0:T(8,128)S(1)}, u32[]{:S(2)}, u32[]{:S(2)}) collective-permute-start(f32[4,128,128]{2,1,0:T(8,128)} %get-tuple-element.45), channel_id=1, source_target_pairs={{0,4},{4,0},{1,5},{5,1},{2,6},{6,2},{3,7},{7,3},{8,12},{12,8},{9,1... | collective-permute-start | bytes 786440 | tf_op jit(solution)/shard_map/ppermute | solution.py:285
  202.2 8.5 %copy-start.3 = (f32[8,128,128]{2,1,0:T(8,128)S(1)}, f32[8,128,128]{2,1,0:T(8,128)}, u32[]{:S(2)}) copy-start(f32[8,128,128]{2,1,0:T(8,128)} %get-tuple-element.48) | copy-start | bytes 1572868
  202.2 49.5 %all-to-all-start.3 = ((bf16[64,96,128]{2,1,0:T(8,128)(2,1)}), bf16[64,96,128]{2,1,0:T(8,128)(2,1)S(1)}, u32[]{:S(2)}, u32[]{:S(2)}) async-start(bf16[64,96,128]{2,1,0:T(8,128)(2,1)} %bitcast.36), calls=%async_computation.3 | async-start | bytes 3145728 | tf_op jit(solution)/shard_map/all_to_all | solution.py:281
  210.8 21.7 %collective-permute-start.6 = (f32[8,128,128]{2,1,0:T(8,128)S(1)}, f32[8,128,128]{2,1,0:T(8,128)S(1)}, u32[]{:S(2)}, u32[]{:S(2)}) collective-permute-start(f32[8,128,128]{2,1,0:T(8,128)S(1)} %copy-done.3), channel_id=1, source_target_pairs={{0,2},{2,0},{1,3},{3,1},{4,6},{6,4},{5,7},{7,5},{8,10},{10,8},{9,1... | collective-permute-start | bytes 1572872 | tf_op jit(solution)/shard_map/ppermute | solution.py:285
  235.0 2.9 %collective-permute-start.7 = (f32[8,2,128,128]{3,2,1,0:T(8,128)}, f32[8,2,128,128]{3,2,1,0:T(8,128)S(1)}, u32[]{:S(2)}, u32[]{:S(2)}) collective-permute-start(f32[8,2,128,128]{3,2,1,0:T(8,128)} %get-tuple-element.50), channel_id=1, source_target_pairs={{0,1},{1,0},{2,3},{3,2},{4,5},{5,4},{6,7},{7,6},{8,9},{9,8},{10,11... | collective-permute-start | bytes 3145736 | tf_op jit(solution)/shard_map/ppermute | solution.py:285
Sparse Core Ops, SparseCore 0:
  10.5 128.8 all-gather.6
  151.1 34.4 all-gather.4

commit v10 on v9

--- a/solution.py
+++ b/solution.py
@@ -191,7 +191,8 @@
 
 
 def inner_kernel(
-    exp_ref, query_ref, key_ref, value_ref, grad_ref, after_ref, gk_ref, gv_ref, *, length
+    exp_ref, query_ref, key_ref, value_ref, grad_ref, next_ref, after_ref, gk_ref, gv_ref,
+    *, length
 ):
     span = query_ref.shape[0]
     source = lax.broadcasted_iota(jnp.int32, (span, span), 0)
@@ -394,8 +395,9 @@
     )
     f_beside = noted(swap(sent, "zl"))
     inner_gk, inner_gv = run(
-        inner_kernel, (2,), [SMEM] + 4 * [head_cols], 2 * [head_cols], 2 * [inner_shape],
-        (exps, query, key, value, grad), r_edges, name="inner",
+        inner_kernel, (2,), [SMEM] + 4 * [head_cols] + [FREE], 2 * [head_cols],
+        2 * [inner_shape],
+        (exps, query, key, value, grad, f_next), r_edges, name="inner",
     )
     r_edges = exchange(r_edges.reshape((2 * groups,) + tile), CHIPS)
     r_edges = noted(r_edges.reshape((groups, 2) + tile))

time: 260 us -> 257 us (0.988)
  waiting for transfers between devices: 131 us -> 126 us
    all_to_all x4, waiting for transfers between devices: 69.4 us -> 52.6 us  [exchange(): return lax.all_to_all(array, axes, split_axis=0, concat_axis=0, tiled=True)]
    ppermute x8, waiting for transfers between devices: 61.4 us -> 72.8 us  [swap(): return lax.ppermute(array, axis, [(0, 1), (1, 0)])]
    all_to_all x4, starting transfers between devices: 27.3 us -> 30 us  [exchange(): return lax.all_to_all(array, axes, split_axis=0, concat_axis=0, tiled=True)]
where the time goes in v10:
time: 257 us; the launch traced here: 256 us
  waiting for transfers between devices  126 us (49%)
  Pallas kernels  59.6 us (23%)
  starting transfers between devices  33.6 us (13%)
  blocking collectives  18.5 us (7%)
  between operations  14.8 us (6%)
  local copies, waits for them, and re-layouts  3.04 us (1%)
    ppermute x8, waiting for transfers between devices, swap(): return lax.ppermute(array, axis, [(0, 1), (1, 0)])  72.8 us
    pallas_call x16, Pallas kernels, call(): pl.pallas_call(kernel, grid=grid, in_specs=in_specs, out_specs=out_specs,...  59.6 us
    all_to_all x4, waiting for transfers between devices, exchange(): return lax.all_to_all(array, axes, split_axis=0, concat_axis=0, tiled=True)  52.6 us
    all_to_all x4, starting transfers between devices, exchange(): return lax.all_to_all(array, axes, split_axis=0, concat_axis=0, tiled=True)  30 us
    unnamed x1, blocking collectives  18.5 us
  transfers between devices with their start and end apart: 14, of which 10 were waited for; matrix products, arithmetic and copies ran while one was open for 1% of the time, Pallas kernels for 21%

profile of v10, /device:TPU:32, one launch (start us, length us, event | category | flops | bytes accessed | tf_op | source)
XLA Modules:
  0.0 256.4 jit_solution(15535044650566290001)
XLA Ops:
  7.2 0.0 all-gather.7.cloned.1.call-start
  7.2 0.7 all-gather.7.cloned.1.call-update
  8.6 1.3 dynamic-slice
  9.8 0.8 dynamic-update-slice
  10.6 18.5 %all-reduce.exp_ref = s32[32]{0:T(128)S(1)} all-reduce(s32[32]{0:T(128)S(1)} %dynamic-update-slice), channel_id=1, replica_groups=mesh['y'=4,'xh'=2,'zh'=4,'zl'=2,'xl'=2,'core'=2] {'zh','zl','xl','core'}, use_global_device_ids=true, to_apply=%add | all-reduce | flops 32 | bytes 256
  29.1 0.7 fusion
  29.8 3.3 %updates.2 = (f32[8,2,128,128]{3,2,1,0:T(8,128)}, f32[8,2,128,128]{3,2,1,0:T(8,128)}) custom-call(s32[3]{0:T(128)S(1)} %get-tuple-element.55.here_ref, s32[32]{0:T(128)S(1)} %all-reduce.exp_ref, bf16[128,4096]{1,0:T(8,128)(2,1)} %bitcast.43, bf16[128,4096]{1,0:T(8,128)(2,1)} %bitcast.39), custom_call_target="tpu_custom_call" | custom-call | tf_op jit(solution)/shard_map/updates/pallas_call | solution.py:294
  33.1 2.9 %collective-permute-done.1.other_ref = f32[8,2,128,128]{3,2,1,0:T(8,128)S(1)} collective-permute-done((f32[8,2,128,128]{3,2,1,0:T(8,128)}, f32[8,2,128,128]{3,2,1,0:T(8,128)S(1)}, u32[]{:S(2)}, u32[]{:S(2)}) %collective-permute-start.1) | collective-permute-done | bytes 1048608 | tf_op jit(solution)/shard_map/ppermute | solution.py:286
  36.0 2.1 pair.1.refs_0_
  38.1 4.5 %all-to-all-start = ((f32[16,128,128]{2,1,0:T(8,128)}), f32[16,128,128]{2,1,0:T(8,128)S(1)}, u32[]{:S(2)}, u32[]{:S(2)}) async-start(f32[16,128,128]{2,1,0:T(8,128)} %bitcast.37), calls=%async_computation | async-start | bytes 2097152 | tf_op jit(solution)/shard_map/all_to_all | solution.py:282
  42.6 3.4 %updates.3 = (f32[8,2,128,128]{3,2,1,0:T(8,128)}, f32[8,2,128,128]{3,2,1,0:T(8,128)}) custom-call(s32[3]{0:T(128)S(1)} %get-tuple-element.56.here_ref, s32[32]{0:T(128)S(1)} %all-reduce.exp_ref, bf16[128,4096]{1,0:T(8,128)(2,1)} %bitcast.28, bf16[128,4096]{1,0:T(8,128)(2,1)} %bitcast.32, f32[8,2,128,128]{3,2,1,0:T(8,128)} %get-tuple-element.30.refs_0_.mine_ref), custom_call_target="tpu_custom_call" | custom-call | tf_op jit(solution)/shard_map/updates/pallas_call | solution.py:294
  46.0 0.0 collective-permute-start
  46.0 2.9 %collective-permute-done.other_ref = f32[8,2,128,128]{3,2,1,0:T(8,128)S(1)} collective-permute-done((f32[8,2,128,128]{3,2,1,0:T(8,128)}, f32[8,2,128,128]{3,2,1,0:T(8,128)S(1)}, u32[]{:S(2)}, u32[]{:S(2)}) %collective-permute-start) | collective-permute-done | bytes 1048608 | tf_op jit(solution)/shard_map/ppermute | solution.py:286
  48.9 2.1 chip.1
  51.0 1.0 copy-done
  52.0 16.5 %all-to-all-done = f32[16,128,128]{2,1,0:T(8,128)S(1)} async-done(((f32[16,128,128]{2,1,0:T(8,128)}), f32[16,128,128]{2,1,0:T(8,128)S(1)}, u32[]{:S(2)}, u32[]{:S(2)}) %all-to-all-start) | async-done | bytes 1048608 | tf_op jit(solution)/shard_map/all_to_all | solution.py:282
  68.5 1.1 scan.1
  69.5 7.2 %all-to-all-start.1 = ((f32[16,128,128]{2,1,0:T(8,128)}), f32[16,128,128]{2,1,0:T(8,128)S(1)}, u32[]{:S(2)}, u32[]{:S(2)}) async-start(f32[16,128,128]{2,1,0:T(8,128)} %bitcast.38), calls=%async_computation.1 | async-start | bytes 2097152 | tf_op jit(solution)/shard_map/all_to_all | solution.py:282
  76.7 1.6 collective-permute-start.2
  78.3 36.0 %collective-permute-done.2.other_ref.next_ref = f32[8,128,128]{2,1,0:T(8,128)S(1)} collective-permute-done((f32[8,128,128]{2,1,0:T(8,128)S(1)}, f32[8,128,128]{2,1,0:T(8,128)S(1)}, u32[]{:S(2)}, u32[]{:S(2)}) %collective-permute-start.2) | collective-permute-done | bytes 524320 | tf_op jit(solution)/shard_map/ppermute | solution.py:286
  114.3 8.8 %inner.1 = (f32[128,4096]{1,0:T(8,128)}, f32[128,4096]{1,0:T(8,128)}) custom-call(s32[32]{0:T(128)S(1)} %all-reduce.exp_ref, bf16[128,4096]{1,0:T(8,128)(2,1)} %bitcast.44, bf16[128,4096]{1,0:T(8,128)(2,1)} %bitcast.29, bf16[128,4096]{1,0:T(8,128)(2,1)} %bitcast.33, bf16[128,4096]{1,0:T(8,128)(2,1)} %bitcast.40, ...), custom_call_target="tpu_custom_call" | custom-call | tf_op jit(solution)/shard_map/inner/pallas_call | solution.py:294
  123.1 0.0 all-to-all-done.1
  123.1 2.5 core_state.2
  125.6 0.0 collective-permute-start.4
  125.6 2.0 line.1
  127.7 0.5 collective-permute-start.3
  128.1 1.0 collective-permute-done.4.other_ref
  129.1 5.5 %key_value.1 = (bf16[128,4096]{1,0:T(8,128)(2,1)}, bf16[128,4096]{1,0:T(8,128)(2,1)}, bf16[8,4,128,256]{3,2,1,0:T(8,128)(2,1)}) custom-call(s32[3]{0:T(128)S(1)} %get-tuple-element.55.here_ref, s32[32]{0:T(128)S(1)} %all-reduce.exp_ref, bf16[128,4096]{1,0:T(8,128)(2,1)} %bitcast.30, bf16[128,4096]{1,0:T(8,128)(2,1)} %bitcast.34, ...), custom_call_target="tpu_custom_call" | custom-call | tf_op jit(solution)/shard_map/key_value/pallas_call | solution.py:294
  134.6 6.9 %all-to-all-start.2 = ((bf16[32,128,256]{2,1,0:T(8,128)(2,1)}), bf16[32,128,256]{2,1,0:T(8,128)(2,1)S(1)}, u32[]{:S(2)}, u32[]{:S(2)}) async-start(bf16[32,128,256]{2,1,0:T(8,128)(2,1)} %bitcast.42), calls=%async_computation.2 | async-start | bytes 4194304 | tf_op jit(solution)/shard_map/all_to_all | solution.py:282
  141.5 0.0 all-gather.5.cloned.1.call-start
  141.6 0.0 collective-permute-done.3.other_ref
  141.6 1.7 line_pair.1
  143.3 0.0 all-gather.5.cloned.1.call-update
  143.3 28.2 %all-to-all-done.2 = bf16[32,128,256]{2,1,0:T(8,128)(2,1)S(1)} async-done(((bf16[32,128,256]{2,1,0:T(8,128)(2,1)}), bf16[32,128,256]{2,1,0:T(8,128)(2,1)S(1)}, u32[]{:S(2)}, u32[]{:S(2)}) %all-to-all-start.2) | async-done | bytes 2097184 | tf_op jit(solution)/shard_map/all_to_all | solution.py:282
  171.5 13.1 %weight.1.after_ref = bf16[8,8,96,128]{3,2,1,0:T(8,128)(2,1)} custom-call(bf16[4096,256]{1,0:T(8,128)(2,1)S(1)} %bitcast.23, bf16[4096,3072]{1,0:T(8,128)(2,1)} %bitcast.27), custom_call_target="tpu_custom_call" | custom-call | tf_op jit(solution)/shard_map/weight/pallas_call | solution.py:294
  184.6 2.3 edge.1
  187.0 0.9 collective-permute-start.5
  187.8 6.3 %collective-permute-done.5.other_edge_ref = f32[4,128,128]{2,1,0:T(8,128)S(1)} collective-permute-done((f32[4,128,128]{2,1,0:T(8,128)}, f32[4,128,128]{2,1,0:T(8,128)S(1)}, u32[]{:S(2)}, u32[]{:S(2)}) %collective-permute-start.5) | collective-permute-done | bytes 262176 | tf_op jit(solution)/shard_map/ppermute | solution.py:286
  194.1 2.2 chip_state.1
  196.4 11.4 %all-to-all-start.3 = ((bf16[64,96,128]{2,1,0:T(8,128)(2,1)}), bf16[64,96,128]{2,1,0:T(8,128)(2,1)S(1)}, u32[]{:S(2)}, u32[]{:S(2)}) async-start(bf16[64,96,128]{2,1,0:T(8,128)(2,1)} %bitcast.36), calls=%async_computation.3 | async-start | bytes 3145728 | tf_op jit(solution)/shard_map/all_to_all | solution.py:282
  207.7 0.7 collective-permute-start.6
  208.4 21.0 %collective-permute-done.6.refs_1_ = f32[8,128,128]{2,1,0:T(8,128)S(1)} collective-permute-done((f32[8,128,128]{2,1,0:T(8,128)S(1)}, f32[8,128,128]{2,1,0:T(8,128)S(1)}, u32[]{:S(2)}, u32[]{:S(2)}) %collective-permute-start.6) | collective-permute-done | bytes 524320 | tf_op jit(solution)/shard_map/ppermute | solution.py:286
  229.4 2.6 %core_state.3 = (f32[8,2,128,128]{3,2,1,0:T(8,128)}, f32[8,2,128,128]{3,2,1,0:T(8,128)}) custom-call(s32[3]{0:T(128)S(1)} %get-tuple-element.56.here_ref, s32[32]{0:T(128)S(1)} %all-reduce.exp_ref, f32[8,2,128,128]{3,2,1,0:T(8,128)} %get-tuple-element.31.mine_ref, f32[8,2,128,128]{3,2,1,0:T(8,128)S(1)} %copy-done.1, ...), custom_call_target="tpu_custom_call" | custom-call | tf_op jit(solution)/shard_map/core_state/pallas_call | solution.py:294
  232.0 0.0 collective-permute-start.7
  232.0 2.9 %collective-permute-done.7.other_ref = f32[8,2,128,128]{3,2,1,0:T(8,128)S(1)} collective-permute-done((f32[8,2,128,128]{3,2,1,0:T(8,128)}, f32[8,2,128,128]{3,2,1,0:T(8,128)S(1)}, u32[]{:S(2)}, u32[]{:S(2)}) %collective-permute-start.7) | collective-permute-done | bytes 1048608 | tf_op jit(solution)/shard_map/ppermute | solution.py:286
  234.9 5.8 %query.1 = bf16[128,4096]{1,0:T(8,128)(2,1)} custom-call(s32[3]{0:T(128)S(1)} %get-tuple-element.56.here_ref, s32[32]{0:T(128)S(1)} %all-reduce.exp_ref, bf16[128,4096]{1,0:T(8,128)(2,1)} %bitcast.31, bf16[128,4096]{1,0:T(8,128)(2,1)} %bitcast.35, bf16[128,4096]{1,0:T(8,128)(2,1)} %bitcast.41, f32[8,2,128,128]{3,2,1,0:T(8,128)} %get-tuple-element.49.mine_ref, ...), custom_call_target="tpu_custom_call" | custom-call | tf_op jit(solution)/shard_map/query/pallas_call | solution.py:294
  240.7 8.0 %all-to-all-done.3 = bf16[64,96,128]{2,1,0:T(8,128)(2,1)S(1)} async-done(((bf16[64,96,128]{2,1,0:T(8,128)(2,1)}), bf16[64,96,128]{2,1,0:T(8,128)(2,1)S(1)}, u32[]{:S(2)}, u32[]{:S(2)}) %all-to-all-start.3) | async-done | bytes 1572896 | tf_op jit(solution)/shard_map/all_to_all | solution.py:282
  248.7 0.9 total.1
  (11 shorter events, 0.0 us)
Async XLA Ops:
  7.2 164.3 %all-gather.7.cloned.1.call-start = ((), (), s32[]{:S(2)}) async-start(), calls=%async_computation.5 | async-start | bytes 25952256 | tf_op jit(solution)/shard_map/all_gather | solution.py:315
  33.1 2.9 %collective-permute-start.1 = (f32[8,2,128,128]{3,2,1,0:T(8,128)}, f32[8,2,128,128]{3,2,1,0:T(8,128)S(1)}, u32[]{:S(2)}, u32[]{:S(2)}) collective-permute-start(f32[8,2,128,128]{3,2,1,0:T(8,128)} %get-tuple-element.33), channel_id=1, source_target_pairs={{0,1},{1,0},{2,3},{3,2},{4,5},{5,4},{6,7},{7,6},{8,9},{9,8},{10,11... | collective-permute-start | bytes 3145736 | tf_op jit(solution)/shard_map/ppermute | solution.py:286
  38.1 30.4 %all-to-all-start = ((f32[16,128,128]{2,1,0:T(8,128)}), f32[16,128,128]{2,1,0:T(8,128)S(1)}, u32[]{:S(2)}, u32[]{:S(2)}) async-start(f32[16,128,128]{2,1,0:T(8,128)} %bitcast.37), calls=%async_computation | async-start | bytes 2097152 | tf_op jit(solution)/shard_map/all_to_all | solution.py:282
  46.0 2.9 %collective-permute-start = (f32[8,2,128,128]{3,2,1,0:T(8,128)}, f32[8,2,128,128]{3,2,1,0:T(8,128)S(1)}, u32[]{:S(2)}, u32[]{:S(2)}) collective-permute-start(f32[8,2,128,128]{3,2,1,0:T(8,128)} %get-tuple-element.32), channel_id=1, source_target_pairs={{0,1},{1,0},{2,3},{3,2},{4,5},{5,4},{6,7},{7,6},{8,9},{9,8},{10,11... | collective-permute-start | bytes 3145736 | tf_op jit(solution)/shard_map/ppermute | solution.py:286
  51.0 1.0 copy-start
  52.0 24.8 %copy-start.2 = (f32[8,128,128]{2,1,0:T(8,128)S(1)}, f32[8,128,128]{2,1,0:T(8,128)}, u32[]{:S(2)}) copy-start(f32[8,128,128]{2,1,0:T(8,128)} %get-tuple-element.35) | copy-start | bytes 1572868
  69.5 53.5 %all-to-all-start.1 = ((f32[16,128,128]{2,1,0:T(8,128)}), f32[16,128,128]{2,1,0:T(8,128)S(1)}, u32[]{:S(2)}, u32[]{:S(2)}) async-start(f32[16,128,128]{2,1,0:T(8,128)} %bitcast.38), calls=%async_computation.1 | async-start | bytes 2097152 | tf_op jit(solution)/shard_map/all_to_all | solution.py:282
  76.7 37.6 %collective-permute-start.2 = (f32[8,128,128]{2,1,0:T(8,128)S(1)}, f32[8,128,128]{2,1,0:T(8,128)S(1)}, u32[]{:S(2)}, u32[]{:S(2)}) collective-permute-start(f32[8,128,128]{2,1,0:T(8,128)S(1)} %copy-done.2), channel_id=1, source_target_pairs={{0,2},{2,0},{1,3},{3,1},{4,6},{6,4},{5,7},{7,5},{8,10},{10,8},{9,1... | collective-permute-start | bytes 1572872 | tf_op jit(solution)/shard_map/ppermute | solution.py:286
  125.6 3.5 %collective-permute-start.4 = (f32[8,2,128,128]{3,2,1,0:T(8,128)}, f32[8,2,128,128]{3,2,1,0:T(8,128)S(1)}, u32[]{:S(2)}, u32[]{:S(2)}) collective-permute-start(f32[8,2,128,128]{3,2,1,0:T(8,128)} %get-tuple-element.42), channel_id=1, source_target_pairs={{0,1},{1,0},{2,3},{3,2},{4,5},{5,4},{6,7},{7,6},{8,9},{9,8},{10,11... | collective-permute-start | bytes 3145736 | tf_op jit(solution)/shard_map/ppermute | solution.py:286
  127.7 13.9 %collective-permute-start.3 = (f32[4,128,128]{2,1,0:T(8,128)}, f32[4,128,128]{2,1,0:T(8,128)S(1)}, u32[]{:S(2)}, u32[]{:S(2)}) collective-permute-start(f32[4,128,128]{2,1,0:T(8,128)} %get-tuple-element.38), channel_id=1, source_target_pairs={{0,4},{4,0},{1,5},{5,1},{2,6},{6,2},{3,7},{7,3},{8,12},{12,8},{9,1... | collective-permute-start | bytes 786440 | tf_op jit(solution)/shard_map/ppermute | solution.py:286
  134.6 36.9 %all-to-all-start.2 = ((bf16[32,128,256]{2,1,0:T(8,128)(2,1)}), bf16[32,128,256]{2,1,0:T(8,128)(2,1)S(1)}, u32[]{:S(2)}, u32[]{:S(2)}) async-start(bf16[32,128,256]{2,1,0:T(8,128)(2,1)} %bitcast.42), calls=%async_computation.2 | async-start | bytes 4194304 | tf_op jit(solution)/shard_map/all_to_all | solution.py:282
  141.5 43.1 %all-gather.5.cloned.1.call-start = ((), (), s32[]{:S(2)}) async-start(), calls=%async_computation.4 | async-start | bytes 1638400 | tf_op jit(solution)/shard_map/all_gather | solution.py:421
  187.0 7.2 %collective-permute-start.5 = (f32[4,128,128]{2,1,0:T(8,128)}, f32[4,128,128]{2,1,0:T(8,128)S(1)}, u32[]{:S(2)}, u32[]{:S(2)}) collective-permute-start(f32[4,128,128]{2,1,0:T(8,128)} %get-tuple-element.45), channel_id=1, source_target_pairs={{0,4},{4,0},{1,5},{5,1},{2,6},{6,2},{3,7},{7,3},{8,12},{12,8},{9,1... | collective-permute-start | bytes 786440 | tf_op jit(solution)/shard_map/ppermute | solution.py:286
  196.4 11.4 %copy-start.3 = (f32[8,128,128]{2,1,0:T(8,128)S(1)}, f32[8,128,128]{2,1,0:T(8,128)}, u32[]{:S(2)}) copy-start(f32[8,128,128]{2,1,0:T(8,128)} %get-tuple-element.48) | copy-start | bytes 1572868
  196.4 33.0 %copy-start.1 = (f32[8,2,128,128]{3,2,1,0:T(8,128)S(1)}, f32[8,2,128,128]{3,2,1,0:T(8,128)}, u32[]{:S(2)}) copy-start(f32[8,2,128,128]{3,2,1,0:T(8,128)} %copy-done) | copy-start | bytes 3145732
  196.4 52.3 %all-to-all-start.3 = ((bf16[64,96,128]{2,1,0:T(8,128)(2,1)}), bf16[64,96,128]{2,1,0:T(8,128)(2,1)S(1)}, u32[]{:S(2)}, u32[]{:S(2)}) async-start(bf16[64,96,128]{2,1,0:T(8,128)(2,1)} %bitcast.36), calls=%async_computation.3 | async-start | bytes 3145728 | tf_op jit(solution)/shard_map/all_to_all | solution.py:282
  207.7 21.7 %collective-permute-start.6 = (f32[8,128,128]{2,1,0:T(8,128)S(1)}, f32[8,128,128]{2,1,0:T(8,128)S(1)}, u32[]{:S(2)}, u32[]{:S(2)}) collective-permute-start(f32[8,128,128]{2,1,0:T(8,128)S(1)} %copy-done.3), channel_id=1, source_target_pairs={{0,2},{2,0},{1,3},{3,1},{4,6},{6,4},{5,7},{7,5},{8,10},{10,8},{9,1... | collective-permute-start | bytes 1572872 | tf_op jit(solution)/shard_map/ppermute | solution.py:286
  232.0 2.9 %collective-permute-start.7 = (f32[8,2,128,128]{3,2,1,0:T(8,128)}, f32[8,2,128,128]{3,2,1,0:T(8,128)S(1)}, u32[]{:S(2)}, u32[]{:S(2)}) collective-permute-start(f32[8,2,128,128]{3,2,1,0:T(8,128)} %get-tuple-element.50), channel_id=1, source_target_pairs={{0,1},{1,0},{2,3},{3,2},{4,5},{5,4},{6,7},{7,6},{8,9},{9,8},{10,11... | collective-permute-start | bytes 3145736 | tf_op jit(solution)/shard_map/ppermute | solution.py:286
Sparse Core Ops, SparseCore 0:
  10.5 128.8 all-gather.6
  144.7 37.8 all-gather.4
